TPU v7x, 32 devices: a whole 2x2x4 slice. The times are simulated.
32 devices in a mesh: section: 2 (over core), dp: 4 (over y, x), tensor: 4 (over z).
Axes of the slice: x: 2, y: 2, z: 4, core: 2. Of those that a mesh axis runs over, the one named last changes fastest.
Arguments:
- inputs: bfloat16 [4, 6, 192, 1024], P('dp', None, 'tensor'), may hold values from -6 to 6
- starts: int32 [4, 6, 192], P('dp'), may hold values from 0 to 1, as said below
- cotangent: bfloat16 [4, 6, 192, 1024], P('dp', None, 'tensor'), may hold values from -6 to 6
- qkv_master: float32 [2, 1024, 3, 1024], P('section', 'dp', None, 'tensor'), may hold values from -0.1875 to 0.1875
- out_master: float32 [2, 1024, 1024], P('section', 'tensor', 'dp'), may hold values from -0.25 to 0.25
- gateup_master: float32 [2, 1024, 2, 2816], P('section', 'dp', None, 'tensor'), may hold values from -0.1875 to 0.1875
- down_master: float32 [2, 2816, 1024], P('section', 'tensor', 'dp'), may hold values from -0.109375 to 0.109375
- gain_master: float32 [2, 2, 1024], P('section', None, ('dp', 'tensor')), may hold values from 0.25 to 1.75
Outputs:
- layer_outputs: bfloat16 [2, 4, 6, 192, 1024], P('section', 'dp', None, 'tensor')
- input_grads: bfloat16 [2, 4, 6, 192, 1024], P('section', 'dp', None, 'tensor')
- qkv_grad: float32 [2, 1024, 3, 1024], P('section', 'dp', None, 'tensor')
- out_grad: float32 [2, 1024, 1024], P('section', 'tensor', 'dp')
- gateup_grad: float32 [2, 1024, 2, 2816], P('section', 'dp', None, 'tensor')
- down_grad: float32 [2, 2816, 1024], P('section', 'tensor', 'dp')
- gain_grad: float32 [2, 2, 1024], P('section', None, ('dp', 'tensor'))
Inputs may be any that keep to these rules, and one draw needn't show every extreme that they name: `starts`: 1 marks the first token of a document and 0 a token that continues the document of the token before it; the first token of every sequence is 1.
All inputs are finite; a program needn't handle non-finite values.
Results may differ from a plain program's by a relative error of at most 0.024.
Values may be sent and summed in bfloat16 or wider, within the bound.
A program may use at most 256 MiB of HBM per device.

v0:
```python
import math

import jax
import jax.numpy as jnp
from jax import lax
from jax.sharding import PartitionSpec as P

DH = 64
BLOCK = 64


EPSILON = 1e-06


def passed_along(value, axis, steps):
    count = lax.axis_size(axis)
    first, last = (max(0, -steps), min(count, count - steps))
    return lax.ppermute(value, axis, [(source, source + steps) for source in range(first, last)])


def blocks_of(flat_rows):
    return flat_rows.reshape(-1, BLOCK, flat_rows.shape[1] // DH, DH)


def rows_of(block_rows):
    return block_rows.reshape(-1, block_rows.shape[2] * DH)


def block_masks(doc_local):
    blocked = doc_local.reshape(-1, BLOCK)
    position = jnp.arange(BLOCK)
    causal = position[:, None] >= position[None, :]
    inside = causal[None] & (blocked[:, :, None] == blocked[:, None, :])
    return (blocked, inside)


def rms_forward(flat_rows, gain_row):
    inverse = lax.rsqrt(jnp.mean(flat_rows * flat_rows, axis=-1, keepdims=True) + EPSILON)
    return (flat_rows * inverse * gain_row, inverse)


def rms_backward(flat_rows, gain_row, inverse, grad_rows):
    scaled = grad_rows * gain_row
    back_rows = inverse * scaled - flat_rows * inverse**3 * jnp.mean(
        scaled * flat_rows, axis=-1, keepdims=True
    )
    return (back_rows, jnp.sum(grad_rows * flat_rows * inverse, axis=0))


def diag_weights(query_rows, key_rows, doc_local):
    blocked, inside = block_masks(doc_local)
    raw_scores = jnp.einsum(
        "bqhd,bkhd->bhqk",
        blocks_of(query_rows),
        blocks_of(key_rows),
        preferred_element_type=jnp.float32,
    )
    scores = jnp.where(inside[:, None], raw_scores * (1.0 / math.sqrt(DH)), -1000000000.0)
    return (jax.nn.softmax(scores, axis=-1), inside)


def diag_forward(query_rows, key_rows, value_rows, doc_local, kv_state):
    weights_soft, inside = diag_weights(query_rows, key_rows, doc_local)
    attended = jnp.einsum(
        "bhqk,bkhd->bqhd",
        weights_soft.astype(jnp.bfloat16),
        blocks_of(value_rows),
        preferred_element_type=jnp.float32,
    )
    return (rows_of(attended).astype(jnp.bfloat16), kv_state)


def diag_backward(query_rows, key_rows, value_rows, doc_local, kv_state, grad_attended, grad_state):
    weights_soft, inside = diag_weights(query_rows, key_rows, doc_local)
    grad_low = blocks_of(grad_attended).astype(jnp.bfloat16)
    grad_value = jnp.einsum(
        "bhqk,bqhd->bkhd",
        weights_soft.astype(jnp.bfloat16),
        grad_low,
        preferred_element_type=jnp.float32,
    )
    grad_weights = jnp.einsum(
        "bqhd,bkhd->bhqk", grad_low, blocks_of(value_rows), preferred_element_type=jnp.float32
    )
    grad_scores = weights_soft * (
        grad_weights - jnp.sum(grad_weights * weights_soft, axis=-1, keepdims=True)
    )
    grad_raw = jnp.where(inside[:, None], grad_scores * (1.0 / math.sqrt(DH)), 0.0).astype(
        jnp.bfloat16
    )
    grad_query = jnp.einsum(
        "bhqk,bkhd->bqhd", grad_raw, blocks_of(key_rows), preferred_element_type=jnp.float32
    )
    grad_key = jnp.einsum(
        "bhqk,bqhd->bkhd", grad_raw, blocks_of(query_rows), preferred_element_type=jnp.float32
    )
    return (rows_of(grad_query), rows_of(grad_key), rows_of(grad_value), grad_state)


def norm_pieces(query_feat, key_feat, value_blocks, doc_local, kv_state):
    blocked, inside = block_masks(doc_local)
    last_doc = blocked[:, -1]
    state_doc = jnp.concatenate([jnp.zeros((1,), jnp.int32), last_doc[:-1]])
    keep_mask = (last_doc == state_doc).astype(jnp.float32)
    carry_mask = (blocked == state_doc[:, None]).astype(jnp.float32)
    tail_mask = (blocked == last_doc[:, None]).astype(jnp.bfloat16)
    raw_scores = jnp.einsum(
        "bqhd,bkhd->bhqk", query_feat, key_feat, preferred_element_type=jnp.float32
    )
    local_scores = jnp.where(inside[:, None], raw_scores, 0.0).astype(jnp.bfloat16)
    kv_terms = jnp.einsum(
        "bkhd,bkhe->bhde",
        key_feat,
        value_blocks * tail_mask[:, :, None, None],
        preferred_element_type=jnp.float32,
    )

    def advance(state_now, block_item):
        keep_value, kv_term = block_item
        return (keep_value * state_now + kv_term, state_now)

    state_end, state_starts = lax.scan(advance, kv_state, (keep_mask, kv_terms))
    mixed_rows = jnp.einsum(
        "bhqk,bkhd->bqhd", local_scores, value_blocks, preferred_element_type=jnp.float32
    )
    carried = jnp.einsum(
        "bqhd,bhde->bqhe",
        query_feat.astype(jnp.float32),
        state_starts,
        precision=lax.Precision.HIGHEST,
    )
    mixed_rows = mixed_rows + carry_mask[:, :, None, None] * carried
    return (
        mixed_rows,
        local_scores,
        state_starts,
        state_end,
        keep_mask,
        carry_mask,
        tail_mask,
        inside,
    )


def norm_forward(query_rows, key_rows, value_rows, doc_local, kv_state):
    query_feat = jax.nn.softplus(blocks_of(query_rows).astype(jnp.float32)).astype(jnp.bfloat16)
    key_feat = jax.nn.softplus(blocks_of(key_rows).astype(jnp.float32)).astype(jnp.bfloat16)
    pieces = norm_pieces(query_feat, key_feat, blocks_of(value_rows), doc_local, kv_state)
    mixed_rows = pieces[0]
    normed = mixed_rows * lax.rsqrt(
        jnp.mean(mixed_rows * mixed_rows, axis=-1, keepdims=True) + EPSILON
    )
    return (rows_of(normed).astype(jnp.bfloat16), pieces[3])


def norm_backward(query_rows, key_rows, value_rows, doc_local, kv_state, grad_attended, grad_state):
    query_float = blocks_of(query_rows).astype(jnp.float32)
    key_float = blocks_of(key_rows).astype(jnp.float32)
    query_feat = jax.nn.softplus(query_float).astype(jnp.bfloat16)
    key_feat = jax.nn.softplus(key_float).astype(jnp.bfloat16)
    value_blocks = blocks_of(value_rows)
    pieces = norm_pieces(query_feat, key_feat, value_blocks, doc_local, kv_state)
    mixed_rows, local_scores, state_starts, _, keep_mask, carry_mask, tail_mask, inside = pieces
    scale_rows = lax.rsqrt(jnp.mean(mixed_rows * mixed_rows, axis=-1, keepdims=True) + EPSILON)
    grad_normed = blocks_of(grad_attended)
    grad_mixed = scale_rows * grad_normed - mixed_rows * scale_rows**3 * jnp.mean(
        grad_normed * mixed_rows, axis=-1, keepdims=True
    )
    grad_low = grad_mixed.astype(jnp.bfloat16)
    carry_wide = carry_mask[:, :, None, None]
    grad_carried = grad_low * carry_wide.astype(jnp.bfloat16)
    use_terms = jnp.einsum(
        "bqhd,bqhe->bhde", query_feat, grad_carried, preferred_element_type=jnp.float32
    )

    def retreat(grad_now, block_item):
        keep_value, use_term = block_item
        return (keep_value * grad_now + use_term, grad_now)

    grad_start, grad_after = lax.scan(retreat, grad_state, (keep_mask, use_terms), reverse=True)
    tail_wide = tail_mask.astype(jnp.float32)[:, :, None, None]
    key_state = tail_wide * jnp.einsum(
        "bkhe,bhde->bkhd",
        value_blocks.astype(jnp.float32),
        grad_after,
        precision=lax.Precision.HIGHEST,
    )
    value_state = tail_wide * jnp.einsum(
        "bkhd,bhde->bkhe", key_feat.astype(jnp.float32), grad_after, precision=lax.Precision.HIGHEST
    )
    query_state = carry_wide * jnp.einsum(
        "bqhe,bhde->bqhd",
        grad_low.astype(jnp.float32),
        state_starts,
        precision=lax.Precision.HIGHEST,
    )
    value_local = jnp.einsum(
        "bhqk,bqhd->bkhd", local_scores, grad_low, preferred_element_type=jnp.float32
    )
    grad_products = jnp.einsum(
        "bqhd,bkhd->bhqk", grad_low, value_blocks, preferred_element_type=jnp.float32
    )
    grad_scores = jnp.where(inside[:, None], grad_products, 0.0).astype(jnp.bfloat16)
    query_local = jnp.einsum(
        "bhqk,bkhd->bqhd", grad_scores, key_feat, preferred_element_type=jnp.float32
    )
    key_local = jnp.einsum(
        "bhqk,bqhd->bkhd", grad_scores, query_feat, preferred_element_type=jnp.float32
    )
    grad_query = (query_local + query_state) * jax.nn.sigmoid(query_float)
    grad_key = (key_local + key_state) * jax.nn.sigmoid(key_float)
    grad_value = value_local + value_state
    return (rows_of(grad_query), rows_of(grad_key), rows_of(grad_value), grad_start)


def on_device(
    inputs, starts, cotangent, qkv_master, out_master, gateup_master, down_master, gain_master
):
    section_index = lax.axis_index("section")
    micro_count = inputs.shape[1]
    row_count = inputs.shape[2]
    model_width = inputs.shape[3]
    local_cols = qkv_master.shape[3]
    local_hidden = gateup_master.shape[3]
    head_count = local_cols // DH
    norm_gains = lax.all_gather(
        gain_master[0].astype(jnp.bfloat16), ("dp", "tensor"), axis=1, tiled=True
    ).astype(jnp.float32)

    def fetch_weights():
        pieces = (
            lax.all_gather(qkv_master[0].astype(jnp.bfloat16), "dp", axis=0, tiled=True),
            lax.all_gather(out_master[0].astype(jnp.bfloat16), "dp", axis=1, tiled=True),
            lax.all_gather(gateup_master[0].astype(jnp.bfloat16), "dp", axis=0, tiled=True),
            lax.all_gather(down_master[0].astype(jnp.bfloat16), "dp", axis=1, tiled=True),
        )
        return (
            pieces[0].reshape(model_width, 3 * local_cols),
            pieces[1],
            pieces[2].reshape(model_width, 2 * local_hidden),
            pieces[3],
        )

    def spread(row_block):
        return lax.all_gather(row_block, "tensor", axis=0, tiled=True)

    def collect(full_rows, weight_rows):

        def term_rows(start_row, row_total):
            return jnp.dot(full_rows, weight_rows, preferred_element_type=jnp.float32)

        return lax.psum_scatter(
            term_rows(jnp.int32(0), lax.axis_size("tensor") * row_count).astype(jnp.bfloat16),
            "tensor",
            scatter_dimension=0,
            tiled=True,
        ).astype(jnp.float32)

    def spread_grad(row_block):
        return lax.all_gather(row_block, "tensor", axis=0, tiled=True)

    def collect_grad(full_rows, weight_rows):

        def term_rows(start_row, row_total):
            return lax.dot_general(
                full_rows, weight_rows, (((1,), (1,)), ((), ())), preferred_element_type=jnp.float32
            )

        return lax.psum_scatter(
            term_rows(jnp.int32(0), lax.axis_size("tensor") * row_count).astype(jnp.bfloat16),
            "tensor",
            scatter_dimension=0,
            tiled=True,
        ).astype(jnp.float32)

    def layer_forward(x_in, weights, doc_local, kv_state):
        wqkv_rows, wout_rows, wgu_rows, wdown_rows = weights
        normed_first, scale_first = rms_forward(x_in, norm_gains[0])
        full_first = spread(normed_first.astype(jnp.bfloat16))
        projected = jnp.dot(full_first, wqkv_rows, preferred_element_type=jnp.float32).astype(
            jnp.bfloat16
        )
        query_rows = projected[:, :local_cols]
        key_rows = projected[:, local_cols : 2 * local_cols]
        value_rows = projected[:, 2 * local_cols :]
        attended, new_state = lax.cond(
            section_index == 0,
            diag_forward,
            norm_forward,
            query_rows,
            key_rows,
            value_rows,
            doc_local,
            kv_state,
        )
        hidden_in = x_in + collect(attended, wout_rows)
        normed_second, scale_second = rms_forward(hidden_in, norm_gains[1])
        full_second = spread(normed_second.astype(jnp.bfloat16))
        gate_up = jnp.dot(full_second, wgu_rows, preferred_element_type=jnp.float32)
        gate_rows = gate_up[:, :local_hidden]
        upward = gate_up[:, local_hidden:]
        product = (gate_rows * upward).astype(jnp.bfloat16)
        output = hidden_in + collect(product, wdown_rows)
        record = (
            full_first,
            projected,
            attended,
            hidden_in,
            scale_first,
            full_second,
            gate_rows,
            upward,
            product,
            scale_second,
        )
        return (output, new_state, record)

    def layer_backward(x_in, grad_out, doc_local, kv_state, grad_state, weights):
        wqkv_rows, wout_rows, wgu_rows, wdown_rows = weights
        _, _, record = layer_forward(x_in, weights, doc_local, kv_state)
        (
            full_first,
            projected,
            attended,
            hidden_in,
            scale_first,
            full_second,
            gate_rows,
            upward,
            product,
            scale_second,
        ) = record
        grad_full = spread_grad(grad_out.astype(jnp.bfloat16))
        down_terms = jnp.einsum("tf,td->fd", product, grad_full, preferred_element_type=jnp.float32)
        grad_product = lax.dot_general(
            grad_full, wdown_rows, (((1,), (1,)), ((), ())), preferred_element_type=jnp.float32
        )
        grad_gate_up = jnp.concatenate(
            [grad_product * upward, grad_product * gate_rows], axis=1
        ).astype(jnp.bfloat16)
        gateup_terms = jnp.einsum(
            "td,tf->df", full_second, grad_gate_up, preferred_element_type=jnp.float32
        )
        grad_second, gain_second = rms_backward(
            hidden_in, norm_gains[1], scale_second, collect_grad(grad_gate_up, wgu_rows)
        )
        grad_hidden = grad_out + grad_second
        grad_branch = spread_grad(grad_hidden.astype(jnp.bfloat16))
        out_terms = jnp.einsum(
            "tc,td->cd", attended, grad_branch, preferred_element_type=jnp.float32
        )
        grad_attended = lax.dot_general(
            grad_branch, wout_rows, (((1,), (1,)), ((), ())), preferred_element_type=jnp.float32
        )
        query_rows = projected[:, :local_cols]
        key_rows = projected[:, local_cols : 2 * local_cols]
        value_rows = projected[:, 2 * local_cols :]
        grad_query, grad_key, grad_value, grad_start = lax.cond(
            section_index == 0,
            diag_backward,
            norm_backward,
            query_rows,
            key_rows,
            value_rows,
            doc_local,
            kv_state,
            grad_attended,
            grad_state,
        )
        grad_projected = jnp.concatenate([grad_query, grad_key, grad_value], axis=1).astype(
            jnp.bfloat16
        )
        qkv_terms = jnp.einsum(
            "td,tc->dc", full_first, grad_projected, preferred_element_type=jnp.float32
        )
        grad_first, gain_first = rms_backward(
            x_in, norm_gains[0], scale_first, collect_grad(grad_projected, wqkv_rows)
        )
        grad_in = grad_hidden + grad_first
        weight_terms = (
            qkv_terms.reshape(model_width, 3, local_cols),
            out_terms,
            gateup_terms.reshape(model_width, 2, local_hidden),
            down_terms,
        )
        return (grad_in, grad_start, weight_terms, jnp.stack([gain_first, gain_second]))

    own_inputs = inputs[0]
    own_starts = starts[0]
    own_cot = cotangent[0]
    kv_state = jnp.zeros((head_count, DH, DH), jnp.float32)
    state_log = jnp.zeros((micro_count, head_count, DH, DH), jnp.float32)
    held_inputs = jnp.zeros((micro_count, row_count, model_width), jnp.bfloat16)
    results = jnp.zeros((micro_count, row_count, model_width), jnp.bfloat16)
    sent_rows = jnp.zeros((row_count, model_width), jnp.bfloat16)
    for tick_number in range(micro_count + 1):
        weights = fetch_weights()
        if tick_number > 0:
            arrived = passed_along(sent_rows, "section", 1)
        else:
            arrived = sent_rows
        tick_order = tick_number - section_index
        is_valid = (tick_order >= 0) & (tick_order < micro_count)
        mb_index = jnp.clip(tick_order, 0, micro_count - 1)
        fresh_rows = lax.dynamic_index_in_dim(own_inputs, mb_index, 0, keepdims=False)
        layer_input = jnp.where(section_index == 0, fresh_rows, arrived)
        doc_local = jnp.cumsum(lax.dynamic_index_in_dim(own_starts, mb_index, 0, keepdims=False))
        output, new_state, _ = layer_forward(
            layer_input.astype(jnp.float32), weights, doc_local, kv_state
        )
        sent_rows = output.astype(jnp.bfloat16)
        held_inputs = jnp.where(
            is_valid,
            lax.dynamic_update_index_in_dim(held_inputs, layer_input, mb_index, 0),
            held_inputs,
        )
        results = jnp.where(
            is_valid, lax.dynamic_update_index_in_dim(results, sent_rows, mb_index, 0), results
        )
        state_log = jnp.where(
            is_valid, lax.dynamic_update_index_in_dim(state_log, kv_state, mb_index, 0), state_log
        )
        kv_state = jnp.where(is_valid, new_state, kv_state)
    grad_state = jnp.zeros((head_count, DH, DH), jnp.float32)
    grad_log = jnp.zeros((micro_count, row_count, model_width), jnp.bfloat16)
    back_sent = jnp.zeros((row_count, model_width), jnp.bfloat16)
    gain_total = jnp.zeros((2, model_width), jnp.float32)
    totals = (
        jnp.zeros(qkv_master.shape[1:], jnp.float32),
        jnp.zeros(out_master.shape[1:], jnp.float32),
        jnp.zeros(gateup_master.shape[1:], jnp.float32),
        jnp.zeros(down_master.shape[1:], jnp.float32),
    )
    for tick_number in range(micro_count + 1):
        weights = fetch_weights()
        if tick_number > 0:
            arrived = passed_along(back_sent, "section", -1)
        else:
            arrived = back_sent
        tick_order = tick_number - (1 - section_index)
        is_valid = (tick_order >= 0) & (tick_order < micro_count)
        mb_index = jnp.clip(micro_count - 1 - tick_order, 0, micro_count - 1)
        layer_input = lax.dynamic_index_in_dim(held_inputs, mb_index, 0, keepdims=False)
        upstream = jnp.where(
            section_index == 1,
            lax.dynamic_index_in_dim(own_cot, mb_index, 0, keepdims=False),
            arrived,
        )
        doc_local = jnp.cumsum(lax.dynamic_index_in_dim(own_starts, mb_index, 0, keepdims=False))
        start_state = lax.dynamic_index_in_dim(state_log, mb_index, 0, keepdims=False)
        grad_in, grad_start, weight_terms, gain_terms = layer_backward(
            layer_input.astype(jnp.float32),
            upstream.astype(jnp.float32),
            doc_local,
            start_state,
            grad_state,
            weights,
        )
        grad_state = jnp.where(is_valid, grad_start, grad_state)
        back_sent = grad_in.astype(jnp.bfloat16)
        grad_log = jnp.where(
            is_valid, lax.dynamic_update_index_in_dim(grad_log, back_sent, mb_index, 0), grad_log
        )
        weight_terms = tuple((jnp.where(is_valid, term_value, 0.0) for term_value in weight_terms))
        gain_total = gain_total + jnp.where(is_valid, gain_terms, 0.0)
        shares = (
            lax.psum_scatter(
                weight_terms[0].astype(jnp.bfloat16), "dp", scatter_dimension=0, tiled=True
            ).astype(jnp.float32),
            lax.psum_scatter(
                weight_terms[1].astype(jnp.bfloat16), "dp", scatter_dimension=1, tiled=True
            ).astype(jnp.float32),
            lax.psum_scatter(
                weight_terms[2].astype(jnp.bfloat16), "dp", scatter_dimension=0, tiled=True
            ).astype(jnp.float32),
            lax.psum_scatter(
                weight_terms[3].astype(jnp.bfloat16), "dp", scatter_dimension=1, tiled=True
            ).astype(jnp.float32),
        )
        totals = tuple((running + share for running, share in zip(totals, shares)))
    gain_share = lax.psum_scatter(gain_total, ("dp", "tensor"), scatter_dimension=1, tiled=True)
    return (
        results[None, None],
        grad_log[None, None],
        totals[0][None],
        totals[1][None],
        totals[2][None],
        totals[3][None],
        gain_share[None],
    )


def solution(mesh):
    return jax.shard_map(
        on_device,
        mesh=mesh,
        in_specs=(
            P("dp", None, "tensor", None),
            P("dp", None, None),
            P("dp", None, "tensor", None),
            P("section", "dp", None, "tensor"),
            P("section", "tensor", "dp"),
            P("section", "dp", None, "tensor"),
            P("section", "tensor", "dp"),
            P("section", None, ("dp", "tensor")),
        ),
        out_specs=(
            P("section", "dp", None, "tensor", None),
            P("section", "dp", None, "tensor", None),
            P("section", "dp", None, "tensor"),
            P("section", "tensor", "dp"),
            P("section", "dp", None, "tensor"),
            P("section", "tensor", "dp"),
            P("section", None, ("dp", "tensor")),
        ),
        check_vma=False,
    )
```

profile of v0, /device:TPU:0, one launch (start us, length us, event | category | flops | bytes accessed | tf_op | source)
XLA Modules:
  0.0 3581.9 jit_solution(14257471232926741850)
XLA Ops:
  10.7 47.7 %all-gather = bf16[1,2,1024]{1,0,2:T(2,128)(2,1)S(1)} all-gather(bf16[1,2,64]{1,0,2:T(2,128)(2,1)S(1)} %copy.3181), channel_id=2, replica_groups=mesh['section'=2,'dp'=4,'tensor'=4] {'dp','tensor'}, dimensions={2}, use_global_device_ids=true | all-gather | bytes 4352 | tf_op jit(solution)/shard_map/all_gather | solution.py:226
  357.4 38.1 %reduce-scatter.75.cloned.1.call-done = bf16[48,1024]{1,0:T(8,128)(2,1)} async-done(((bf16[192,1024]{1,0:T(8,128)(2,1)}), bf16[48,1024]{1,0:T(8,128)(2,1)}) %reduce-scatter.75.cloned.1.call-update) | async-done | bytes 98320 | tf_op jit(solution)/shard_map/reduce_scatter | solution.py:252
  477.7 38.2 %reduce-scatter.79.cloned.1.call-done = bf16[48,1024]{1,0:T(8,128)(2,1)} async-done(((bf16[192,1024]{1,0:T(8,128)(2,1)}), bf16[48,1024]{1,0:T(8,128)(2,1)}) %reduce-scatter.79.cloned.1.call-update) | async-done | bytes 98320 | tf_op jit(solution)/shard_map/reduce_scatter | solution.py:252
  598.5 38.9 %reduce-scatter.83.cloned.1.call-done = bf16[48,1024]{1,0:T(8,128)(2,1)} async-done(((bf16[192,1024]{1,0:T(8,128)(2,1)}), bf16[48,1024]{1,0:T(8,128)(2,1)}) %reduce-scatter.83.cloned.1.call-update) | async-done | bytes 98320 | tf_op jit(solution)/shard_map/reduce_scatter | solution.py:252
  719.8 38.3 %reduce-scatter.87.cloned.1.call-done = bf16[48,1024]{1,0:T(8,128)(2,1)} async-done(((bf16[192,1024]{1,0:T(8,128)(2,1)}), bf16[48,1024]{1,0:T(8,128)(2,1)}) %reduce-scatter.87.cloned.1.call-update) | async-done | bytes 98320 | tf_op jit(solution)/shard_map/reduce_scatter | solution.py:252
  1228.3 58.0 %reduce-scatter.107.cloned.1.call-done = bf16[48,1024]{1,0:T(8,128)(2,1)} async-done(((bf16[192,1024]{1,0:T(8,128)(2,1)}), bf16[48,1024]{1,0:T(8,128)(2,1)}) %reduce-scatter.107.cloned.1.call-update) | async-done | bytes 98320 | tf_op jit(solution)/shard_map/reduce_scatter | solution.py:252
  1286.3 58.5 %reduce-scatter.101.cloned.1.call-done = bf16[48,1024]{1,0:T(8,128)(2,1)} async-done(((bf16[192,1024]{1,0:T(8,128)(2,1)}), bf16[48,1024]{1,0:T(8,128)(2,1)}) %reduce-scatter.101.cloned.1.call-update) | async-done | bytes 98320 | tf_op jit(solution)/shard_map/reduce_scatter | solution.py:252
  1344.8 57.5 %reduce-scatter.131.cloned.1.call-done = bf16[48,1024]{1,0:T(8,128)(2,1)} async-done(((bf16[192,1024]{1,0:T(8,128)(2,1)}), bf16[48,1024]{1,0:T(8,128)(2,1)}) %reduce-scatter.131.cloned.1.call-update) | async-done | bytes 98320 | tf_op jit(solution)/shard_map/reduce_scatter | solution.py:252
  1540.3 49.5 %reduce-scatter.105.cloned.1.call-done = bf16[48,1024]{1,0:T(8,128)(2,1)} async-done(((bf16[192,1024]{1,0:T(8,128)(2,1)}), bf16[48,1024]{1,0:T(8,128)(2,1)}) %reduce-scatter.105.cloned.1.call-update) | async-done | bytes 98320 | tf_op jit(solution)/shard_map/reduce_scatter | solution.py:269
  1657.1 34.7 conditional.115
  1711.6 49.8 %reduce-scatter.111.cloned.1.call-done = bf16[48,1024]{1,0:T(8,128)(2,1)} async-done(((bf16[192,1024]{1,0:T(8,128)(2,1)}), bf16[48,1024]{1,0:T(8,128)(2,1)}) %reduce-scatter.111.cloned.1.call-update) | async-done | bytes 98320 | tf_op jit(solution)/shard_map/reduce_scatter | solution.py:269
  1828.6 34.9 conditional.117
  1883.4 50.5 %reduce-scatter.117.cloned.1.call-done = bf16[48,1024]{1,0:T(8,128)(2,1)} async-done(((bf16[192,1024]{1,0:T(8,128)(2,1)}), bf16[48,1024]{1,0:T(8,128)(2,1)}) %reduce-scatter.117.cloned.1.call-update) | async-done | bytes 98320 | tf_op jit(solution)/shard_map/reduce_scatter | solution.py:269
  2001.7 34.7 conditional.119
  2056.5 49.0 %reduce-scatter.123.cloned.1.call-done = bf16[48,1024]{1,0:T(8,128)(2,1)} async-done(((bf16[192,1024]{1,0:T(8,128)(2,1)}), bf16[48,1024]{1,0:T(8,128)(2,1)}) %reduce-scatter.123.cloned.1.call-update) | async-done | bytes 98320 | tf_op jit(solution)/shard_map/reduce_scatter | solution.py:269
  2225.7 50.2 %reduce-scatter.129.cloned.1.call-done = bf16[48,1024]{1,0:T(8,128)(2,1)} async-done(((bf16[192,1024]{1,0:T(8,128)(2,1)}), bf16[48,1024]{1,0:T(8,128)(2,1)}) %reduce-scatter.129.cloned.1.call-update) | async-done | bytes 98320 | tf_op jit(solution)/shard_map/reduce_scatter | solution.py:269
  2385.1 62.1 %reduce-scatter.135.cloned.1.call-done = bf16[48,1024]{1,0:T(8,128)(2,1)} async-done(((bf16[192,1024]{1,0:T(8,128)(2,1)}), bf16[48,1024]{1,0:T(8,128)(2,1)}) %reduce-scatter.135.cloned.1.call-update) | async-done | bytes 98320 | tf_op jit(solution)/shard_map/reduce_scatter | solution.py:269
  3260.2 41.9 %reduce-scatter.165.cloned.1.call-done = bf16[256,2,704]{0,2,1:T(8,128)(2,1)} async-done(((bf16[1024,2,704]{0,2,1:T(8,128)(2,1)}), bf16[256,2,704]{0,2,1:T(8,128)(2,1)}) %reduce-scatter.165.cloned.1.call-update) | async-done | bytes 720912 | tf_op jit(solution)/shard_map/reduce_scatter | solution.py:473
  3302.1 44.8 %reduce-scatter.167.cloned.1.call-done = bf16[256,2,704]{0,2,1:T(8,128)(2,1)} async-done(((bf16[1024,2,704]{0,2,1:T(8,128)(2,1)}), bf16[256,2,704]{0,2,1:T(8,128)(2,1)}) %reduce-scatter.167.cloned.1.call-update) | async-done | bytes 720912 | tf_op jit(solution)/shard_map/reduce_scatter | solution.py:473
  3347.0 44.7 %reduce-scatter.169.cloned.1.call-done = bf16[256,2,704]{0,2,1:T(8,128)(2,1)} async-done(((bf16[1024,2,704]{0,2,1:T(8,128)(2,1)}), bf16[256,2,704]{0,2,1:T(8,128)(2,1)}) %reduce-scatter.169.cloned.1.call-update) | async-done | bytes 720912 | tf_op jit(solution)/shard_map/reduce_scatter | solution.py:473
  3391.6 44.7 %reduce-scatter.171.cloned.1.call-done = bf16[256,2,704]{0,2,1:T(8,128)(2,1)} async-done(((bf16[1024,2,704]{0,2,1:T(8,128)(2,1)}), bf16[256,2,704]{0,2,1:T(8,128)(2,1)}) %reduce-scatter.171.cloned.1.call-update) | async-done | bytes 720912 | tf_op jit(solution)/shard_map/reduce_scatter | solution.py:473
  3436.3 44.8 %reduce-scatter.173.cloned.1.call-done = bf16[256,2,704]{0,2,1:T(8,128)(2,1)} async-done(((bf16[1024,2,704]{0,2,1:T(8,128)(2,1)}), bf16[256,2,704]{0,2,1:T(8,128)(2,1)}) %reduce-scatter.173.cloned.1.call-update) | async-done | bytes 720912 | tf_op jit(solution)/shard_map/reduce_scatter | solution.py:473
  3481.1 44.7 %reduce-scatter.175.cloned.1.call-done = bf16[256,2,704]{0,2,1:T(8,128)(2,1)} async-done(((bf16[1024,2,704]{0,2,1:T(8,128)(2,1)}), bf16[256,2,704]{0,2,1:T(8,128)(2,1)}) %reduce-scatter.175.cloned.1.call-update) | async-done | bytes 720912 | tf_op jit(solution)/shard_map/reduce_scatter | solution.py:473
  3525.8 44.7 %reduce-scatter.177.cloned.1.call-done = bf16[256,2,704]{0,2,1:T(8,128)(2,1)} async-done(((bf16[1024,2,704]{0,2,1:T(8,128)(2,1)}), bf16[256,2,704]{0,2,1:T(8,128)(2,1)}) %reduce-scatter.177.cloned.1.call-update) | async-done | bytes 720912 | tf_op jit(solution)/shard_map/reduce_scatter | solution.py:473
  (1400 shorter events, 2877.4 us)
Async XLA Ops:
  906.9 289.9 %reduce-scatter.99.cloned.1.call-start = ((), (), s32[]{:S(2)}) async-start(), calls=%async_computation.80 | async-start | bytes 491520 | tf_op jit(solution)/shard_map/reduce_scatter | solution.py:269
  2477.5 289.2 %reduce-scatter.163.cloned.1.call-start = ((), (), s32[]{:S(2)}) async-start(), calls=%async_computation.112 | async-start | bytes 655360 | tf_op jit(solution)/shard_map/reduce_scatter | solution.py:470
  2479.7 319.9 %reduce-scatter.179.cloned.1.call-start = ((), (), s32[]{:S(2)}) async-start(), calls=%async_computation.120 | async-start | bytes 1802240 | tf_op jit(solution)/shard_map/reduce_scatter | solution.py:476
  2481.8 351.0 %reduce-scatter.181.cloned.1.call-start = ((), (), s32[]{:S(2)}) async-start(), calls=%async_computation.121 | async-start | bytes 1802240 | tf_op jit(solution)/shard_map/reduce_scatter | solution.py:476
  2485.2 380.5 %reduce-scatter.183.cloned.1.call-start = ((), (), s32[]{:S(2)}) async-start(), calls=%async_computation.122 | async-start | bytes 1802240 | tf_op jit(solution)/shard_map/reduce_scatter | solution.py:476
  2487.4 411.6 %reduce-scatter.185.cloned.1.call-start = ((), (), s32[]{:S(2)}) async-start(), calls=%async_computation.123 | async-start | bytes 1802240 | tf_op jit(solution)/shard_map/reduce_scatter | solution.py:476
  2490.8 441.2 %reduce-scatter.187.cloned.1.call-start = ((), (), s32[]{:S(2)}) async-start(), calls=%async_computation.124 | async-start | bytes 1802240 | tf_op jit(solution)/shard_map/reduce_scatter | solution.py:476
  2492.9 472.3 %reduce-scatter.189.cloned.1.call-start = ((), (), s32[]{:S(2)}) async-start(), calls=%async_computation.125 | async-start | bytes 1802240 | tf_op jit(solution)/shard_map/reduce_scatter | solution.py:476
  2496.5 502.4 %reduce-scatter.191.cloned.1.call-start = ((), (), s32[]{:S(2)}) async-start(), calls=%async_computation.126 | async-start | bytes 1802240 | tf_op jit(solution)/shard_map/reduce_scatter | solution.py:476
  2498.6 523.1 %reduce-scatter.93.cloned.1.call-start = ((), (), s32[]{:S(2)}) async-start(), calls=%async_computation.77 | async-start | bytes 491520 | tf_op jit(solution)/shard_map/reduce_scatter | solution.py:252
  2519.8 534.2 %reduce-scatter.137.cloned.1.call-start = ((), (), s32[]{:S(2)}) async-start(), calls=%async_computation.99 | async-start | bytes 1966080 | tf_op jit(solution)/shard_map/reduce_scatter | solution.py:467
  2523.0 564.9 %reduce-scatter.139.cloned.1.call-start = ((), (), s32[]{:S(2)}) async-start(), calls=%async_computation.100 | async-start | bytes 1966080 | tf_op jit(solution)/shard_map/reduce_scatter | solution.py:467
  2526.3 595.5 %reduce-scatter.141.cloned.1.call-start = ((), (), s32[]{:S(2)}) async-start(), calls=%async_computation.101 | async-start | bytes 1966080 | tf_op jit(solution)/shard_map/reduce_scatter | solution.py:467
  2529.7 626.1 %reduce-scatter.143.cloned.1.call-start = ((), (), s32[]{:S(2)}) async-start(), calls=%async_computation.102 | async-start | bytes 1966080 | tf_op jit(solution)/shard_map/reduce_scatter | solution.py:467
  2533.0 656.6 %reduce-scatter.145.cloned.1.call-start = ((), (), s32[]{:S(2)}) async-start(), calls=%async_computation.103 | async-start | bytes 1966080 | tf_op jit(solution)/shard_map/reduce_scatter | solution.py:467
  2536.3 687.1 %reduce-scatter.147.cloned.1.call-start = ((), (), s32[]{:S(2)}) async-start(), calls=%async_computation.104 | async-start | bytes 1966080 | tf_op jit(solution)/shard_map/reduce_scatter | solution.py:467
  2539.6 717.7 %reduce-scatter.149.cloned.1.call-start = ((), (), s32[]{:S(2)}) async-start(), calls=%async_computation.105 | async-start | bytes 1966080 | tf_op jit(solution)/shard_map/reduce_scatter | solution.py:467
  2542.8 759.3 %reduce-scatter.165.cloned.1.call-start = ((), (), s32[]{:S(2)}) async-start(), calls=%async_computation.113 | async-start | bytes 3604480 | tf_op jit(solution)/shard_map/reduce_scatter | solution.py:473
  2551.4 795.5 %reduce-scatter.167.cloned.1.call-start = ((), (), s32[]{:S(2)}) async-start(), calls=%async_computation.114 | async-start | bytes 3604480 | tf_op jit(solution)/shard_map/reduce_scatter | solution.py:473
  2559.8 831.8 %reduce-scatter.169.cloned.1.call-start = ((), (), s32[]{:S(2)}) async-start(), calls=%async_computation.115 | async-start | bytes 3604480 | tf_op jit(solution)/shard_map/reduce_scatter | solution.py:473
  2568.4 867.9 %reduce-scatter.171.cloned.1.call-start = ((), (), s32[]{:S(2)}) async-start(), calls=%async_computation.116 | async-start | bytes 3604480 | tf_op jit(solution)/shard_map/reduce_scatter | solution.py:473
  2576.9 904.2 %reduce-scatter.173.cloned.1.call-start = ((), (), s32[]{:S(2)}) async-start(), calls=%async_computation.117 | async-start | bytes 3604480 | tf_op jit(solution)/shard_map/reduce_scatter | solution.py:473
  2585.3 940.5 %reduce-scatter.175.cloned.1.call-start = ((), (), s32[]{:S(2)}) async-start(), calls=%async_computation.118 | async-start | bytes 3604480 | tf_op jit(solution)/shard_map/reduce_scatter | solution.py:473
  2593.8 976.7 %reduce-scatter.177.cloned.1.call-start = ((), (), s32[]{:S(2)}) async-start(), calls=%async_computation.119 | async-start | bytes 3604480 | tf_op jit(solution)/shard_map/reduce_scatter | solution.py:473
  (280 other events, 8337.7 us)
Sparse Core Ops, SparseCore 0:
  116.6 39.9 all-gather.11
  598.5 38.7 reduce-scatter.82
  841.6 39.3 reduce-scatter.94
  988.8 65.0 reduce-scatter.98
  1056.9 56.4 reduce-scatter.124
  1115.4 55.6 reduce-scatter.118
  1173.5 54.7 reduce-scatter.112
  1230.6 55.6 reduce-scatter.106
  1288.7 56.0 reduce-scatter.100
  1347.5 54.7 reduce-scatter.130
  1524.8 64.9 reduce-scatter.104
  1696.5 64.9 reduce-scatter.110
  1868.3 65.5 reduce-scatter.116
  2041.2 64.2 reduce-scatter.122
  2210.6 65.2 reduce-scatter.128
  2379.8 67.3 reduce-scatter.134
  2500.3 75.4 reduce-scatter.192
  3260.3 41.7 reduce-scatter.164
  3305.2 41.7 reduce-scatter.166
  3349.8 41.7 reduce-scatter.168
  3394.5 41.7 reduce-scatter.170
  3439.3 41.7 reduce-scatter.172
  3484.0 41.7 reduce-scatter.174
  3528.7 41.7 reduce-scatter.176
  (43 shorter events, 1124.6 us)
where the time goes:
time: 3610 us; the launch traced here: 3580 us
  waiting for transfers between devices  1930 us (53%)
  blocking collectives  690 us (19%)
  local copies, waits for them, and re-layouts  420 us (12%)
  matrix products  279 us (8%)
  other arithmetic  218 us (6%)
    reduce_scatter x21, waiting for transfers between devices, collect(): lax.psum_scatter(term_rows(jnp.int32(0), lax.axis_size('tensor') * row_co...  519 us
    reduce_scatter x14, waiting for transfers between devices, collect_grad(): lax.psum_scatter(term_rows(jnp.int32(0), lax.axis_size('tensor') * row_co...  424 us
    all_gather x28, blocking collectives, spread(): return lax.all_gather(row_block, 'tensor', axis=0, tiled=True)  421 us
    reduce_scatter x7, waiting for transfers between devices, on_device(): lax.psum_scatter(weight_terms[2].astype(jnp.bfloat16), 'dp', scatter_dime...  310 us
    reduce_scatter x7, waiting for transfers between devices, on_device(): lax.psum_scatter(weight_terms[0].astype(jnp.bfloat16), 'dp', scatter_dime...  235 us
    reduce_scatter x7, waiting for transfers between devices, on_device(): lax.psum_scatter(weight_terms[3].astype(jnp.bfloat16), 'dp', scatter_dime...  230 us
    all_gather x14, blocking collectives, spread_grad(): return lax.all_gather(row_block, 'tensor', axis=0, tiled=True)  210 us
    reduce_scatter x7, waiting for transfers between devices, on_device(): lax.psum_scatter(weight_terms[1].astype(jnp.bfloat16), 'dp', scatter_dime...  160 us
  transfers between devices with their start and end apart: 79, of which 60 were waited for; matrix products, arithmetic and copies ran while one was open for 10% of the time, Pallas kernels for 0%

commit v1 on v0

--- a/solution.py
+++ b/solution.py
@@ -16,6 +16,11 @@
     count = lax.axis_size(axis)
     first, last = (max(0, -steps), min(count, count - steps))
     return lax.ppermute(value, axis, [(source, source + steps) for source in range(first, last)])
+
+
+def running_sum(marks):
+    position = jnp.arange(marks.shape[0])
+    return jnp.sum(jnp.where(position[:, None] >= position[None, :], marks[None, :], 0), axis=1)
 
 
 def blocks_of(flat_rows):
@@ -393,8 +398,8 @@
     held_inputs = jnp.zeros((micro_count, row_count, model_width), jnp.bfloat16)
     results = jnp.zeros((micro_count, row_count, model_width), jnp.bfloat16)
     sent_rows = jnp.zeros((row_count, model_width), jnp.bfloat16)
+    weights = fetch_weights()
     for tick_number in range(micro_count + 1):
-        weights = fetch_weights()
         if tick_number > 0:
             arrived = passed_along(sent_rows, "section", 1)
         else:
@@ -404,7 +409,7 @@
         mb_index = jnp.clip(tick_order, 0, micro_count - 1)
         fresh_rows = lax.dynamic_index_in_dim(own_inputs, mb_index, 0, keepdims=False)
         layer_input = jnp.where(section_index == 0, fresh_rows, arrived)
-        doc_local = jnp.cumsum(lax.dynamic_index_in_dim(own_starts, mb_index, 0, keepdims=False))
+        doc_local = running_sum(lax.dynamic_index_in_dim(own_starts, mb_index, 0, keepdims=False))
         output, new_state, _ = layer_forward(
             layer_input.astype(jnp.float32), weights, doc_local, kv_state
         )
@@ -426,13 +431,12 @@
     back_sent = jnp.zeros((row_count, model_width), jnp.bfloat16)
     gain_total = jnp.zeros((2, model_width), jnp.float32)
     totals = (
-        jnp.zeros(qkv_master.shape[1:], jnp.float32),
-        jnp.zeros(out_master.shape[1:], jnp.float32),
-        jnp.zeros(gateup_master.shape[1:], jnp.float32),
-        jnp.zeros(down_master.shape[1:], jnp.float32),
+        jnp.zeros((model_width, 3, local_cols), jnp.float32),
+        jnp.zeros((local_cols, model_width), jnp.float32),
+        jnp.zeros((model_width, 2, local_hidden), jnp.float32),
+        jnp.zeros((local_hidden, model_width), jnp.float32),
     )
     for tick_number in range(micro_count + 1):
-        weights = fetch_weights()
         if tick_number > 0:
             arrived = passed_along(back_sent, "section", -1)
         else:
@@ -446,7 +450,7 @@
             lax.dynamic_index_in_dim(own_cot, mb_index, 0, keepdims=False),
             arrived,
         )
-        doc_local = jnp.cumsum(lax.dynamic_index_in_dim(own_starts, mb_index, 0, keepdims=False))
+        doc_local = running_sum(lax.dynamic_index_in_dim(own_starts, mb_index, 0, keepdims=False))
         start_state = lax.dynamic_index_in_dim(state_log, mb_index, 0, keepdims=False)
         grad_in, grad_start, weight_terms, gain_terms = layer_backward(
             layer_input.astype(jnp.float32),
@@ -463,21 +467,13 @@
         )
         weight_terms = tuple((jnp.where(is_valid, term_value, 0.0) for term_value in weight_terms))
         gain_total = gain_total + jnp.where(is_valid, gain_terms, 0.0)
-        shares = (
-            lax.psum_scatter(
-                weight_terms[0].astype(jnp.bfloat16), "dp", scatter_dimension=0, tiled=True
-            ).astype(jnp.float32),
-            lax.psum_scatter(
-                weight_terms[1].astype(jnp.bfloat16), "dp", scatter_dimension=1, tiled=True
-            ).astype(jnp.float32),
-            lax.psum_scatter(
-                weight_terms[2].astype(jnp.bfloat16), "dp", scatter_dimension=0, tiled=True
-            ).astype(jnp.float32),
-            lax.psum_scatter(
-                weight_terms[3].astype(jnp.bfloat16), "dp", scatter_dimension=1, tiled=True
-            ).astype(jnp.float32),
-        )
-        totals = tuple((running + share for running, share in zip(totals, shares)))
+        totals = tuple((running + term for running, term in zip(totals, weight_terms)))
+    totals = (
+        lax.psum_scatter(totals[0].astype(jnp.bfloat16), "dp", scatter_dimension=0, tiled=True).astype(jnp.float32),
+        lax.psum_scatter(totals[1].astype(jnp.bfloat16), "dp", scatter_dimension=1, tiled=True).astype(jnp.float32),
+        lax.psum_scatter(totals[2].astype(jnp.bfloat16), "dp", scatter_dimension=0, tiled=True).astype(jnp.float32),
+        lax.psum_scatter(totals[3].astype(jnp.bfloat16), "dp", scatter_dimension=1, tiled=True).astype(jnp.float32),
+    )
     gain_share = lax.psum_scatter(gain_total, ("dp", "tensor"), scatter_dimension=1, tiled=True)
     return (
         results[None, None],

time: 3610 us -> 2760 us (0.76)
  waiting for transfers between devices: 1930 us -> 1160 us
  local copies, waits for them, and re-layouts: 420 us -> 346 us
  matrix products: 279 us -> 319 us
    reduce_scatter x28 -> x4, waiting for transfers between devices: 935 us -> 129 us  [the longest x1 42.7 us: on_device(): lax.psum_scatter(totals[2].astype(jnp.bfloat16), 'dp', scatter_dimension=...]
    reduce_scatter x21, waiting for transfers between devices: 519 us -> 559 us  [collect(): lax.psum_scatter(term_rows(jnp.int32(0), lax.axis_size('tensor') * row_co...]
    convert_element_type x14 -> x2, local copies, waits for them, and re-layouts: 43.8 us -> 4.53 us  [the longest x1 2.93 us: on_device(): totals[2].astype(jnp.bfloat16)]
    another operation x36 -> x0, other arithmetic: 38.4 us -> none
    another operation x105 -> x78, local copies, waits for them, and re-layouts: 116 us -> 90.7 us
  transfers between devices with their start and end apart: 79 -> 55, of which waited for: 60 -> 38; matrix products, arithmetic and copies ran while one was open for 10% -> 10% of each run, Pallas kernels for 0% -> 0%
where the time goes in v1:
time: 2760 us; the launch traced here: 2740 us
  waiting for transfers between devices  1160 us (42%)
  blocking collectives  688 us (25%)
  local copies, waits for them, and re-layouts  346 us (13%)
  matrix products  319 us (12%)
  other arithmetic  185 us (7%)
    reduce_scatter x21, waiting for transfers between devices, collect(): lax.psum_scatter(term_rows(jnp.int32(0), lax.axis_size('tensor') * row_co...  559 us
    all_gather x28, blocking collectives, spread(): return lax.all_gather(row_block, 'tensor', axis=0, tiled=True)  420 us
    reduce_scatter x14, waiting for transfers between devices, collect_grad(): lax.psum_scatter(term_rows(jnp.int32(0), lax.axis_size('tensor') * row_co...  404 us
    all_gather x14, blocking collectives, spread_grad(): return lax.all_gather(row_block, 'tensor', axis=0, tiled=True)  210 us
    reshape x63, local copies, waits for them, and re-layouts, blocks_of(): return flat_rows.reshape(-1, BLOCK, flat_rows.shape[1] // DH, DH)  95.8 us
    another operation x78, local copies, waits for them, and re-layouts  90.7 us
    unnamed x453, local copies, waits for them, and re-layouts  55.2 us
  transfers between devices with their start and end apart: 55, of which 38 were waited for; matrix products, arithmetic and copies ran while one was open for 10% of the time, Pallas kernels for 0%

profile of v1, /device:TPU:0, one launch (start us, length us, event | category | flops | bytes accessed | tf_op | source)
XLA Modules:
  0.0 2736.0 jit_solution(724241720173491564)
XLA Ops:
  9.6 47.8 %all-gather = bf16[1,2,1024]{1,0,2:T(2,128)(2,1)S(1)} all-gather(bf16[1,2,64]{1,0,2:T(2,128)(2,1)S(1)} %copy.3650), channel_id=2, replica_groups=mesh['section'=2,'dp'=4,'tensor'=4] {'dp','tensor'}, dimensions={2}, use_global_device_ids=true | all-gather | bytes 4352 | tf_op jit(solution)/shard_map/all_gather | solution.py:231
  239.6 35.3 %reduce-scatter.47.cloned.1.call-done = bf16[48,1024]{1,0:T(8,128)(2,1)} async-done(((bf16[192,1024]{1,0:T(8,128)(2,1)}), bf16[48,1024]{1,0:T(8,128)(2,1)}) %reduce-scatter.47.cloned.1.call-update) | async-done | bytes 98320 | tf_op jit(solution)/shard_map/reduce_scatter | solution.py:257
  357.7 38.1 %reduce-scatter.51.cloned.1.call-done = bf16[48,1024]{1,0:T(8,128)(2,1)} async-done(((bf16[192,1024]{1,0:T(8,128)(2,1)}), bf16[48,1024]{1,0:T(8,128)(2,1)}) %reduce-scatter.51.cloned.1.call-update) | async-done | bytes 98320 | tf_op jit(solution)/shard_map/reduce_scatter | solution.py:257
  478.1 37.7 %reduce-scatter.55.cloned.1.call-done = bf16[48,1024]{1,0:T(8,128)(2,1)} async-done(((bf16[192,1024]{1,0:T(8,128)(2,1)}), bf16[48,1024]{1,0:T(8,128)(2,1)}) %reduce-scatter.55.cloned.1.call-update) | async-done | bytes 98320 | tf_op jit(solution)/shard_map/reduce_scatter | solution.py:257
  598.2 38.2 %reduce-scatter.59.cloned.1.call-done = bf16[48,1024]{1,0:T(8,128)(2,1)} async-done(((bf16[192,1024]{1,0:T(8,128)(2,1)}), bf16[48,1024]{1,0:T(8,128)(2,1)}) %reduce-scatter.59.cloned.1.call-update) | async-done | bytes 98320 | tf_op jit(solution)/shard_map/reduce_scatter | solution.py:257
  718.9 37.4 %reduce-scatter.63.cloned.1.call-done = bf16[48,1024]{1,0:T(8,128)(2,1)} async-done(((bf16[192,1024]{1,0:T(8,128)(2,1)}), bf16[48,1024]{1,0:T(8,128)(2,1)}) %reduce-scatter.63.cloned.1.call-update) | async-done | bytes 98320 | tf_op jit(solution)/shard_map/reduce_scatter | solution.py:257
  944.5 34.1 %conditional.111 = (f32[4,64,64]{2,1,0:T(8,128)}, bf16[192,256]{1,0:T(8,128)(2,1)}, bf16[192,256]{1,0:T(8,128)(2,1)}, bf16[192,256]{1,0:T(8,128)(2,1)}) conditional(s32[]{:T(128)} %convert_element_type.2072, (bf16[192,256]{1,0:T(8,128)(2,1)}, s32[192]{0:T(256)}, bf16[192,256]{1,0:T(8,128)(2,1)}, bf16[192,256]{1,0:T(8,128)(2,1)}, ...), branch_computations={%region_97.104_spmd, %region_104.108_spmd} | conditional | flops 203816336 | bytes 19280816 | solution.py:363
  1224.1 57.2 %reduce-scatter.83.cloned.1.call-done = bf16[48,1024]{1,0:T(8,128)(2,1)} async-done(((bf16[192,1024]{1,0:T(8,128)(2,1)}), bf16[48,1024]{1,0:T(8,128)(2,1)}) %reduce-scatter.83.cloned.1.call-update) | async-done | bytes 98320 | tf_op jit(solution)/shard_map/reduce_scatter | solution.py:257
  1281.3 57.6 %reduce-scatter.77.cloned.1.call-done = bf16[48,1024]{1,0:T(8,128)(2,1)} async-done(((bf16[192,1024]{1,0:T(8,128)(2,1)}), bf16[48,1024]{1,0:T(8,128)(2,1)}) %reduce-scatter.77.cloned.1.call-update) | async-done | bytes 98320 | tf_op jit(solution)/shard_map/reduce_scatter | solution.py:257
  1338.9 57.4 %reduce-scatter.107.cloned.1.call-done = bf16[48,1024]{1,0:T(8,128)(2,1)} async-done(((bf16[192,1024]{1,0:T(8,128)(2,1)}), bf16[48,1024]{1,0:T(8,128)(2,1)}) %reduce-scatter.107.cloned.1.call-update) | async-done | bytes 98320 | tf_op jit(solution)/shard_map/reduce_scatter | solution.py:257
  1480.8 33.0 %conditional.113 = (f32[4,64,64]{2,1,0:T(8,128)}, bf16[192,256]{1,0:T(8,128)(2,1)}, bf16[192,256]{1,0:T(8,128)(2,1)}, bf16[192,256]{1,0:T(8,128)(2,1)}) conditional(s32[]{:T(128)} %convert_element_type.2072, (bf16[192,256]{1,0:T(8,128)(2,1)}, s32[192]{0:T(256)}, bf16[192,256]{1,0:T(8,128)(2,1)}, bf16[192,256]{1,0:T(8,128)(2,1)}, ...), branch_computations={%region_122.129_spmd, %region_129.133_spmd} | conditional | flops 203783568 | bytes 19280798 | solution.py:363
  1534.1 49.6 %reduce-scatter.81.cloned.1.call-done = bf16[48,1024]{1,0:T(8,128)(2,1)} async-done(((bf16[192,1024]{1,0:T(8,128)(2,1)}), bf16[48,1024]{1,0:T(8,128)(2,1)}) %reduce-scatter.81.cloned.1.call-update) | async-done | bytes 98320 | tf_op jit(solution)/shard_map/reduce_scatter | solution.py:274
  1651.0 34.5 %conditional.115 = (f32[4,64,64]{2,1,0:T(8,128)}, bf16[192,256]{1,0:T(8,128)(2,1)}, bf16[192,256]{1,0:T(8,128)(2,1)}, bf16[192,256]{1,0:T(8,128)(2,1)}) conditional(s32[]{:T(128)} %convert_element_type.2072, (bf16[192,256]{1,0:T(8,128)(2,1)}, s32[192]{0:T(256)}, bf16[192,256]{1,0:T(8,128)(2,1)}, bf16[192,256]{1,0:T(8,128)(2,1)}, ...), branch_computations={%region_148.155_spmd, %region_155.159_spmd} | conditional | flops 203783568 | bytes 19411870 | solution.py:363
  1705.5 50.1 %reduce-scatter.87.cloned.1.call-done = bf16[48,1024]{1,0:T(8,128)(2,1)} async-done(((bf16[192,1024]{1,0:T(8,128)(2,1)}), bf16[48,1024]{1,0:T(8,128)(2,1)}) %reduce-scatter.87.cloned.1.call-update) | async-done | bytes 98320 | tf_op jit(solution)/shard_map/reduce_scatter | solution.py:274
  1823.1 34.7 %conditional.117 = (f32[4,64,64]{2,1,0:T(8,128)}, bf16[192,256]{1,0:T(8,128)(2,1)}, bf16[192,256]{1,0:T(8,128)(2,1)}, bf16[192,256]{1,0:T(8,128)(2,1)}) conditional(s32[]{:T(128)} %convert_element_type.2072, (bf16[192,256]{1,0:T(8,128)(2,1)}, s32[192]{0:T(256)}, bf16[192,256]{1,0:T(8,128)(2,1)}, bf16[192,256]{1,0:T(8,128)(2,1)}, ...), branch_computations={%region_174.181_spmd, %region_181.185_spmd} | conditional | flops 203783568 | bytes 19411870 | solution.py:363
  1877.7 49.6 %reduce-scatter.93.cloned.1.call-done = bf16[48,1024]{1,0:T(8,128)(2,1)} async-done(((bf16[192,1024]{1,0:T(8,128)(2,1)}), bf16[48,1024]{1,0:T(8,128)(2,1)}) %reduce-scatter.93.cloned.1.call-update) | async-done | bytes 98320 | tf_op jit(solution)/shard_map/reduce_scatter | solution.py:274
  1994.6 34.5 %conditional.119 = (f32[4,64,64]{2,1,0:T(8,128)}, bf16[192,256]{1,0:T(8,128)(2,1)}, bf16[192,256]{1,0:T(8,128)(2,1)}, bf16[192,256]{1,0:T(8,128)(2,1)}) conditional(s32[]{:T(128)} %convert_element_type.2072, (bf16[192,256]{1,0:T(8,128)(2,1)}, s32[192]{0:T(256)}, bf16[192,256]{1,0:T(8,128)(2,1)}, bf16[192,256]{1,0:T(8,128)(2,1)}, ...), branch_computations={%region_200.207_spmd, %region_207.211_spmd} | conditional | flops 203783568 | bytes 19411870 | solution.py:363
  2055.6 42.8 %reduce-scatter.99.cloned.1.call-done = bf16[48,1024]{1,0:T(8,128)(2,1)} async-done(((bf16[192,1024]{1,0:T(8,128)(2,1)}), bf16[48,1024]{1,0:T(8,128)(2,1)}) %reduce-scatter.99.cloned.1.call-update) | async-done | bytes 98320 | tf_op jit(solution)/shard_map/reduce_scatter | solution.py:274
  2165.8 33.3 %conditional.121 = (f32[4,64,64]{2,1,0:T(8,128)}, bf16[192,256]{1,0:T(8,128)(2,1)}, bf16[192,256]{1,0:T(8,128)(2,1)}, bf16[192,256]{1,0:T(8,128)(2,1)}) conditional(s32[]{:T(128)} %convert_element_type.2072, (bf16[192,256]{1,0:T(8,128)(2,1)}, s32[192]{0:T(256)S(1)}, bf16[192,256]{1,0:T(8,128)(2,1)}, bf16[192,256]{1,0:T(8,128)(2,1)}, ...), branch_computations={%region_225.232_spmd, %region_232.236_spmd} | conditional | flops 203783568 | bytes 19408770 | solution.py:363
  2224.6 44.4 %reduce-scatter.105.cloned.1.call-done = bf16[48,1024]{1,0:T(8,128)(2,1)} async-done(((bf16[192,1024]{1,0:T(8,128)(2,1)}), bf16[48,1024]{1,0:T(8,128)(2,1)}) %reduce-scatter.105.cloned.1.call-update) | async-done | bytes 98320 | tf_op jit(solution)/shard_map/reduce_scatter | solution.py:274
  2338.3 32.0 %conditional.123 = (bf16[192,256]{1,0:T(8,128)(2,1)}, bf16[192,256]{1,0:T(8,128)(2,1)}, bf16[192,256]{1,0:T(8,128)(2,1)}) conditional(s32[]{:T(128)} %convert_element_type.2072, (bf16[192,256]{1,0:T(8,128)(2,1)}, s32[192]{0:T(256)S(1)}, bf16[192,256]{1,0:T(8,128)(2,1)}, bf16[192,256]{1,0:T(8,128)(2,1)}, f32[4,64,64]{2,1,0:T(8,128)}, ...), branch_computations={%region_251.258_spmd, %region_258.262_spmd} | conditional | flops 203799952 | bytes 19474300 | solution.py:363
  2380.7 60.3 %reduce-scatter.111.cloned.1.call-done = bf16[48,1024]{1,0:T(8,128)(2,1)} async-done(((bf16[192,1024]{1,0:T(8,128)(2,1)}), bf16[48,1024]{1,0:T(8,128)(2,1)}) %reduce-scatter.111.cloned.1.call-update) | async-done | bytes 98320 | tf_op jit(solution)/shard_map/reduce_scatter | solution.py:274
  2594.8 32.0 %reduce-scatter.119.cloned.1.call-done = bf16[704,256]{1,0:T(8,128)(2,1)} async-done(((bf16[704,1024]{1,0:T(8,128)(2,1)}), bf16[704,256]{1,0:T(8,128)(2,1)}) %reduce-scatter.119.cloned.1.call-update) | async-done | bytes 360464 | tf_op jit(solution)/shard_map/reduce_scatter | solution.py:475
  2684.0 42.7 %reduce-scatter.117.cloned.1.call-done = bf16[256,2,704]{0,2,1:T(8,128)(2,1)} async-done(((bf16[1024,2,704]{0,2,1:T(8,128)(2,1)}), bf16[256,2,704]{0,2,1:T(8,128)(2,1)}) %reduce-scatter.117.cloned.1.call-update) | async-done | bytes 720912 | tf_op jit(solution)/shard_map/reduce_scatter | solution.py:474
  (1285 shorter events, 2120.1 us)
Async XLA Ops:
  98.3 113.4 %reduce-scatter.45.cloned.1.call-start = ((), (), s32[]{:S(2)}) async-start(), calls=%async_computation.41 | async-start | bytes 491520 | tf_op jit(solution)/shard_map/reduce_scatter | solution.py:257
  904.5 289.2 %reduce-scatter.75.cloned.1.call-start = ((), (), s32[]{:S(2)}) async-start(), calls=%async_computation.56 | async-start | bytes 491520 | tf_op jit(solution)/shard_map/reduce_scatter | solution.py:274
  983.3 210.4 %reduce-scatter.101.cloned.1.call-start = ((), (), s32[]{:S(2)}) async-start(), calls=%async_computation.69 | async-start | bytes 491520 | tf_op jit(solution)/shard_map/reduce_scatter | solution.py:257
  1021.0 172.7 %reduce-scatter.95.cloned.1.call-start = ((), (), s32[]{:S(2)}) async-start(), calls=%async_computation.66 | async-start | bytes 491520 | tf_op jit(solution)/shard_map/reduce_scatter | solution.py:257
  1054.8 169.3 %reduce-scatter.89.cloned.1.call-start = ((), (), s32[]{:S(2)}) async-start(), calls=%async_computation.63 | async-start | bytes 491520 | tf_op jit(solution)/shard_map/reduce_scatter | solution.py:257
  1088.8 192.5 %reduce-scatter.83.cloned.1.call-start = ((), (), s32[]{:S(2)}) async-start(), calls=%async_computation.60 | async-start | bytes 491520 | tf_op jit(solution)/shard_map/reduce_scatter | solution.py:257
  1125.1 213.8 %reduce-scatter.77.cloned.1.call-start = ((), (), s32[]{:S(2)}) async-start(), calls=%async_computation.57 | async-start | bytes 491520 | tf_op jit(solution)/shard_map/reduce_scatter | solution.py:257
  1159.2 237.1 %reduce-scatter.107.cloned.1.call-start = ((), (), s32[]{:S(2)}) async-start(), calls=%async_computation.72 | async-start | bytes 491520 | tf_op jit(solution)/shard_map/reduce_scatter | solution.py:257
  1193.6 267.1 %reduce-scatter.79.cloned.1.call-start = ((), (), s32[]{:S(2)}) async-start(), calls=%async_computation.58 | async-start | bytes 491520 | tf_op jit(solution)/shard_map/reduce_scatter | solution.py:274
  1441.6 142.1 %reduce-scatter.81.cloned.1.call-start = ((), (), s32[]{:S(2)}) async-start(), calls=%async_computation.59 | async-start | bytes 491520 | tf_op jit(solution)/shard_map/reduce_scatter | solution.py:274
  1518.5 113.1 %reduce-scatter.85.cloned.1.call-start = ((), (), s32[]{:S(2)}) async-start(), calls=%async_computation.61 | async-start | bytes 491520 | tf_op jit(solution)/shard_map/reduce_scatter | solution.py:274
  1612.3 143.3 %reduce-scatter.87.cloned.1.call-start = ((), (), s32[]{:S(2)}) async-start(), calls=%async_computation.62 | async-start | bytes 491520 | tf_op jit(solution)/shard_map/reduce_scatter | solution.py:274
  1690.2 113.5 %reduce-scatter.91.cloned.1.call-start = ((), (), s32[]{:S(2)}) async-start(), calls=%async_computation.64 | async-start | bytes 491520 | tf_op jit(solution)/shard_map/reduce_scatter | solution.py:274
  1784.1 143.3 %reduce-scatter.93.cloned.1.call-start = ((), (), s32[]{:S(2)}) async-start(), calls=%async_computation.65 | async-start | bytes 491520 | tf_op jit(solution)/shard_map/reduce_scatter | solution.py:274
  1956.2 142.3 %reduce-scatter.99.cloned.1.call-start = ((), (), s32[]{:S(2)}) async-start(), calls=%async_computation.68 | async-start | bytes 491520 | tf_op jit(solution)/shard_map/reduce_scatter | solution.py:274
  2126.9 142.1 %reduce-scatter.105.cloned.1.call-start = ((), (), s32[]{:S(2)}) async-start(), calls=%async_computation.71 | async-start | bytes 491520 | tf_op jit(solution)/shard_map/reduce_scatter | solution.py:274
  2203.7 115.1 %reduce-scatter.109.cloned.1.call-start = ((), (), s32[]{:S(2)}) async-start(), calls=%async_computation.73 | async-start | bytes 491520 | tf_op jit(solution)/shard_map/reduce_scatter | solution.py:274
  2299.1 141.9 %reduce-scatter.111.cloned.1.call-start = ((), (), s32[]{:S(2)}) async-start(), calls=%async_computation.74 | async-start | bytes 491520 | tf_op jit(solution)/shard_map/reduce_scatter | solution.py:274
  2375.0 119.3 %reduce-scatter.67.cloned.1.call-start = ((), (), s32[]{:S(2)}) async-start(), calls=%async_computation.52 | async-start | bytes 491520 | tf_op jit(solution)/shard_map/reduce_scatter | solution.py:257
  2470.4 122.8 %reduce-scatter.115.cloned.1.call-start = ((), (), s32[]{:S(2)}) async-start(), calls=%async_computation.76 | async-start | bytes 655360 | tf_op jit(solution)/shard_map/reduce_scatter | solution.py:473
  2471.6 155.2 %reduce-scatter.119.cloned.1.call-start = ((), (), s32[]{:S(2)}) async-start(), calls=%async_computation.78 | async-start | bytes 1802240 | tf_op jit(solution)/shard_map/reduce_scatter | solution.py:475
  2481.7 168.1 %reduce-scatter.69.cloned.1.call-start = ((), (), s32[]{:S(2)}) async-start(), calls=%async_computation.53 | async-start | bytes 491520 | tf_op jit(solution)/shard_map/reduce_scatter | solution.py:257
  2515.9 166.1 %reduce-scatter.113.cloned.1.call-start = ((), (), s32[]{:S(2)}) async-start(), calls=%async_computation.75 | async-start | bytes 1966080 | tf_op jit(solution)/shard_map/reduce_scatter | solution.py:472
  2524.8 201.9 %reduce-scatter.117.cloned.1.call-start = ((), (), s32[]{:S(2)}) async-start(), calls=%async_computation.77 | async-start | bytes 3604480 | tf_op jit(solution)/shard_map/reduce_scatter | solution.py:474
  (268 other events, 3588.7 us)
Sparse Core Ops, SparseCore 0:
  10.4 35.7 all-gather.9
  116.2 39.9 all-gather.11
  239.7 35.1 reduce-scatter.46
  357.8 37.9 reduce-scatter.50
  478.2 37.5 reduce-scatter.54
  598.3 38.1 reduce-scatter.58
  719.0 37.2 reduce-scatter.62
  839.8 39.7 reduce-scatter.70
  983.4 64.3 reduce-scatter.74
  1050.1 60.1 reduce-scatter.100
  1112.4 55.1 reduce-scatter.94
  1170.0 54.0 reduce-scatter.88
  1226.3 54.8 reduce-scatter.82
  1283.6 55.1 reduce-scatter.76
  1341.6 54.6 reduce-scatter.106
  1518.6 65.0 reduce-scatter.80
  1690.4 65.1 reduce-scatter.86
  1862.6 64.6 reduce-scatter.92
  2033.9 64.5 reduce-scatter.98
  2203.9 65.1 reduce-scatter.104
  2375.1 65.9 reduce-scatter.110
  2492.9 75.4 reduce-scatter.120
  2596.7 30.0 reduce-scatter.118
  2684.9 41.7 reduce-scatter.116
  (19 shorter events, 392.1 us)

commit v2 on v1

v2 whole, which is shorter than its diff:
```python
import functools
import math

import jax
import jax.numpy as jnp
from jax import lax
from jax.experimental import pallas as pl
from jax.experimental.pallas import tpu as pltpu
from jax.sharding import PartitionSpec as P

DH = 64
BLOCK = 64
EPS = 1e-6
BF = jnp.bfloat16
F32 = jnp.float32
MESH = pl.DeviceIdType.MESH
NN = (((1,), (0,)), ((), ()))
NT = (((1,), (1,)), ((), ()))
TN = (((0,), (0,)), ((), ()))


def mm(a, b, dims=NN):
    return lax.dot_general(a, b, dims, preferred_element_type=F32)


def ceil_to(value, unit):
    return (value + unit - 1) // unit * unit


class Sizes:
    def __init__(self, mesh, model, micro, rows, cols, hidden):
        self.nd, self.nt = mesh.shape["dp"], mesh.shape["tensor"]
        self.D, self.M, self.R, self.C, self.F = model, micro, rows, cols, hidden
        self.FP = ceil_to(hidden, 128)
        self.Dr = model // self.nd
        self.MH, self.Hn = micro // 2, self.nt // 2
        self.MB = rows * self.nt
        self.T = self.MH * self.MB
        self.NH = cols // DH
        self.NB = self.MB // BLOCK
        self.NBH = self.MH * self.NB
        self.oO, self.oG = 3 * cols, 4 * cols
        self.oU, self.oD = self.oG + self.FP, self.oG + 2 * self.FP
        self.N = self.oG + 3 * self.FP
        self.pieces = (
            (0, 3 * cols),
            (self.oO, cols),
            (self.oG, self.FP),
            (self.oU, self.FP),
            (self.oD, self.FP),
        )


def body(
    z_,
    wsh,
    xin,
    cot,
    marks,
    gain_in,
    out_y,
    out_g,
    out_w,
    out_gain,
    W,
    LW,
    L2,
    XF,
    GF,
    N1,
    N2,
    QKV,
    O,
    GATE,
    UP,
    HID,
    H,
    Y,
    GA,
    GGU,
    GQKV,
    GH,
    GX,
    PT,
    RL1,
    RL2,
    RSB,
    AP,
    UU,
    DU,
    ST,
    SIN,
    SEND_STATE,
    MSK,
    CAR,
    TAIL,
    KEEP,
    GL1,
    GL2,
    GV,
    GOWN,
    DG,
    DL0,
    DL1,
    DL2,
    in_sem,
    x_ss,
    x_rs,
    x_fs,
    w1_ss,
    w1_rs,
    w2_ss,
    w2_rs,
    ag_ss,
    ag_fs,
    ag_rs,
    r1_ss,
    r1_rs,
    r2_ss,
    r2_rs,
    st_ss,
    st_rs,
    o_ss,
    o_rs,
    d1_ss,
    d1_rs,
    d2_ss,
    d2_rs,
    g_ss,
    g_rs,
):
    D, R, C, FP, Dr, MH, Hn, MB, T, NH, NB, NBH = (
        z_.D,
        z_.R,
        z_.C,
        z_.FP,
        z_.Dr,
        z_.MH,
        z_.Hn,
        z_.MB,
        z_.T,
        z_.NH,
        z_.NB,
        z_.NBH,
    )
    nd, nt = z_.nd, z_.nt
    pieces = z_.pieces
    s, d, z = lax.axis_index("section"), lax.axis_index("dp"), lax.axis_index("tensor")
    zh, zl = z // Hn, z % Hn
    own = s * Hn + zl
    core_dev = (1 - s, d, z)

    def remote(src, dst, ssem, rsem, dev):
        return pltpu.make_async_remote_copy(
            src_ref=src, dst_ref=dst, send_sem=ssem, recv_sem=rsem, device_id=dev, device_id_type=MESH
        )

    def got(dst, sem):
        pltpu.make_async_copy(dst, dst, sem).wait()

    def dp_dev(step):
        return (s, (d + step) % nd, z)

    def z_dev(step):
        return (s, d, (z + step) % nt)

    def peer_zl(step):
        return (zl + step) % Hn

    barrier = pltpu.get_barrier_semaphore()
    for step in range(1, nt):
        pl.semaphore_signal(barrier, inc=1, device_id=z_dev(step), device_id_type=MESH)
    for step in range(1, nd):
        pl.semaphore_signal(barrier, inc=1, device_id=dp_dev(step), device_id_type=MESH)
    pl.semaphore_signal(barrier, inc=1, device_id=core_dev, device_id_type=MESH)
    far_dev = (1 - s, d, (z + Hn) % nt)
    pl.semaphore_signal(barrier, inc=1, device_id=far_dev, device_id_type=MESH)
    pl.semaphore_wait(barrier, nt - 1 + nd - 1 + 2)

    def spread_tokens(src, dst):
        for m in range(MH):
            mine = dst.at[pl.ds(m * MB + z * R, R)]
            pltpu.make_async_copy(src.at[zh * MH + m], mine, in_sem.at[s, m]).start()
            for step in range(1, nt):
                other = (z + step) % nt
                remote(
                    src.at[(other // Hn) * MH + m],
                    mine,
                    x_ss.at[m, step - 1],
                    x_rs.at[s, m, step - 1],
                    z_dev(step),
                ).start()

    def forward_tokens(dst, array):
        for m in range(MH):
            got(dst.at[pl.ds(m * MB + z * R, R)], in_sem.at[array, m])
            for step in range(1, nt):
                rows = dst.at[pl.ds(m * MB + (z + nt - step) % nt * R, R)]
                got(rows, x_rs.at[array, m, step - 1])
                remote(
                    rows, rows, x_fs.at[m, step - 1], x_rs.at[array, m, step - 1], core_dev
                ).start()

    def await_tokens(src, dst, array):
        for m in range(MH):
            got(dst.at[pl.ds(m * MB + z * R, R)], in_sem.at[array, m])
            for step in range(1, nt):
                rows = dst.at[pl.ds(m * MB + (z + nt - step) % nt * R, R)]
                got(rows, x_rs.at[array, m, step - 1])

    def own_tokens(src, dst, array):
        for m in range(MH):
            mine = dst.at[pl.ds(m * MB + z * R, R)]
            pltpu.make_async_copy(src.at[zh * MH + m], mine, in_sem.at[array, m]).start()

    def w_rows(l, block, p):
        col, width = pieces[p]
        return W.at[l, pl.ds(block * Dr, Dr), pl.ds(col, width)]

    def shard_cols(p):
        col, width = pieces[p]
        return wsh.at[:, pl.ds(col, width)]

    def w_hand_out(l, p):
        for half in range(2):
            dest_z = half * Hn + zl
            to_self = (zh == s) & (half == zh)

            @pl.when(to_self)
            def _():
                pltpu.make_async_copy(shard_cols(p), w_rows(l, d, p), w1_rs.at[l, p]).start()

            @pl.when(jnp.logical_not(to_self))
            def _():
                remote(
                    shard_cols(p),
                    w_rows(l, d, p),
                    w1_ss.at[p, half],
                    w1_rs.at[l, p],
                    (zh, d, dest_z),
                ).start()

    def w_handed_out(l, p):
        for half in range(2):
            to_self = (zh == s) & (half == zh)

            @pl.when(jnp.logical_not(to_self))
            def _():
                remote(
                    shard_cols(p), w_rows(l, d, p), w1_ss.at[p, half], w1_rs.at[l, p], core_dev
                ).wait_send()

    def w_share(l, p):
        got(w_rows(l, d, p), w1_rs.at[l, p])

        def one(step, carry):
            remote(
                w_rows(l, d, p),
                w_rows(l, d, p),
                w2_ss.at[l, p, step - 1],
                w2_rs.at[l, p, step - 1],
                dp_dev(step),
            ).start()
            return carry

        lax.fori_loop(1, nd, one, 0)

    def w_ready(l, p):
        def one(step, carry):
            got(w_rows(l, (d + nd - step) % nd, p), w2_rs.at[l, p, step - 1])
            return carry

        lax.fori_loop(1, nd, one, 0)

    def w_shared(l, p):
        def one(step, carry):
            remote(
                w_rows(l, d, p),
                w_rows(l, d, p),
                w2_ss.at[l, p, step - 1],
                w2_rs.at[l, p, step - 1],
                dp_dev(step),
            ).wait_send()
            return carry

        lax.fori_loop(1, nd, one, 0)

    def d_send(l, p):
        col, width = pieces[p]

        def one(step, carry):
            remote(
                w_rows(l, (d + step) % nd, p),
                LW.at[l, step - 1, :, pl.ds(col, width)],
                d1_ss.at[l, p, step - 1],
                d1_rs.at[l, p, step - 1],
                dp_dev(step),
            ).start()
            return carry

        lax.fori_loop(1, nd, one, 0)

    def d_sum(l, p):
        col, width = pieces[p]

        def one(step, carry):
            got(LW.at[l, step - 1, :, pl.ds(col, width)], d1_rs.at[l, p, step - 1])
            return carry

        lax.fori_loop(1, nd, one, 0)
        rows = pl.ds(d * Dr, Dr)
        total = W[l, rows, pl.ds(col, width)].astype(F32)
        for step in range(1, nd):
            total = total + LW[l, step - 1, :, pl.ds(col, width)].astype(F32)
        W[l, rows, pl.ds(col, width)] = total.astype(BF)
        dest = L2.at[zh, :, pl.ds(col, width)]
        to_self = (s == l) & (zh == s)

        @pl.when(to_self)
        def _():
            pltpu.make_async_copy(w_rows(l, d, p), dest, d2_rs.at[p, zh]).start()

        @pl.when(jnp.logical_not(to_self))
        def _():
            remote(
                w_rows(l, d, p), dest, d2_ss.at[l, p], d2_rs.at[p, zh], (l, d, s * Hn + zl)
            ).start()

    def d_sent(l, p):
        col, width = pieces[p]

        def one(step, carry):
            remote(
                w_rows(l, (d + step) % nd, p),
                LW.at[l, step - 1, :, pl.ds(col, width)],
                d1_ss.at[l, p, step - 1],
                d1_rs.at[l, p, step - 1],
                dp_dev(step),
            ).wait_send()
            return carry

        lax.fori_loop(1, nd, one, 0)
        to_self = (s == l) & (zh == s)

        @pl.when(jnp.logical_not(to_self))
        def _():
            remote(
                w_rows(l, d, p),
                L2.at[zh, :, pl.ds(col, width)],
                d2_ss.at[l, p],
                d2_rs.at[p, zh],
                core_dev,
            ).wait_send()

    def d_final(p):
        col, width = pieces[p]
        for half in range(2):
            got(L2.at[half, :, pl.ds(col, width)], d2_rs.at[p, half])
        cols = pl.ds(col, width)
        out_w[:, cols] = L2[0, :, cols].astype(F32) + L2[1, :, cols].astype(F32)

    def chunk_rows(m, c):
        return pl.ds(m * MB + c * R, R)

    def ag_send(k, buf, m):
        rows = buf.at[chunk_rows(m, own)]
        for step in range(1, Hn):
            remote(
                rows,
                rows,
                ag_ss.at[k, m, step],
                ag_rs.at[k, m, own],
                (s, d, zh * Hn + peer_zl(step)),
            ).start()
        remote(rows, rows, ag_ss.at[k, m, 0], ag_rs.at[k, m, own], core_dev).start()

    def ag_forward(k, buf, m):
        for step in range(1, Hn):
            c = s * Hn + peer_zl(step)
            rows = buf.at[chunk_rows(m, c)]
            got(rows, ag_rs.at[k, m, c])
            remote(rows, rows, ag_fs.at[k, m, step - 1], ag_rs.at[k, m, c], core_dev).start()

    def ag_wait(k, buf, m):
        for step in range(Hn):
            c = (1 - s) * Hn + step
            got(buf.at[chunk_rows(m, c)], ag_rs.at[k, m, c])

    def ag_sent(k, buf, m):
        rows = buf.at[chunk_rows(m, own)]
        for step in range(Hn):
            remote(rows, rows, ag_ss.at[k, m, step], ag_rs.at[k, m, own], core_dev).wait_send()
        for step in range(1, Hn):
            rows = buf.at[chunk_rows(m, s * Hn + peer_zl(step))]
            remote(rows, rows, ag_fs.at[k, m, step - 1], ag_rs.at[k, m, own], core_dev).wait_send()

    def rs_copy1(k, m):
        par = k % 2
        return remote(
            PT.at[par, pl.ds(m * MB + (1 - s) * Hn * R, Hn * R)],
            RL1.at[par, m],
            r1_ss.at[k, m],
            r1_rs.at[k, m],
            core_dev,
        )

    def rs_copy2(k, m, step):
        par = k % 2
        return remote(
            RSB.at[par, m, step - 1],
            RL2.at[par, m, step - 1],
            r2_ss.at[k, m, step - 1],
            r2_rs.at[k, m, step - 1],
            (s, d, zh * Hn + peer_zl(step)),
        )

    def rs_first(k, m, value):
        PT[k % 2, pl.ds(m * MB, MB), :] = value.astype(BF)
        rs_copy1(k, m).start()

    def rs_second(k, m):
        par = k % 2
        copy = rs_copy1(k, m)
        copy.wait_send()
        copy.wait_recv()
        for step in range(1, Hn):
            there = peer_zl(step)
            part = PT[par, chunk_rows(m, s * Hn + there), :].astype(F32) + RL1[
                par, m, pl.ds(there * R, R), :
            ].astype(F32)
            RSB[par, m, step - 1] = part.astype(BF)
            rs_copy2(k, m, step).start()

    def rs_third(k, m):
        par = k % 2
        total = PT[par, chunk_rows(m, own), :].astype(F32) + RL1[
            par, m, pl.ds(zl * R, R), :
        ].astype(F32)
        for step in range(1, Hn):
            copy = rs_copy2(k, m, step)
            copy.wait_send()
            copy.wait_recv()
            total = total + RL2[par, m, step - 1].astype(F32)
        return total

    def own_rows(m):
        return pl.ds(m * R, R)

    def rms(rows):
        return lax.rsqrt(jnp.mean(rows * rows, axis=-1, keepdims=True) + EPS)

    def gain(l, which):
        return GV[l, which : which + 1, :]

    def rms_back(l, which, rows, grad):
        inverse = rms(rows)
        scaled = grad * gain(l, which)
        back = inverse * scaled - rows * (inverse * inverse * inverse) * jnp.mean(
            scaled * rows, axis=-1, keepdims=True
        )
        DG[l, which : which + 1, :] += jnp.sum(grad * rows * inverse, axis=0, keepdims=True)
        return back

    def send_out(buf, l, out, which, m):
        src = buf.at[l, own_rows(m)]
        dst = out.at[zh * MH + m]
        to_self = (s == l) & (zh == s)

        @pl.when(to_self)
        def _():
            pltpu.make_async_copy(src, dst, o_rs.at[which, zh, m]).start()

        @pl.when(jnp.logical_not(to_self))
        def _():
            remote(
                src, dst, o_ss.at[which, l, m], o_rs.at[which, zh, m], (l, d, s * Hn + zl)
            ).start()

    def sent_out(buf, l, out, which, m):
        to_self = (s == l) & (zh == s)

        @pl.when(jnp.logical_not(to_self))
        def _():
            remote(
                buf.at[l, own_rows(m)],
                out.at[zh * MH + m],
                o_ss.at[which, l, m],
                o_rs.at[which, zh, m],
                core_dev,
            ).wait_send()

    lane_head = lax.broadcasted_iota(jnp.int32, (1, C), 1) // DH
    head_bf = [(lane_head == h).astype(F32).astype(BF) for h in range(NH)]
    head_f = [(lane_head == h).astype(F32) for h in range(NH)]

    def stack(rows):
        return jnp.concatenate([rows * head_bf[h] for h in range(NH)], axis=0)

    def unstack(wide):
        out = wide[0:DH] * head_f[0]
        for h in range(1, NH):
            out = out + wide[h * DH : (h + 1) * DH] * head_f[h]
        return out

    def tall(mask):
        return jnp.concatenate([mask] * NH, axis=0)

    def head_mean(values):
        row = lax.broadcasted_iota(jnp.int32, (C, C), 0) // DH
        col = lax.broadcasted_iota(jnp.int32, (C, C), 1) // DH
        same = jnp.where(row == col, 1.0 / DH, 0.0).astype(BF)
        high = values.astype(BF)
        low = (values - high.astype(F32)).astype(BF)
        return mm(high, same) + mm(low, same)

    def block_rows(b):
        return pl.ds(pl.multiple_of(b * BLOCK, BLOCK), BLOCK)

    def qkv_block(l, b):
        rows = block_rows(b)
        return (QKV[l, rows, 0:C], QKV[l, rows, C : 2 * C], QKV[l, rows, 2 * C : 3 * C])

    def softplus(values):
        return jnp.maximum(values, 0.0) + jnp.log(1.0 + jnp.exp(-jnp.abs(values)))

    def features(values):
        return softplus(values.astype(F32)).astype(BF)

    def diag_forward(b):
        q, k, v = qkv_block(0, b)
        scores = mm(stack(q), k, NT) * (1.0 / math.sqrt(DH))
        scores = jnp.where(tall(MSK[b]) > 0.5, scores, -1e9)
        top = jnp.max(scores, axis=-1, keepdims=True)
        weights = jnp.exp(scores - top)
        weights = (weights / jnp.sum(weights, axis=-1, keepdims=True)).astype(BF)
        AP[0, b] = weights
        O[0, block_rows(b), :] = unstack(mm(weights, v)).astype(BF)

    def diag_backward(b, grad_o):
        q, k, v = qkv_block(0, b)
        low = stack(grad_o.astype(BF))
        weights = AP[0, b]
        wide = weights.astype(F32)
        grad_v = mm(weights, low, TN)
        grad_w = mm(low, v, NT)
        grad_s = wide * (grad_w - jnp.sum(grad_w * wide, axis=-1, keepdims=True))
        grad_s = (grad_s * (1.0 / math.sqrt(DH))).astype(BF)
        grad_q = unstack(mm(grad_s, k))
        grad_k = mm(grad_s, stack(q), TN)
        rows = block_rows(b)
        GQKV[rows, 0:C] = grad_q.astype(BF)
        GQKV[rows, C : 2 * C] = grad_k.astype(BF)
        GQKV[rows, 2 * C : 3 * C] = grad_v.astype(BF)

    def fold(square):
        out = square[0:DH] * head_f[0]
        for h in range(1, NH):
            out = out + square[h * DH : (h + 1) * DH] * head_f[h]
        return out

    def unfold(flat):
        return stack(flat.astype(BF))

    def wide_lanes(column):
        return jnp.concatenate([column] * (C // 128), axis=1)

    def norm_state(b, state):
        q, k, v = qkv_block(1, b)
        ST[b] = state
        key = features(k)
        term = mm(key, (v.astype(F32) * wide_lanes(TAIL[b])).astype(BF), TN)
        return wide_lanes(KEEP[b, 0:1, :]) * state + fold(term)

    def norm_forward(b, passed):
        q, k, v = qkv_block(1, b)
        query, key = features(q), features(k)
        local = jnp.where(tall(MSK[b]) > 0.5, mm(stack(query), key, NT), 0.0).astype(BF)
        AP[1, b] = local
        state = ST[b] + passed * SIN[0]
        ST[b] = state
        mixed = unstack(mm(local, v)) + wide_lanes(CAR[b]) * mm(query, unfold(state))
        rows = block_rows(b)
        UU[rows, :] = mixed
        O[1, rows, :] = (mixed * lax.rsqrt(head_mean(mixed * mixed) + EPS)).astype(BF)
        return passed * wide_lanes(KEEP[b, 0:1, :])

    def norm_back_first(b, grad_o, state):
        rows = block_rows(b)
        mixed = UU[rows, :]
        scale = lax.rsqrt(head_mean(mixed * mixed) + EPS)
        grad = scale * grad_o - mixed * (scale * scale * scale) * head_mean(grad_o * mixed)
        low = grad.astype(BF)
        DU[rows, :] = low
        ST2_store(b, state)
        query = features(QKV[1, rows, 0:C])
        term = mm(query, (low.astype(F32) * wide_lanes(CAR[b])).astype(BF), TN)
        return wide_lanes(KEEP[b, 0:1, :]) * state + fold(term)

    def ST2_store(b, state):
        ST[NBH + b] = state

    def norm_back_second(b, passed):
        rows = block_rows(b)
        q, k, v = qkv_block(1, b)
        query, key = features(q), features(k)
        low = DU[rows, :]
        stacked = stack(low)
        grad_state = ST[NBH + b] + passed * SIN[1]
        grad_wide = unfold(grad_state)
        grad_a = jnp.where(tall(MSK[b]) > 0.5, mm(stacked, v, NT), 0.0).astype(BF)
        tail, carry = wide_lanes(TAIL[b]), wide_lanes(CAR[b])
        grad_q = unstack(mm(grad_a, key)) + carry * mm(low, unfold(ST[b]), NT)
        grad_k = mm(grad_a, stack(query), TN) + tail * mm(v, grad_wide, NT)
        grad_v = mm(AP[1, b], stacked, TN) + tail * mm(key, grad_wide)
        sig_q = 1.0 / (1.0 + jnp.exp(-q.astype(F32)))
        sig_k = 1.0 / (1.0 + jnp.exp(-k.astype(F32)))
        GQKV[rows, 0:C] = (grad_q * sig_q).astype(BF)
        GQKV[rows, C : 2 * C] = (grad_k * sig_k).astype(BF)
        GQKV[rows, 2 * C : 3 * C] = grad_v.astype(BF)
        return passed * wide_lanes(KEEP[b, 0:1, :])

    def masks():
        row = lax.broadcasted_iota(jnp.int32, (BLOCK, BLOCK), 0)
        col = lax.broadcasted_iota(jnp.int32, (BLOCK, BLOCK), 1)
        upper = (row <= col).astype(F32).astype(BF)
        start = marks[...].astype(BF)
        count_row = mm(start, upper)
        count_col = mm(upper, start, (((0,), (1,)), ((), ())))
        lane = lax.broadcasted_iota(jnp.int32, count_col.shape, 1)
        for b in range(NBH):
            c_row = count_row[b : b + 1, :]
            c_col = jnp.sum(jnp.where(lane == b, count_col, 0.0), axis=1, keepdims=True)
            last = jnp.sum(
                jnp.where(col[0:1] == BLOCK - 1, c_row, 0.0), axis=1, keepdims=True
            )
            MSK[b] = jnp.where((c_row == c_col) & (row >= col), 1.0, 0.0)
            CAR[b] = jnp.broadcast_to(jnp.where(c_col == 0.0, 1.0, 0.0), (BLOCK, 128))
            TAIL[b] = jnp.broadcast_to(jnp.where(c_col == last, 1.0, 0.0), (BLOCK, 128))
            KEEP[b] = jnp.broadcast_to(jnp.where(last == 0.0, 1.0, 0.0), (8, 128))

    def gains():
        GOWN[...] = gain_in[...]

        def copy(stage, src, dst, step, dev):
            return remote(src, dst, g_ss.at[stage, step - 1], g_rs.at[stage, step - 1], dev)

        for step in range(1, nd):
            copy(0, GOWN, GL1.at[step - 1], step, dp_dev(step)).start()
        total = GOWN[...]
        for step in range(1, nd):
            copy(0, GOWN, GL1.at[step - 1], step, dp_dev(step)).wait()
            total = total + GL1[step - 1]
        GOWN[...] = total
        for step in range(1, nt):
            copy(1, GOWN, GL2.at[step - 1], step, z_dev(step)).start()
        for step in range(1, nt):
            copy(1, GOWN, GL2.at[step - 1], step, z_dev(step)).wait()
            total = total + GL2[step - 1]
        GV[s] = total
        last = remote(GV.at[s], GV.at[s], g_ss.at[2, 0], g_rs.at[2, 0], core_dev)
        last.start()
        last.wait_send()
        got(GV.at[1 - s], g_rs.at[2, 0])

    def gain_grads():
        first = remote(DG.at[1 - s], DL0, g_ss.at[3, 0], g_rs.at[3, 0], core_dev)
        first.start()
        first.wait()
        total = DG[s] + DL0[...]
        DG[s] = total
        for step in range(1, nt):
            remote(
                DG.at[s], DL1.at[step - 1], g_ss.at[4, step - 1], g_rs.at[4, step - 1], z_dev(step)
            ).start()
        for step in range(1, nt):
            remote(
                DG.at[s], DL1.at[step - 1], g_ss.at[4, step - 1], g_rs.at[4, step - 1], z_dev(step)
            ).wait()
            total = total + DL1[step - 1]
        GOWN[...] = total
        for step in range(1, nd):
            remote(
                GOWN, DL2.at[step - 1], g_ss.at[5, step - 1], g_rs.at[5, step - 1], dp_dev(step)
            ).start()
        for step in range(1, nd):
            remote(
                GOWN, DL2.at[step - 1], g_ss.at[5, step - 1], g_rs.at[5, step - 1], dp_dev(step)
            ).wait()
            total = total + DL2[step - 1]
        out_gain[...] = total

    def loop(count, fn):
        def step(i, carry):
            fn(i)
            return carry

        lax.fori_loop(0, count, step, 0)

    def chunk(m):
        return pl.ds(pl.multiple_of(m * MB, BLOCK), MB)

    def w_cols(l, p):
        col, width = pieces[p]
        return W[l, :, col : col + width]

    def pass_state(slot, value, sender):
        near = sender
        SEND_STATE[slot] = value

        def copy():
            return remote(
                SEND_STATE.at[slot],
                SIN.at[slot],
                st_ss.at[slot],
                st_rs.at[slot],
                (s, d, (z + Hn) % nt),
            )

        @pl.when(zh == near)
        def _():
            SIN[slot] = jnp.zeros((DH, C), F32)
            copy().start()
            copy().wait_send()

        @pl.when(zh != near)
        def _():
            copy().wait_recv()

    @pl.when(s == 0)
    def _():
        spread_tokens(xin, XF)

    @pl.when(s == 1)
    def _():
        own_tokens(xin, XF, 0)

    for p in range(5):

        @pl.when(s == 0)
        def _():
            w_hand_out(0, p)

    masks()
    gains()
    for l in range(2):
        DG[l] = jnp.zeros((2, D), F32)

    @pl.when(s == 0)
    def _():
        forward_tokens(XF, 0)
        own_tokens(cot, GF.at[1], 1)

    @pl.when(s == 1)
    def _():
        await_tokens(xin, XF, 0)
        spread_tokens(cot, GF.at[1])

    for p in range(5):
        w_share(0, p)
    for p in range(5):

        @pl.when(s == 1)
        def _():
            w_hand_out(1, p)

    def input_rows(l, m):
        if l == 0:
            return XF[chunk_rows(m, own), :].astype(F32)
        return Y[0, own_rows(m), :].astype(F32)

    def forward(l, ag1, rs1, ag2, rs2, ag3):
        w_ready(l, 0)

        def qkv_chunk(m):
            if l == 0:
                rows = XF[chunk(m), :].astype(F32)
                N1[0, chunk(m), :] = (rows * rms(rows) * gain(0, 0)).astype(BF)
            else:
                ag_forward(ag1, N1.at[1], m)
                ag_wait(ag1, N1.at[1], m)
            QKV[l, chunk(m), :] = mm(N1[l, chunk(m), :], w_cols(l, 0)).astype(BF)

        def out_chunk(m):
            rs_first(rs1, m, mm(O[l, chunk(m), :], w_cols(l, 1), NT))

        if l == 0:

            def attend(m):
                qkv_chunk(m)
                for i in range(NB):
                    diag_forward(m * NB + i)

            loop(MH, attend)
            w_ready(l, 1)
            loop(MH, out_chunk)
        else:

            def states(m, state):
                qkv_chunk(m)
                for i in range(NB):
                    state = norm_state(m * NB + i, state)
                return state

            last = lax.fori_loop(0, MH, states, jnp.zeros((DH, C), F32))
            pass_state(0, last, 0)
            w_ready(l, 1)

            def attend(m, passed):
                for i in range(NB):
                    passed = norm_forward(m * NB + i, passed)
                out_chunk(m)
                return passed

            lax.fori_loop(0, MH, attend, jnp.ones((1, C), F32))

        def second(m):
            rs_second(rs1, m)

        loop(MH, second)

        def hidden_rows(m):
            rows = input_rows(l, m) + rs_third(rs1, m)
            H[l, own_rows(m), :] = rows
            N2[l, chunk_rows(m, own), :] = (rows * rms(rows) * gain(l, 1)).astype(BF)
            ag_send(ag2, N2.at[l], m)

        loop(MH, hidden_rows)
        w_ready(l, 2)
        w_ready(l, 3)
        w_ready(l, 4)

        def feed(m):
            ag_forward(ag2, N2.at[l], m)
            ag_wait(ag2, N2.at[l], m)
            rows = N2[l, chunk(m), :]
            gate = mm(rows, w_cols(l, 2))
            up = mm(rows, w_cols(l, 3))
            GATE[l, chunk(m), :] = gate.astype(BF)
            UP[l, chunk(m), :] = up.astype(BF)
            hidden = (gate * up).astype(BF)
            HID[l, chunk(m), :] = hidden
            rs_first(rs2, m, mm(hidden, w_cols(l, 4), NT))

        loop(MH, feed)

        def feed_second(m):
            rs_second(rs2, m)

        loop(MH, feed_second)

        def result(m):
            rows = (H[l, own_rows(m), :] + rs_third(rs2, m)).astype(BF)
            Y[l, own_rows(m), :] = rows
            send_out(Y, l, out_y, 0, m)
            if l == 0:
                wide = rows.astype(F32)
                N1[1, chunk_rows(m, own), :] = (wide * rms(wide) * gain(1, 0)).astype(BF)
                ag_send(ag3, N1.at[1], m)

        loop(MH, result)

    forward(0, None, 0, 0, 1, 1)
    for p in range(5):
        w_share(1, p)

    @pl.when(s == 1)
    def _():
        forward_tokens(GF.at[1], 1)

    @pl.when(s == 0)
    def _():
        await_tokens(cot, GF.at[1], 1)

    forward(1, 1, 2, 2, 3, None)

    RB = min(D, 256)

    def grad_weight(l, p, left, right):
        col, width = pieces[p]
        for r in range(D // RB):
            W[l, r * RB : (r + 1) * RB, col : col + width] = mm(
                left[:, r * RB : (r + 1) * RB], right, TN
            ).astype(BF)
        d_send(l, p)

    def backward(l, ag_in, rs1, ag2, rs2, ag_out):
        for p in range(5):
            w_shared(l, p)

        def feed_back(m):
            if l == 0:
                ag_forward(ag_in, GF.at[0], m)
                ag_wait(ag_in, GF.at[0], m)
            grad = mm(GF[l, chunk(m), :], w_cols(l, 4))
            GGU[chunk(m), 0:FP] = (grad * UP[l, chunk(m), :].astype(F32)).astype(BF)
            GGU[chunk(m), FP : 2 * FP] = (grad * GATE[l, chunk(m), :].astype(F32)).astype(BF)
            rs_first(
                rs1,
                m,
                mm(GGU[chunk(m), :], W[l, :, z_.oG : z_.oG + 2 * FP], NT),
            )

        loop(MH, feed_back)

        def second(m):
            rs_second(rs1, m)

        loop(MH, second)
        grad_weight(l, 4, GF[l], HID[l])

        def middle(m):
            rows = H[l, own_rows(m), :]
            grad = GF[l, chunk_rows(m, own), :].astype(F32) + rms_back(
                l, 1, rows, rs_third(rs1, m)
            )
            GH[own_rows(m), :] = grad
            GA[l, chunk_rows(m, own), :] = grad.astype(BF)
            ag_send(ag2, GA.at[l], m)

        loop(MH, middle)
        grad_weight(l, 2, N2[l], GGU[:, 0:FP])
        grad_weight(l, 3, N2[l], GGU[:, FP : 2 * FP])

        def grad_o(m):
            ag_forward(ag2, GA.at[l], m)
            ag_wait(ag2, GA.at[l], m)
            return mm(GA[l, chunk(m), :], w_cols(l, 1))

        def qkv_back(m):
            rs_first(rs2, m, mm(GQKV[chunk(m), :], w_cols(l, 0), NT))

        if l == 0:

            def attend(m):
                grad = grad_o(m)
                for i in range(NB):
                    diag_backward(m * NB + i, grad[i * BLOCK : (i + 1) * BLOCK])
                qkv_back(m)

            loop(MH, attend)
        else:

            def states(i, state):
                m = MH - 1 - i
                grad = grad_o(m)
                for j in reversed(range(NB)):
                    state = norm_back_first(m * NB + j, grad[j * BLOCK : (j + 1) * BLOCK], state)
                return state

            last = lax.fori_loop(0, MH, states, jnp.zeros((DH, C), F32))
            pass_state(1, last, 1)

            def attend(i, passed):
                m = MH - 1 - i
                for j in reversed(range(NB)):
                    passed = norm_back_second(m * NB + j, passed)
                qkv_back(m)
                return passed

            lax.fori_loop(0, MH, attend, jnp.ones((1, C), F32))

        def third(m):
            rs_second(rs2, m)

        loop(MH, third)
        grad_weight(l, 1, GA[l], O[l])
        grad_weight(l, 0, N1[l], GQKV[...])

        def result(m):
            grad = GH[own_rows(m), :] + rms_back(l, 0, input_rows(l, m), rs_third(rs2, m))
            low = grad.astype(BF)
            GX[l, own_rows(m), :] = low
            send_out(GX, l, out_g, 1, m)
            if l == 1:
                GF[0, chunk_rows(m, own), :] = low
                ag_send(ag_out, GF.at[0], m)

        loop(MH, result)

    backward(1, None, 4, 3, 5, 4)
    for p in (4, 2, 3, 1, 0):
        d_sum(1, p)
    backward(0, 4, 6, 5, 7, None)
    for p in (4, 2, 3, 1, 0):
        d_sum(0, p)
    gain_grads()

    for p in (4, 2, 3, 1, 0):
        d_final(p)
    for l in range(2):
        for p in range(5):
            d_sent(l, p)

            @pl.when(s == l)
            def _():
                w_handed_out(l, p)

    ags = ((0, N2.at[0]), (1, N1.at[1]), (2, N2.at[1]), (3, GA.at[1]), (4, GF.at[0]), (5, GA.at[0]))

    def finish(m):
        for k, buf in ags:
            ag_sent(k, buf, m)
        for l in range(2):
            sent_out(Y, l, out_y, 0, m)
            sent_out(GX, l, out_g, 1, m)
        for half in range(2):
            got(out_y.at[half * MH + m], o_rs.at[0, half, m])
            got(out_g.at[half * MH + m], o_rs.at[1, half, m])

    loop(MH, finish)
    for array, src, dst in ((0, xin, XF), (1, cot, GF.at[1])):

        @pl.when(s == array)
        def _():
            for m in range(MH):
                mine = dst.at[pl.ds(m * MB + z * R, R)]
                for step in range(1, nt):
                    copy = remote(
                        src.at[m], mine, x_ss.at[m, step - 1], x_rs.at[array, m, step - 1], core_dev
                    )
                    copy.wait_send()
                    remote(
                        mine, mine, x_fs.at[m, step - 1], x_rs.at[array, m, step - 1], core_dev
                    ).wait_send()


def solution(mesh):
    nd, nt = mesh.shape["dp"], mesh.shape["tensor"]

    def on_device(inputs, starts, cotangent, qkv_m, out_m, gateup_m, down_m, gain_m):
        z_ = Sizes(
            mesh,
            inputs.shape[3],
            inputs.shape[1],
            inputs.shape[2],
            qkv_m.shape[3],
            gateup_m.shape[3],
        )
        D, R, C, F, FP, Dr, M, MH, Hn, MB, T, NBH, N, NH = (
            z_.D,
            z_.R,
            z_.C,
            z_.F,
            z_.FP,
            z_.Dr,
            z_.M,
            z_.MH,
            z_.Hn,
            z_.MB,
            z_.T,
            z_.NBH,
            z_.N,
            z_.NH,
        )
        pad = ((0, 0), (0, FP - F))
        shard = jnp.concatenate(
            [
                qkv_m[0].reshape(Dr, 3 * C).astype(BF),
                out_m[0].T.astype(BF),
                jnp.pad(gateup_m[0, :, 0].astype(BF), pad),
                jnp.pad(gateup_m[0, :, 1].astype(BF), pad),
                jnp.pad(down_m[0].T.astype(BF), pad),
            ],
            axis=1,
        )
        half = lax.axis_index("tensor") // Hn
        marks = (
            lax.dynamic_slice_in_dim(starts[0], half * MH, MH, 0)
            .reshape(NBH, BLOCK)
            .astype(F32)
        )
        width = gain_m.shape[2]
        place = lax.axis_index("dp") * nt + lax.axis_index("tensor")
        low = gain_m[0].astype(BF).astype(F32)
        gain_in = jnp.where(
            jnp.arange(D)[None] // width == place, jnp.tile(low, (1, D // width)), 0.0
        )
        anywhere = pl.BlockSpec(memory_space=pl.ANY)
        vmem = pl.BlockSpec(memory_space=pltpu.VMEM)
        DMA = pltpu.SemaphoreType.DMA
        V = pltpu.VMEM
        scratch = [
            V((2, D, N), BF),
            V((2, nd - 1, Dr, N), BF),
            V((2, Dr, N), BF),
            V((T, D), BF),
            V((2, T, D), BF),
            V((2, T, D), BF),
            V((2, T, D), BF),
            V((2, T, 3 * C), BF),
            V((2, T, C), BF),
            V((2, T, FP), BF),
            V((2, T, FP), BF),
            V((2, T, FP), BF),
            V((2, MH * R, D), F32),
            V((2, MH * R, D), BF),
            V((2, T, D), BF),
            V((T, 2 * FP), BF),
            V((T, 3 * C), BF),
            V((MH * R, D), F32),
            V((2, MH * R, D), BF),
            V((2, T, D), BF),
            V((2, MH, Hn * R, D), BF),
            V((2, MH, Hn - 1, R, D), BF),
            V((2, MH, Hn - 1, R, D), BF),
            V((2, NBH, NH * BLOCK, BLOCK), BF),
            V((T, C), F32),
            V((T, C), BF),
            V((2 * NBH, DH, C), F32),
            V((2, DH, C), F32),
            V((2, DH, C), F32),
            V((NBH, BLOCK, BLOCK), F32),
            V((NBH, BLOCK, 128), F32),
            V((NBH, BLOCK, 128), F32),
            V((NBH, 8, 128), F32),
            V((nd - 1, 2, D), F32),
            V((nt - 1, 2, D), F32),
            V((2, 2, D), F32),
            V((2, D), F32),
            V((2, 2, D), F32),
            V((2, D), F32),
            V((nt - 1, 2, D), F32),
            V((nd - 1, 2, D), F32),
            DMA((2, MH)),
            DMA((MH, nt - 1)),
            DMA((2, MH, nt - 1)),
            DMA((MH, nt - 1)),
            DMA((5, 2)),
            DMA((2, 5)),
            DMA((2, 5, nd - 1)),
            DMA((2, 5, nd - 1)),
            DMA((6, MH, Hn)),
            DMA((6, MH, Hn - 1)),
            DMA((6, MH, nt)),
            DMA((8, MH)),
            DMA((8, MH)),
            DMA((8, MH, Hn - 1)),
            DMA((8, MH, Hn - 1)),
            DMA((2,)),
            DMA((2,)),
            DMA((2, 2, MH)),
            DMA((2, 2, MH)),
            DMA((2, 5, nd - 1)),
            DMA((2, 5, nd - 1)),
            DMA((2, 5)),
            DMA((5, 2)),
            DMA((6, max(nd, nt) - 1)),
            DMA((6, max(nd, nt) - 1)),
        ]
        out_y, out_g, out_w, out_gain = pl.pallas_call(
            functools.partial(body, z_),
            out_shape=(
                jax.ShapeDtypeStruct((M, R, D), BF),
                jax.ShapeDtypeStruct((M, R, D), BF),
                jax.ShapeDtypeStruct((Dr, N), F32),
                jax.ShapeDtypeStruct((2, D), F32),
            ),
            in_specs=[anywhere, anywhere, anywhere, vmem, vmem],
            out_specs=(anywhere, anywhere, vmem, vmem),
            scratch_shapes=scratch,
            compiler_params=pltpu.CompilerParams(
                collective_id=0, has_side_effects=True, vmem_limit_bytes=63 * 1024 * 1024
            ),
        )(shard, inputs[0], cotangent[0], marks, gain_in)
        gateup = jnp.stack(
            [out_w[:, z_.oG : z_.oG + F], out_w[:, z_.oU : z_.oU + F]], axis=1
        )
        gain_share = lax.dynamic_slice_in_dim(out_gain, place * width, width, 1)
        return (
            out_y[None, None],
            out_g[None, None],
            out_w[:, : 3 * C].reshape(1, Dr, 3, C),
            out_w[:, z_.oO : z_.oO + C].T[None],
            gateup[None],
            out_w[:, z_.oD : z_.oD + F].T[None],
            gain_share[None],
        )

    return jax.shard_map(
        on_device,
        mesh=mesh,
        in_specs=(
            P("dp", None, "tensor", None),
            P("dp", None, None),
            P("dp", None, "tensor", None),
            P("section", "dp", None, "tensor"),
            P("section", "tensor", "dp"),
            P("section", "dp", None, "tensor"),
            P("section", "tensor", "dp"),
            P("section", None, ("dp", "tensor")),
        ),
        out_specs=(
            P("section", "dp", None, "tensor", None),
            P("section", "dp", None, "tensor", None),
            P("section", "dp", None, "tensor"),
            P("section", "tensor", "dp"),
            P("section", "dp", None, "tensor"),
            P("section", "tensor", "dp"),
            P("section", None, ("dp", "tensor")),
        ),
        check_vma=False,
    )
```

time: 2760 us -> 456 us (0.17)
  waiting for transfers between devices: 1160 us -> 0 us
  blocking collectives: 688 us -> 0 us
  Pallas kernels: 0 us -> 433 us
  local copies, waits for them, and re-layouts: 346 us -> 19.6 us
  matrix products: 319 us -> 0 us
  other arithmetic: 185 us -> 2.16 us
    reduce_scatter x39 -> x0, waiting for transfers between devices: 1090 us -> none  [the longest x21 559 us: collect(): lax.psum_scatter(term_rows(jnp.int32(0), lax.axis_size('tensor') * row_co...]
    all_gather x44 -> x0, blocking collectives: 688 us -> none  [the longest x28 420 us: spread(): return lax.all_gather(row_block, 'tensor', axis=0, tiled=True)]
    pallas_call x0 -> x1, Pallas kernels: none -> 433 us  [on_device(): pl.pallas_call(functools.partial(body, z_), out_shape=(jax.ShapeDtypeStru...]
    dot_general x168 -> x0, matrix products: 319 us -> none  [the longest x14 39.3 us: layer_forward(): gate_up = jnp.dot(full_second, wgu_rows, preferred_element_type=jnp.float32)]
    reshape x63 -> x0, local copies, waits for them, and re-layouts: 95.8 us -> none  [blocks_of(): return flat_rows.reshape(-1, BLOCK, flat_rows.shape[1] // DH, DH)]
    another operation x78 -> x2, local copies, waits for them, and re-layouts: 90.7 us -> 0.08 us  [on_device(): jnp.tile(low, (1, D // width))]
    convert_element_type x38 -> x3, local copies, waits for them, and re-layouts: 57 us -> 0.9 us  [the longest x1 0.68 us: on_device(): marks = lax.dynamic_slice_in_dim(starts[0], half * MH, MH, 0).reshape(NBH...]
    all_gather x3 -> x0, waiting for transfers between devices: 54.8 us -> none  [the longest x1 29.2 us: fetch_weights(): lax.all_gather(down_master[0].astype(jnp.bfloat16), 'dp', axis=1, tiled=T...]
  transfers between devices with their start and end apart: 55 -> 0, of which waited for: 38 -> 0; matrix products, arithmetic and copies ran while one was open for 10% -> 0% of each run, Pallas kernels for 0% -> 0%
where the time goes in v2:
time: 456 us
  Pallas kernels  433 us (95%)
  local copies, waits for them, and re-layouts  19.6 us (4%)
    pallas_call x1, Pallas kernels, on_device(): pl.pallas_call(functools.partial(body, z_), out_shape=(jax.ShapeDtypeStru...  433 us
    unnamed x22, local copies, waits for them, and re-layouts  12.3 us

profile of v2, /device:TPU:0, one launch (start us, length us, event | category | flops | bytes accessed | tf_op | source)
XLA Modules:
  0.0 456.1 jit_solution(5277199169716548693)
XLA Ops:
  0.7 0.7 bitcast_convert_fusion
  1.4 0.7 convert_reduce_fusion
  2.1 0.7 convert_element_type.70.marks
  2.9 0.6 broadcast_select_fusion.gain_in
  3.5 1.2 copy.24
  4.7 1.3 copy.23
  6.3 0.3 copy.25
  6.7 0.8 constant_dynamic-update-slice_fusion
  7.5 0.7 bitcast_dynamic-update-slice_fusion
  8.2 0.8 pad_dynamic-update-slice_fusion.2
  9.0 0.8 pad_dynamic-update-slice_fusion.1
  9.8 0.8 pad_dynamic-update-slice_fusion.wsh
  10.7 433.5 %shard_map.135 = (bf16[6,48,1024]{2,1,0:T(8,128)(2,1)}, bf16[6,48,1024]{2,1,0:T(8,128)(2,1)}, f32[256,3328]{1,0:T(8,128)}, f32[2,1024]{1,0:T(2,128)}) custom-call(bf16[256,3328]{1,0:T(8,128)(2,1)} %pad_dynamic-update-slice_fusion.wsh, bf16[6,48,1024]{2,1,0:T(8,128)(2,1)} %bitcast.43, bf16[6,48,1024]{2,1,0:T(8,128)(2,1)} %bitcast.44, ...), custom_call_target="tpu_custom_call" | custom-call | tf_op jit(solution)/shard_map/pallas_call | solution.py:1150
  444.1 1.3 dynamic-slice_bitcast_fusion
  445.4 1.0 slice_bitcast_fusion.5
  446.4 0.8 copy.30
  447.3 1.2 slice.25
  448.4 1.8 slice_bitcast_fusion
  450.2 1.1 copy.32
  451.3 0.3 copy.28
  451.6 1.1 copy.29
  452.9 1.6 copy.31
  454.4 0.8 copy.39
  455.2 0.8 copy.40
  (15 shorter events, 0.6 us)
Async XLA Ops:
  0.6 5.5 %copy-start.1 = (f32[1,704,256]{2,1,0:T(8,128)S(1)}, f32[1,704,256]{2,1,0:T(8,128)}, u32[]{:S(2)}) copy-start(f32[1,704,256]{2,1,0:T(8,128)} %param.14) | copy-start | bytes 2162692
  3.5 2.8 copy-start
  452.8 1.6 copy-start.3
  452.9 2.4 copy-start.2

commit v3 on v2

--- a/solution.py
+++ b/solution.py
@@ -25,6 +25,15 @@
 
 def ceil_to(value, unit):
     return (value + unit - 1) // unit * unit
+
+
+def scoped(fn):
+    @functools.wraps(fn)
+    def inner(*args):
+        with jax.named_scope(fn.__name__):
+            return fn(*args)
+
+    return inner
 
 
 class Sizes:
@@ -48,6 +57,7 @@
             (self.oG, self.FP),
             (self.oU, self.FP),
             (self.oD, self.FP),
+            (0, 4 * cols),
         )
 
 
@@ -95,8 +105,7 @@
     CAR,
     TAIL,
     KEEP,
-    GL1,
-    GL2,
+    GL,
     GV,
     GOWN,
     DG,
@@ -128,6 +137,8 @@
     d2_rs,
     g_ss,
     g_rs,
+    gl_ss,
+    gl_rs,
 ):
     D, R, C, FP, Dr, MH, Hn, MB, T, NH, NB, NBH = (
         z_.D,
@@ -168,51 +179,50 @@
         return (zl + step) % Hn
 
     barrier = pltpu.get_barrier_semaphore()
-    for step in range(1, nt):
-        pl.semaphore_signal(barrier, inc=1, device_id=z_dev(step), device_id_type=MESH)
-    for step in range(1, nd):
-        pl.semaphore_signal(barrier, inc=1, device_id=dp_dev(step), device_id_type=MESH)
+
+    def section_dev(i):
+        return (s, (d + i // nt) % nd, (z + i % nt) % nt)
+
+    def greet(i, carry):
+        pl.semaphore_signal(barrier, inc=1, device_id=section_dev(i), device_id_type=MESH)
+        return carry
+
+    lax.fori_loop(1, nd * nt, greet, 0)
     pl.semaphore_signal(barrier, inc=1, device_id=core_dev, device_id_type=MESH)
     far_dev = (1 - s, d, (z + Hn) % nt)
     pl.semaphore_signal(barrier, inc=1, device_id=far_dev, device_id_type=MESH)
-    pl.semaphore_wait(barrier, nt - 1 + nd - 1 + 2)
-
-    def spread_tokens(src, dst):
+    pl.semaphore_wait(barrier, nd * nt + 1)
+
+    def own_tokens(src, dst, array):
         for m in range(MH):
             mine = dst.at[pl.ds(m * MB + z * R, R)]
-            pltpu.make_async_copy(src.at[zh * MH + m], mine, in_sem.at[s, m]).start()
+            pltpu.make_async_copy(src.at[zh * MH + m], mine, in_sem.at[array, m]).start()
+
+    def spread_tokens(src, dst, array):
+        for m in range(MH):
+            mine = dst.at[pl.ds(m * MB + z * R, R)]
             for step in range(1, nt):
                 other = (z + step) % nt
                 remote(
                     src.at[(other // Hn) * MH + m],
                     mine,
                     x_ss.at[m, step - 1],
-                    x_rs.at[s, m, step - 1],
+                    x_rs.at[array, m, step - 1],
                     z_dev(step),
                 ).start()
 
-    def forward_tokens(dst, array):
-        for m in range(MH):
-            got(dst.at[pl.ds(m * MB + z * R, R)], in_sem.at[array, m])
-            for step in range(1, nt):
-                rows = dst.at[pl.ds(m * MB + (z + nt - step) % nt * R, R)]
-                got(rows, x_rs.at[array, m, step - 1])
+    def await_tokens(dst, array, m):
+        got(dst.at[pl.ds(m * MB + z * R, R)], in_sem.at[array, m])
+        for step in range(1, nt):
+            rows = dst.at[pl.ds(m * MB + (z + nt - step) % nt * R, R)]
+            got(rows, x_rs.at[array, m, step - 1])
+
+            @pl.when(s == array)
+            def _():
                 remote(
                     rows, rows, x_fs.at[m, step - 1], x_rs.at[array, m, step - 1], core_dev
                 ).start()
 
-    def await_tokens(src, dst, array):
-        for m in range(MH):
-            got(dst.at[pl.ds(m * MB + z * R, R)], in_sem.at[array, m])
-            for step in range(1, nt):
-                rows = dst.at[pl.ds(m * MB + (z + nt - step) % nt * R, R)]
-                got(rows, x_rs.at[array, m, step - 1])
-
-    def own_tokens(src, dst, array):
-        for m in range(MH):
-            mine = dst.at[pl.ds(m * MB + z * R, R)]
-            pltpu.make_async_copy(src.at[zh * MH + m], mine, in_sem.at[array, m]).start()
-
     def w_rows(l, block, p):
         col, width = pieces[p]
         return W.at[l, pl.ds(block * Dr, Dr), pl.ds(col, width)]
@@ -221,137 +231,165 @@
         col, width = pieces[p]
         return wsh.at[:, pl.ds(col, width)]
 
-    def w_hand_out(l, p):
-        for half in range(2):
-            dest_z = half * Hn + zl
-            to_self = (zh == s) & (half == zh)
-
-            @pl.when(to_self)
-            def _():
-                pltpu.make_async_copy(shard_cols(p), w_rows(l, d, p), w1_rs.at[l, p]).start()
-
-            @pl.when(jnp.logical_not(to_self))
-            def _():
-                remote(
-                    shard_cols(p),
-                    w_rows(l, d, p),
-                    w1_ss.at[p, half],
-                    w1_rs.at[l, p],
-                    (zh, d, dest_z),
-                ).start()
+    def w_hand_near(l, p):
+        @pl.when(zh == s)
+        def _():
+            pltpu.make_async_copy(shard_cols(p), w_rows(l, d, p), w1_rs.at[l, p]).start()
+
+        @pl.when(zh != s)
+        def _():
+            w_hand(l, p, 0, core_dev).start()
+
+    def w_hand(l, p, which, dev):
+        return remote(
+            shard_cols(p), w_rows(l, d, p), w1_ss.at[p, which], w1_rs.at[l, p], dev
+        )
+
+    def w_hand_far(l, p):
+        w_hand(l, p, 1, (zh, d, (z + Hn) % nt)).start()
 
     def w_handed_out(l, p):
-        for half in range(2):
-            to_self = (zh == s) & (half == zh)
-
-            @pl.when(jnp.logical_not(to_self))
-            def _():
-                remote(
-                    shard_cols(p), w_rows(l, d, p), w1_ss.at[p, half], w1_rs.at[l, p], core_dev
-                ).wait_send()
+        @pl.when(zh != s)
+        def _():
+            w_hand(l, p, 0, core_dev).wait_send()
+
+        w_hand(l, p, 1, core_dev).wait_send()
+
+    square = nd == 4
+    half_rows = Dr // 2
+    dp_x, dp_y = d + 1 - 2 * (d % 2), (d + 2) % nd
+
+    def w_half(l, block, half, p):
+        col, width = pieces[p]
+        return W.at[l, pl.ds(block * Dr + half * half_rows, half_rows), pl.ds(col, width)]
+
+    def w_copy(l, p, k):
+        if not square:
+            rows, dev = w_rows(l, d, p), dp_dev(k + 1)
+        elif k < 2:
+            rows, dev = w_rows(l, d, p), (s, (dp_x, dp_y)[k], z)
+        elif k == 2:
+            rows, dev = w_half(l, dp_x, 0, p), (s, dp_y, z)
+        else:
+            rows, dev = w_half(l, dp_y, 1, p), (s, dp_x, z)
+        return remote(rows, rows, w2_ss.at[l, p, k], w2_rs.at[l, p, k], dev)
 
     def w_share(l, p):
         got(w_rows(l, d, p), w1_rs.at[l, p])
-
-        def one(step, carry):
-            remote(
-                w_rows(l, d, p),
-                w_rows(l, d, p),
-                w2_ss.at[l, p, step - 1],
-                w2_rs.at[l, p, step - 1],
-                dp_dev(step),
-            ).start()
-            return carry
-
-        lax.fori_loop(1, nd, one, 0)
+        for k in range(2 if square else nd - 1):
+            w_copy(l, p, k).start()
+
+    def w_forward(l, p):
+        if square:
+            got(w_rows(l, dp_x, p), w2_rs.at[l, p, 0])
+            w_copy(l, p, 2).start()
+            got(w_rows(l, dp_y, p), w2_rs.at[l, p, 1])
+            w_copy(l, p, 3).start()
 
     def w_ready(l, p):
-        def one(step, carry):
-            got(w_rows(l, (d + nd - step) % nd, p), w2_rs.at[l, p, step - 1])
-            return carry
-
-        lax.fori_loop(1, nd, one, 0)
+        if square:
+            got(w_half(l, 3 - d, 0, p), w2_rs.at[l, p, 2])
+            got(w_half(l, 3 - d, 1, p), w2_rs.at[l, p, 3])
+        else:
+            for step in range(1, nd):
+                got(w_rows(l, (d + nd - step) % nd, p), w2_rs.at[l, p, step - 1])
 
     def w_shared(l, p):
-        def one(step, carry):
-            remote(
-                w_rows(l, d, p),
-                w_rows(l, d, p),
-                w2_ss.at[l, p, step - 1],
-                w2_rs.at[l, p, step - 1],
-                dp_dev(step),
-            ).wait_send()
-            return carry
-
-        lax.fori_loop(1, nd, one, 0)
+        for k in range(4 if square else nd - 1):
+            w_copy(l, p, k).wait_send()
+
+    def pump(ops):
+        for what, l, p in ops:
+            with jax.named_scope(what + str(l) + str(p)):
+                {"s": w_share, "f": w_forward}[what](l, p)
+
+    near = s == zh
+    gathered = (5, 2, 3, 4)
+
+    def pump_near(ops):
+        pl.when(near)(lambda: pump(ops))
+
+    def pump_far(ops):
+        pl.when(jnp.logical_not(near))(lambda: pump(ops))
+
+    def d_copy(l, p, k):
+        col, width = pieces[p]
+        cols = pl.ds(col, width)
+        if not square:
+            src, dst, dev = w_rows(l, (d + k + 1) % nd, p), LW.at[l, k, :, cols], dp_dev(k + 1)
+        else:
+            first, second = pl.ds(0, half_rows), pl.ds(half_rows, half_rows)
+            block, half, slot, rows, to = (
+                (3 - d, 0, 2, first, dp_x),
+                (3 - d, 1, 2, second, dp_y),
+                (dp_x, 0, 0, first, dp_x),
+                (dp_y, 1, 1, second, dp_y),
+                (dp_y, 0, 1, first, dp_y),
+                (dp_x, 1, 0, second, dp_x),
+            )[k]
+            src, dst, dev = w_half(l, block, half, p), LW.at[l, slot, rows, cols], (s, to, z)
+        return remote(src, dst, d1_ss.at[l, p, k], d1_rs.at[l, p, k], dev)
 
     def d_send(l, p):
+        for k in range(4 if square else nd - 1):
+            d_copy(l, p, k).start()
+
+    @scoped
+    def d_mid(l, p):
+        if square:
+            col, width = pieces[p]
+            cols = pl.ds(col, width)
+            for k, block, half in ((0, dp_y, 0), (1, dp_x, 1)):
+                copy = d_copy(l, p, k)
+                copy.wait_recv()
+                rows = pl.ds(block * Dr + half * half_rows, half_rows)
+                arrived = LW[l, 2, half * half_rows : (half + 1) * half_rows, cols]
+                W[l, rows, cols] = (W[l, rows, cols].astype(F32) + arrived.astype(F32)).astype(BF)
+                d_copy(l, p, 4 + k).start()
+
+    def d_hop(l, p):
         col, width = pieces[p]
-
-        def one(step, carry):
-            remote(
-                w_rows(l, (d + step) % nd, p),
-                LW.at[l, step - 1, :, pl.ds(col, width)],
-                d1_ss.at[l, p, step - 1],
-                d1_rs.at[l, p, step - 1],
-                dp_dev(step),
-            ).start()
-            return carry
-
-        lax.fori_loop(1, nd, one, 0)
-
+        return remote(
+            w_rows(l, d, p),
+            L2.at[zh, :, pl.ds(col, width)],
+            d2_ss.at[l, p],
+            d2_rs.at[p, zh],
+            (l, d, s * Hn + zl),
+        )
+
+    @scoped
     def d_sum(l, p):
         col, width = pieces[p]
-
-        def one(step, carry):
-            got(LW.at[l, step - 1, :, pl.ds(col, width)], d1_rs.at[l, p, step - 1])
-            return carry
-
-        lax.fori_loop(1, nd, one, 0)
+        for k in (2, 3, 4, 5) if square else range(nd - 1):
+            d_copy(l, p, k).wait_recv()
         rows = pl.ds(d * Dr, Dr)
-        total = W[l, rows, pl.ds(col, width)].astype(F32)
-        for step in range(1, nd):
-            total = total + LW[l, step - 1, :, pl.ds(col, width)].astype(F32)
-        W[l, rows, pl.ds(col, width)] = total.astype(BF)
-        dest = L2.at[zh, :, pl.ds(col, width)]
+        cols = pl.ds(col, width)
+        total = W[l, rows, cols].astype(F32)
+        for slot in range(2 if square else nd - 1):
+            total = total + LW[l, slot, :, cols].astype(F32)
+        W[l, rows, cols] = total.astype(BF)
         to_self = (s == l) & (zh == s)
 
         @pl.when(to_self)
         def _():
-            pltpu.make_async_copy(w_rows(l, d, p), dest, d2_rs.at[p, zh]).start()
+            pltpu.make_async_copy(
+                w_rows(l, d, p), L2.at[zh, :, cols], d2_rs.at[p, zh]
+            ).start()
 
         @pl.when(jnp.logical_not(to_self))
         def _():
-            remote(
-                w_rows(l, d, p), dest, d2_ss.at[l, p], d2_rs.at[p, zh], (l, d, s * Hn + zl)
-            ).start()
+            d_hop(l, p).start()
 
     def d_sent(l, p):
-        col, width = pieces[p]
-
-        def one(step, carry):
-            remote(
-                w_rows(l, (d + step) % nd, p),
-                LW.at[l, step - 1, :, pl.ds(col, width)],
-                d1_ss.at[l, p, step - 1],
-                d1_rs.at[l, p, step - 1],
-                dp_dev(step),
-            ).wait_send()
-            return carry
-
-        lax.fori_loop(1, nd, one, 0)
+        for k in range(6 if square else nd - 1):
+            d_copy(l, p, k).wait_send()
         to_self = (s == l) & (zh == s)
 
         @pl.when(jnp.logical_not(to_self))
         def _():
-            remote(
-                w_rows(l, d, p),
-                L2.at[zh, :, pl.ds(col, width)],
-                d2_ss.at[l, p],
-                d2_rs.at[p, zh],
-                core_dev,
-            ).wait_send()
-
+            d_hop(l, p).wait_send()
+
+    @scoped
     def d_final(p):
         col, width = pieces[p]
         for half in range(2):
@@ -430,6 +468,11 @@
             ].astype(F32)
             RSB[par, m, step - 1] = part.astype(BF)
             rs_copy2(k, m, step).start()
+
+    def after(k, i, m):
+        @pl.when(i > 0)
+        def _():
+            rs_second(k, m)
 
     def rs_third(k, m):
         par = k % 2
@@ -576,7 +619,7 @@
         query, key = features(q), features(k)
         local = jnp.where(tall(MSK[b]) > 0.5, mm(stack(query), key, NT), 0.0).astype(BF)
         AP[1, b] = local
-        state = ST[b] + passed * SIN[0]
+        state = ST[b] + passed * SIN[0].astype(F32)
         ST[b] = state
         mixed = unstack(mm(local, v)) + wide_lanes(CAR[b]) * mm(query, unfold(state))
         rows = block_rows(b)
@@ -605,7 +648,7 @@
         query, key = features(q), features(k)
         low = DU[rows, :]
         stacked = stack(low)
-        grad_state = ST[NBH + b] + passed * SIN[1]
+        grad_state = ST[NBH + b] + passed * SIN[1].astype(F32)
         grad_wide = unfold(grad_state)
         grad_a = jnp.where(tall(MSK[b]) > 0.5, mm(stacked, v, NT), 0.0).astype(BF)
         tail, carry = wide_lanes(TAIL[b]), wide_lanes(CAR[b])
@@ -619,6 +662,7 @@
         GQKV[rows, 2 * C : 3 * C] = grad_v.astype(BF)
         return passed * wide_lanes(KEEP[b, 0:1, :])
 
+    @scoped
     def masks():
         row = lax.broadcasted_iota(jnp.int32, (BLOCK, BLOCK), 0)
         col = lax.broadcasted_iota(jnp.int32, (BLOCK, BLOCK), 1)
@@ -638,54 +682,79 @@
             TAIL[b] = jnp.broadcast_to(jnp.where(c_col == last, 1.0, 0.0), (BLOCK, 128))
             KEEP[b] = jnp.broadcast_to(jnp.where(last == 0.0, 1.0, 0.0), (8, 128))
 
-    def gains():
-        GOWN[...] = gain_in[...]
-
-        def copy(stage, src, dst, step, dev):
-            return remote(src, dst, g_ss.at[stage, step - 1], g_rs.at[stage, step - 1], dev)
-
-        for step in range(1, nd):
-            copy(0, GOWN, GL1.at[step - 1], step, dp_dev(step)).start()
-        total = GOWN[...]
-        for step in range(1, nd):
-            copy(0, GOWN, GL1.at[step - 1], step, dp_dev(step)).wait()
-            total = total + GL1[step - 1]
-        GOWN[...] = total
+    place = d * nt + z
+
+    def gain_copy(i):
+        return remote(GL.at[place], GL.at[place], gl_ss.at[i], gl_rs.at[i], section_dev(i))
+
+    def gains_out():
+        GL[place] = gain_in[...]
+
+        def one(i, carry):
+            gain_copy(i).start()
+            return carry
+
+        lax.fori_loop(1, nd * nt, one, 0)
+
+    @scoped
+    def gains_in():
+        def one(i, carry):
+            gain_copy(i).wait_send()
+            source = (d + nd - i // nt) % nd * nt + (z + nt - i % nt) % nt
+            got(GL.at[source], gl_rs.at[i])
+            return carry
+
+        lax.fori_loop(1, nd * nt, one, 0)
+        each = nd * nt * 128 // D
+        for t in range(D // 128):
+            total = GL[t * each]
+            for i in range(1, each):
+                total = total + GL[t * each + i]
+            GV[s, :, t * 128 : (t + 1) * 128] = total
+        gain_swap().start()
+
+    def gain_swap():
+        return remote(GV.at[s], GV.at[s], g_ss.at[2, 0], g_rs.at[2, 0], core_dev)
+
+    def gains_other():
+        gain_swap().wait_send()
+        got(GV.at[1 - s], g_rs.at[2, 0])
+
+    def dp_gain(step):
+        return remote(
+            GOWN, DL2.at[step - 1], g_ss.at[5, step - 1], g_rs.at[5, step - 1], dp_dev(step)
+        )
+
+    def core_gain():
+        return remote(DG.at[1 - s], DL0, g_ss.at[3, 0], g_rs.at[3, 0], core_dev)
+
+    def z_gain(step):
+        return remote(
+            DG.at[s], DL1.at[step - 1], g_ss.at[4, step - 1], g_rs.at[4, step - 1], z_dev(step)
+        )
+
+    @scoped
+    def gain_second():
+        core_gain().wait()
+        DG[s] = DG[s] + DL0[...]
         for step in range(1, nt):
-            copy(1, GOWN, GL2.at[step - 1], step, z_dev(step)).start()
+            z_gain(step).start()
+
+    @scoped
+    def gain_third():
+        total = DG[s]
         for step in range(1, nt):
-            copy(1, GOWN, GL2.at[step - 1], step, z_dev(step)).wait()
-            total = total + GL2[step - 1]
-        GV[s] = total
-        last = remote(GV.at[s], GV.at[s], g_ss.at[2, 0], g_rs.at[2, 0], core_dev)
-        last.start()
-        last.wait_send()
-        got(GV.at[1 - s], g_rs.at[2, 0])
-
-    def gain_grads():
-        first = remote(DG.at[1 - s], DL0, g_ss.at[3, 0], g_rs.at[3, 0], core_dev)
-        first.start()
-        first.wait()
-        total = DG[s] + DL0[...]
-        DG[s] = total
-        for step in range(1, nt):
-            remote(
-                DG.at[s], DL1.at[step - 1], g_ss.at[4, step - 1], g_rs.at[4, step - 1], z_dev(step)
-            ).start()
-        for step in range(1, nt):
-            remote(
-                DG.at[s], DL1.at[step - 1], g_ss.at[4, step - 1], g_rs.at[4, step - 1], z_dev(step)
-            ).wait()
+            z_gain(step).wait()
             total = total + DL1[step - 1]
         GOWN[...] = total
         for step in range(1, nd):
-            remote(
-                GOWN, DL2.at[step - 1], g_ss.at[5, step - 1], g_rs.at[5, step - 1], dp_dev(step)
-            ).start()
+            dp_gain(step).start()
+
+    @scoped
+    def gain_final():
+        total = GOWN[...]
         for step in range(1, nd):
-            remote(
-                GOWN, DL2.at[step - 1], g_ss.at[5, step - 1], g_rs.at[5, step - 1], dp_dev(step)
-            ).wait()
+            dp_gain(step).wait()
             total = total + DL2[step - 1]
         out_gain[...] = total
 
@@ -694,7 +763,8 @@
             fn(i)
             return carry
 
-        lax.fori_loop(0, count, step, 0)
+        with jax.named_scope(fn.__name__):
+            lax.fori_loop(0, count, step, 0)
 
     def chunk(m):
         return pl.ds(pl.multiple_of(m * MB, BLOCK), MB)
@@ -703,76 +773,164 @@
         col, width = pieces[p]
         return W[l, :, col : col + width]
 
+    @scoped
+    def state_copy(slot):
+        return remote(
+            SEND_STATE.at[slot],
+            SIN.at[slot],
+            st_ss.at[slot],
+            st_rs.at[slot],
+            (s, d, (z + Hn) % nt),
+        )
+
+    @scoped
     def pass_state(slot, value, sender):
-        near = sender
-        SEND_STATE[slot] = value
-
-        def copy():
-            return remote(
-                SEND_STATE.at[slot],
-                SIN.at[slot],
-                st_ss.at[slot],
-                st_rs.at[slot],
-                (s, d, (z + Hn) % nt),
-            )
-
-        @pl.when(zh == near)
-        def _():
-            SIN[slot] = jnp.zeros((DH, C), F32)
-            copy().start()
-            copy().wait_send()
-
-        @pl.when(zh != near)
-        def _():
-            copy().wait_recv()
-
-    @pl.when(s == 0)
-    def _():
-        spread_tokens(xin, XF)
-
-    @pl.when(s == 1)
-    def _():
-        own_tokens(xin, XF, 0)
-
-    for p in range(5):
-
-        @pl.when(s == 0)
-        def _():
-            w_hand_out(0, p)
-
+        SEND_STATE[slot] = value.astype(BF)
+
+        @pl.when(zh == sender)
+        def _():
+            SIN[slot] = jnp.zeros((DH, C), BF)
+            state_copy(slot).start()
+
+        @pl.when(zh != sender)
+        def _():
+            state_copy(slot).wait_recv()
+
+    outer = zh == zl
+    inner, far = jnp.logical_not(outer), jnp.logical_not(near)
+
+    def only(cond, fn):
+        pl.when(cond)(fn)
+
+    def hand_far(l, cond, ps):
+        def go():
+            for p in ps:
+                w_hand_far(l, p)
+
+        pl.when((s == l) & cond)(go)
+
+    gains_out()
+    hand_far(0, s == 0, [5])
+    for l in range(2):
+
+        @pl.when(s == l)
+        def _():
+            for p in gathered:
+                w_hand_near(l, p)
+
+    own_tokens(xin, XF, 0)
+    own_tokens(cot, GF.at[1], 1)
+
+    def x_out():
+        spread_tokens(xin, XF, 0)
+
+    def x_and_feed():
+        x_out()
+        for p in (2, 3, 4):
+            w_hand_far(0, p)
+
+    only((s == 0) & inner, x_and_feed)
     masks()
-    gains()
     for l in range(2):
         DG[l] = jnp.zeros((2, D), F32)
-
-    @pl.when(s == 0)
-    def _():
-        forward_tokens(XF, 0)
-        own_tokens(cot, GF.at[1], 1)
-
-    @pl.when(s == 1)
-    def _():
-        await_tokens(xin, XF, 0)
-        spread_tokens(cot, GF.at[1])
-
-    for p in range(5):
-        w_share(0, p)
-    for p in range(5):
-
-        @pl.when(s == 1)
-        def _():
-            w_hand_out(1, p)
+    pump_near([("s", 0, 5), ("s", 0, 2)])
+    gains_in()
+    pump_far([("s", 0, 5)])
+    only((s == 0) & outer & far, x_out)
+    pump([("f", 0, 5)])
+    hand_far(0, outer & far, [2, 3, 4])
+    pump_near([("f", 0, 2), ("s", 0, 3)])
+    only((s == 0) & outer & near, x_out)
+    pump_near([("f", 0, 3), ("s", 0, 4)])
+    hand_far(0, outer & near, [2, 3, 4])
+    only(s == 1, gains_other)
+
+    def cot_out():
+        spread_tokens(cot, GF.at[1], 1)
+
+    stage = {
+        (0, "attended"): lambda: (
+            pump_near([("f", 0, 4), ("s", 1, 5)]),
+            pump_far([("s", 0, 2), ("s", 0, 3), ("f", 0, 2), ("s", 0, 4)]),
+        ),
+        (0, "hidden"): lambda: (
+            hand_far(1, inner, gathered),
+            hand_far(1, outer, [5]),
+            pump_near([("f", 1, 5)]),
+            pump_far([("f", 0, 3), ("f", 0, 4)]),
+        ),
+        (0, "ready"): lambda: (
+            hand_far(1, outer, [2, 3]),
+            pump_near([("s", 1, 2)]),
+        ),
+        (0, "fed"): lambda: (
+            hand_far(1, outer, [4]),
+            pump_near([("f", 1, 2), ("s", 1, 3)]),
+            pump_far([("s", 1, 5)]),
+            only(s == 0, gains_other),
+        ),
+        (0, "result"): lambda: (
+            pump_near([("f", 1, 3), ("s", 1, 4)]),
+            pump_far([("f", 1, 5), ("s", 1, 2)]),
+        ),
+        (1, "states"): lambda: (
+            only(s == 1, cot_out),
+            pump_near([("f", 1, 4)]),
+            pump_far([("f", 1, 2), ("s", 1, 3)]),
+        ),
+        (1, "attended"): lambda: (pump_far([("f", 1, 3), ("s", 1, 4)]),),
+        (1, "hidden"): lambda: (pump_far([("f", 1, 4)]),),
+        (1, "ready"): lambda: (),
+        (1, "fed"): lambda: (),
+        (1, "result"): lambda: (),
+        "b1 second": lambda: (),
+        "b1 middle": lambda: (),
+        "b1 feed": lambda: (d_mid(1, 4),),
+        "b1 third": lambda: (d_mid(1, 2),),
+        "b1 end": lambda: (d_mid(1, 3),),
+        "b0 second": lambda: (d_mid(1, 0), d_mid(1, 1), d_sum(1, 4)),
+        "b0 middle": lambda: (d_sum(1, 2),),
+        "b0 feed": lambda: (d_sum(1, 3), d_mid(0, 4)),
+        "b0 third": lambda: (d_sum(1, 0), d_sum(1, 1)),
+        "b0 end": lambda: (
+            core_gain().start(),
+            d_mid(0, 2),
+            d_sum(0, 4),
+            gain_second(),
+            d_mid(0, 3),
+            d_sum(0, 2),
+            d_mid(0, 0),
+            d_sum(0, 3),
+            gain_third(),
+            d_mid(0, 1),
+            d_sum(0, 0),
+            d_sum(0, 1),
+        ),
+    }
 
     def input_rows(l, m):
         if l == 0:
             return XF[chunk_rows(m, own), :].astype(F32)
         return Y[0, own_rows(m), :].astype(F32)
 
+    def finish_layer(l, rs2, ag3):
+        def result(m):
+            rows = (H[l, own_rows(m), :] + rs_third(rs2, m)).astype(BF)
+            Y[l, own_rows(m), :] = rows
+            send_out(Y, l, out_y, 0, m)
+            if l == 0:
+                wide = rows.astype(F32)
+                N1[1, chunk_rows(m, own), :] = (wide * rms(wide) * gain(1, 0)).astype(BF)
+                ag_send(ag3, N1.at[1], m)
+
+        loop(MH, result)
+
     def forward(l, ag1, rs1, ag2, rs2, ag3):
-        w_ready(l, 0)
+        w_ready(l, 5)
 
         def qkv_chunk(m):
             if l == 0:
+                await_tokens(XF, 0, m)
                 rows = XF[chunk(m), :].astype(F32)
                 N1[0, chunk(m), :] = (rows * rms(rows) * gain(0, 0)).astype(BF)
             else:
@@ -789,10 +947,12 @@
                 qkv_chunk(m)
                 for i in range(NB):
                     diag_forward(m * NB + i)
+                out_chunk(m)
+                after(rs1, m, m - 1)
 
             loop(MH, attend)
-            w_ready(l, 1)
-            loop(MH, out_chunk)
+            rs_second(rs1, MH - 1)
+            stage[l, "attended"]()
         else:
 
             def states(m, state):
@@ -801,22 +961,22 @@
                     state = norm_state(m * NB + i, state)
                 return state
 
-            last = lax.fori_loop(0, MH, states, jnp.zeros((DH, C), F32))
+            with jax.named_scope('states'):
+                last = lax.fori_loop(0, MH, states, jnp.zeros((DH, C), F32))
             pass_state(0, last, 0)
-            w_ready(l, 1)
+            stage[l, "states"]()
 
             def attend(m, passed):
                 for i in range(NB):
                     passed = norm_forward(m * NB + i, passed)
                 out_chunk(m)
+                after(rs1, m, m - 1)
                 return passed
 
-            lax.fori_loop(0, MH, attend, jnp.ones((1, C), F32))
-
-        def second(m):
-            rs_second(rs1, m)
-
-        loop(MH, second)
+            with jax.named_scope('attend'):
+                lax.fori_loop(0, MH, attend, jnp.ones((1, C), F32))
+            rs_second(rs1, MH - 1)
+            stage[l, "attended"]()
 
         def hidden_rows(m):
             rows = input_rows(l, m) + rs_third(rs1, m)
@@ -825,9 +985,11 @@
             ag_send(ag2, N2.at[l], m)
 
         loop(MH, hidden_rows)
+        stage[l, "hidden"]()
         w_ready(l, 2)
         w_ready(l, 3)
         w_ready(l, 4)
+        stage[l, "ready"]()
 
         def feed(m):
             ag_forward(ag2, N2.at[l], m)
@@ -840,41 +1002,22 @@
             hidden = (gate * up).astype(BF)
             HID[l, chunk(m), :] = hidden
             rs_first(rs2, m, mm(hidden, w_cols(l, 4), NT))
+            after(rs2, m, m - 1)
 
         loop(MH, feed)
-
-        def feed_second(m):
-            rs_second(rs2, m)
-
-        loop(MH, feed_second)
-
-        def result(m):
-            rows = (H[l, own_rows(m), :] + rs_third(rs2, m)).astype(BF)
-            Y[l, own_rows(m), :] = rows
-            send_out(Y, l, out_y, 0, m)
-            if l == 0:
-                wide = rows.astype(F32)
-                N1[1, chunk_rows(m, own), :] = (wide * rms(wide) * gain(1, 0)).astype(BF)
-                ag_send(ag3, N1.at[1], m)
-
-        loop(MH, result)
+        rs_second(rs2, MH - 1)
+        stage[l, "fed"]()
+
+        if l == 0:
+            finish_layer(l, rs2, ag3)
+            stage[l, "result"]()
 
     forward(0, None, 0, 0, 1, 1)
-    for p in range(5):
-        w_share(1, p)
-
-    @pl.when(s == 1)
-    def _():
-        forward_tokens(GF.at[1], 1)
-
-    @pl.when(s == 0)
-    def _():
-        await_tokens(cot, GF.at[1], 1)
-
     forward(1, 1, 2, 2, 3, None)
 
     RB = min(D, 256)
 
+    @scoped
     def grad_weight(l, p, left, right):
         col, width = pieces[p]
         for r in range(D // RB):
@@ -884,13 +1027,16 @@
         d_send(l, p)
 
     def backward(l, ag_in, rs1, ag2, rs2, ag_out):
-        for p in range(5):
+        for p in gathered:
             w_shared(l, p)
 
-        def feed_back(m):
+        def feed_back(i):
+            m = MH - 1 - i
             if l == 0:
                 ag_forward(ag_in, GF.at[0], m)
                 ag_wait(ag_in, GF.at[0], m)
+            else:
+                await_tokens(GF.at[1], 1, m)
             grad = mm(GF[l, chunk(m), :], w_cols(l, 4))
             GGU[chunk(m), 0:FP] = (grad * UP[l, chunk(m), :].astype(F32)).astype(BF)
             GGU[chunk(m), FP : 2 * FP] = (grad * GATE[l, chunk(m), :].astype(F32)).astype(BF)
@@ -899,16 +1045,17 @@
                 m,
                 mm(GGU[chunk(m), :], W[l, :, z_.oG : z_.oG + 2 * FP], NT),
             )
+            after(rs1, i, m + 1)
 
         loop(MH, feed_back)
-
-        def second(m):
-            rs_second(rs1, m)
-
-        loop(MH, second)
+        rs_second(rs1, 0)
         grad_weight(l, 4, GF[l], HID[l])
-
-        def middle(m):
+        if l == 1:
+            finish_layer(1, 3, None)
+        stage[f"b{l} second"]()
+
+        def middle(i):
+            m = MH - 1 - i
             rows = H[l, own_rows(m), :]
             grad = GF[l, chunk_rows(m, own), :].astype(F32) + rms_back(
                 l, 1, rows, rs_third(rs1, m)
@@ -918,24 +1065,28 @@
             ag_send(ag2, GA.at[l], m)
 
         loop(MH, middle)
+        stage[f"b{l} middle"]()
         grad_weight(l, 2, N2[l], GGU[:, 0:FP])
         grad_weight(l, 3, N2[l], GGU[:, FP : 2 * FP])
+        stage[f"b{l} feed"]()
 
         def grad_o(m):
             ag_forward(ag2, GA.at[l], m)
             ag_wait(ag2, GA.at[l], m)
             return mm(GA[l, chunk(m), :], w_cols(l, 1))
 
-        def qkv_back(m):
+        def qkv_back(i, m):
             rs_first(rs2, m, mm(GQKV[chunk(m), :], w_cols(l, 0), NT))
+            after(rs2, i, m + 1)
 
         if l == 0:
 
-            def attend(m):
+            def attend(i):
+                m = MH - 1 - i
                 grad = grad_o(m)
-                for i in range(NB):
-                    diag_backward(m * NB + i, grad[i * BLOCK : (i + 1) * BLOCK])
-                qkv_back(m)
+                for j in range(NB):
+                    diag_backward(m * NB + j, grad[j * BLOCK : (j + 1) * BLOCK])
+                qkv_back(i, m)
 
             loop(MH, attend)
         else:
@@ -947,26 +1098,27 @@
                     state = norm_back_first(m * NB + j, grad[j * BLOCK : (j + 1) * BLOCK], state)
                 return state
 
-            last = lax.fori_loop(0, MH, states, jnp.zeros((DH, C), F32))
+            with jax.named_scope("states"):
+                last = lax.fori_loop(0, MH, states, jnp.zeros((DH, C), F32))
             pass_state(1, last, 1)
 
             def attend(i, passed):
                 m = MH - 1 - i
                 for j in reversed(range(NB)):
                     passed = norm_back_second(m * NB + j, passed)
-                qkv_back(m)
+                qkv_back(i, m)
                 return passed
 
-            lax.fori_loop(0, MH, attend, jnp.ones((1, C), F32))
-
-        def third(m):
-            rs_second(rs2, m)
-
-        loop(MH, third)
+            with jax.named_scope("attend"):
+                lax.fori_loop(0, MH, attend, jnp.ones((1, C), F32))
+
+        rs_second(rs2, 0)
+        stage[f"b{l} third"]()
+        grad_weight(l, 0, N1[l], GQKV[...])
         grad_weight(l, 1, GA[l], O[l])
-        grad_weight(l, 0, N1[l], GQKV[...])
-
-        def result(m):
+
+        def result(i):
+            m = MH - 1 - i
             grad = GH[own_rows(m), :] + rms_back(l, 0, input_rows(l, m), rs_third(rs2, m))
             low = grad.astype(BF)
             GX[l, own_rows(m), :] = low
@@ -976,26 +1128,30 @@
                 ag_send(ag_out, GF.at[0], m)
 
         loop(MH, result)
+        stage[f"b{l} end"]()
 
     backward(1, None, 4, 3, 5, 4)
-    for p in (4, 2, 3, 1, 0):
-        d_sum(1, p)
     backward(0, 4, 6, 5, 7, None)
-    for p in (4, 2, 3, 1, 0):
-        d_sum(0, p)
-    gain_grads()
-
-    for p in (4, 2, 3, 1, 0):
+
+    for p in (4, 2, 3, 0, 1):
         d_final(p)
+    gain_final()
     for l in range(2):
         for p in range(5):
             d_sent(l, p)
+        for p in gathered:
 
             @pl.when(s == l)
             def _():
                 w_handed_out(l, p)
 
     ags = ((0, N2.at[0]), (1, N1.at[1]), (2, N2.at[1]), (3, GA.at[1]), (4, GF.at[0]), (5, GA.at[0]))
+
+    for slot in range(2):
+
+        @pl.when(zh == slot)
+        def _():
+            state_copy(slot).wait_send()
 
     def finish(m):
         for k, buf in ags:
@@ -1072,8 +1228,9 @@
         width = gain_m.shape[2]
         place = lax.axis_index("dp") * nt + lax.axis_index("tensor")
         low = gain_m[0].astype(BF).astype(F32)
+        each = 128 // width
         gain_in = jnp.where(
-            jnp.arange(D)[None] // width == place, jnp.tile(low, (1, D // width)), 0.0
+            jnp.arange(128)[None] // width == place % each, jnp.tile(low, (1, each)), 0.0
         )
         anywhere = pl.BlockSpec(memory_space=pl.ANY)
         vmem = pl.BlockSpec(memory_space=pltpu.VMEM)
@@ -1107,14 +1264,13 @@
             V((T, C), F32),
             V((T, C), BF),
             V((2 * NBH, DH, C), F32),
-            V((2, DH, C), F32),
-            V((2, DH, C), F32),
+            V((2, DH, C), BF),
+            V((2, DH, C), BF),
             V((NBH, BLOCK, BLOCK), F32),
             V((NBH, BLOCK, 128), F32),
             V((NBH, BLOCK, 128), F32),
             V((NBH, 8, 128), F32),
-            V((nd - 1, 2, D), F32),
-            V((nt - 1, 2, D), F32),
+            V((nd * nt, 2, 128), F32),
             V((2, 2, D), F32),
             V((2, D), F32),
             V((2, 2, D), F32),
@@ -1125,10 +1281,10 @@
             DMA((MH, nt - 1)),
             DMA((2, MH, nt - 1)),
             DMA((MH, nt - 1)),
-            DMA((5, 2)),
-            DMA((2, 5)),
-            DMA((2, 5, nd - 1)),
-            DMA((2, 5, nd - 1)),
+            DMA((6, 2)),
+            DMA((2, 6)),
+            DMA((2, 6, max(4, nd - 1))),
+            DMA((2, 6, max(4, nd - 1))),
             DMA((6, MH, Hn)),
             DMA((6, MH, Hn - 1)),
             DMA((6, MH, nt)),
@@ -1140,12 +1296,14 @@
             DMA((2,)),
             DMA((2, 2, MH)),
             DMA((2, 2, MH)),
-            DMA((2, 5, nd - 1)),
-            DMA((2, 5, nd - 1)),
+            DMA((2, 5, max(6, nd - 1))),
+            DMA((2, 5, max(6, nd - 1))),
             DMA((2, 5)),
             DMA((5, 2)),
             DMA((6, max(nd, nt) - 1)),
             DMA((6, max(nd, nt) - 1)),
+            DMA((nd * nt,)),
+            DMA((nd * nt,)),
         ]
         out_y, out_g, out_w, out_gain = pl.pallas_call(
             functools.partial(body, z_),

time: 456 us -> 328 us (0.72)
  Pallas kernels: 433 us -> 305 us
    pallas_call x1, Pallas kernels: 433 us -> 305 us  [on_device(): pl.pallas_call(functools.partial(body, z_), out_shape=(jax.ShapeDtypeStru...]
where the time goes in v3:
time: 328 us
  Pallas kernels  305 us (93%)
  local copies, waits for them, and re-layouts  19.7 us (6%)
    pallas_call x1, Pallas kernels, on_device(): pl.pallas_call(functools.partial(body, z_), out_shape=(jax.ShapeDtypeStru...  305 us
    unnamed x22, local copies, waits for them, and re-layouts  12.3 us

profile of v3, /device:TPU:0, one launch (start us, length us, event | category | flops | bytes accessed | tf_op | source)
XLA Modules:
  0.0 328.0 jit_solution(3385229170495442907)
XLA Ops:
  0.7 0.7 bitcast_convert_fusion
  1.5 0.6 broadcast_select_fusion.gain_in
  2.1 0.7 convert_reduce_fusion
  2.8 0.7 convert_element_type.70.marks
  3.5 1.2 copy.24
  4.6 1.3 copy.23
  6.3 0.3 copy.25
  6.6 0.8 constant_dynamic-update-slice_fusion
  7.5 0.7 bitcast_dynamic-update-slice_fusion
  8.2 0.8 pad_dynamic-update-slice_fusion.2
  9.0 0.8 pad_dynamic-update-slice_fusion.1
  9.8 0.8 pad_dynamic-update-slice_fusion.wsh
  10.6 305.4 %shard_map.135 = (bf16[6,48,1024]{2,1,0:T(8,128)(2,1)}, bf16[6,48,1024]{2,1,0:T(8,128)(2,1)}, f32[256,3328]{1,0:T(8,128)}, f32[2,1024]{1,0:T(2,128)}) custom-call(bf16[256,3328]{1,0:T(8,128)(2,1)} %pad_dynamic-update-slice_fusion.wsh, bf16[6,48,1024]{2,1,0:T(8,128)(2,1)} %bitcast.43, bf16[6,48,1024]{2,1,0:T(8,128)(2,1)} %bitcast.44, ...), custom_call_target="tpu_custom_call" | custom-call | tf_op jit(solution)/shard_map/pallas_call | solution.py:1308
  316.1 1.3 dynamic-slice_bitcast_fusion
  317.4 1.0 slice_bitcast_fusion.5
  318.3 0.8 copy.30
  319.2 1.2 slice.25
  320.4 1.8 slice_bitcast_fusion
  322.1 1.1 copy.32
  323.2 0.3 copy.28
  323.5 1.1 copy.29
  324.8 1.6 copy.31
  326.3 0.8 copy.39
  327.2 0.8 copy.40
  (15 shorter events, 0.6 us)
Async XLA Ops:
  0.6 5.5 %copy-start.1 = (f32[1,704,256]{2,1,0:T(8,128)S(1)}, f32[1,704,256]{2,1,0:T(8,128)}, u32[]{:S(2)}) copy-start(f32[1,704,256]{2,1,0:T(8,128)} %param.14) | copy-start | bytes 2162692
  3.5 2.8 copy-start
  324.8 1.6 copy-start.3
  324.8 2.4 copy-start.2

commit v4 on v3

--- a/solution.py
+++ b/solution.py
@@ -40,7 +40,7 @@
     def __init__(self, mesh, model, micro, rows, cols, hidden):
         self.nd, self.nt = mesh.shape["dp"], mesh.shape["tensor"]
         self.D, self.M, self.R, self.C, self.F = model, micro, rows, cols, hidden
-        self.FP = ceil_to(hidden, 128)
+        self.GUw, self.Dw = ceil_to(2 * hidden, 128), ceil_to(hidden, 128)
         self.Dr = model // self.nd
         self.MH, self.Hn = micro // 2, self.nt // 2
         self.MB = rows * self.nt
@@ -49,29 +49,40 @@
         self.NB = self.MB // BLOCK
         self.NBH = self.MH * self.NB
         self.oO, self.oG = 3 * cols, 4 * cols
-        self.oU, self.oD = self.oG + self.FP, self.oG + 2 * self.FP
-        self.N = self.oG + 3 * self.FP
+        self.oD = self.oG + self.GUw
+        self.N = self.oD + self.Dw
+        first = ceil_to(self.GUw // 2, 128)
         self.pieces = (
             (0, 3 * cols),
             (self.oO, cols),
-            (self.oG, self.FP),
-            (self.oU, self.FP),
-            (self.oD, self.FP),
+            (self.oG, first),
+            (self.oG + first, self.GUw - first),
+            (self.oD, self.Dw),
             (0, 4 * cols),
         )
 
 
 def body(
     z_,
-    wsh,
+    qkv_in,
+    o_in,
+    gu_in,
+    d_in,
     xin,
     cot,
-    marks,
+    starts_in,
     gain_in,
     out_y,
     out_g,
-    out_w,
+    out_qkv,
+    out_o,
+    out_gu,
+    out_d,
     out_gain,
+    MQ,
+    MO,
+    MGU,
+    MD,
     W,
     LW,
     L2,
@@ -81,8 +92,7 @@
     N2,
     QKV,
     O,
-    GATE,
-    UP,
+    GU,
     HID,
     H,
     Y,
@@ -139,12 +149,13 @@
     g_rs,
     gl_ss,
     gl_rs,
+    m_sem,
 ):
-    D, R, C, FP, Dr, MH, Hn, MB, T, NH, NB, NBH = (
+    D, R, C, F, Dr, MH, Hn, MB, T, NH, NB, NBH = (
         z_.D,
         z_.R,
         z_.C,
-        z_.FP,
+        z_.F,
         z_.Dr,
         z_.MH,
         z_.Hn,
@@ -178,6 +189,15 @@
     def peer_zl(step):
         return (zl + step) % Hn
 
+    masters = (
+        pltpu.make_async_copy(qkv_in, MQ, m_sem.at[0]),
+        pltpu.make_async_copy(o_in, MO, m_sem.at[1]),
+        pltpu.make_async_copy(gu_in, MGU, m_sem.at[2]),
+        pltpu.make_async_copy(d_in, MD, m_sem.at[3]),
+    )
+    for copy in masters:
+        copy.start()
+
     barrier = pltpu.get_barrier_semaphore()
 
     def section_dev(i):
@@ -229,7 +249,7 @@
 
     def shard_cols(p):
         col, width = pieces[p]
-        return wsh.at[:, pl.ds(col, width)]
+        return L2.at[0, :, pl.ds(col, width)]
 
     def w_hand_near(l, p):
         @pl.when(zh == s)
@@ -347,18 +367,32 @@
                 W[l, rows, cols] = (W[l, rows, cols].astype(F32) + arrived.astype(F32)).astype(BF)
                 d_copy(l, p, 4 + k).start()
 
-    def d_hop(l, p):
+    part_rows = Dr // 4
+
+    def d_hop(l, p, q):
         col, width = pieces[p]
-        return remote(
-            w_rows(l, d, p),
-            L2.at[zh, :, pl.ds(col, width)],
-            d2_ss.at[l, p],
-            d2_rs.at[p, zh],
-            (l, d, s * Hn + zl),
+        cols = pl.ds(col, width)
+        return (
+            W.at[l, pl.ds(d * Dr + q * part_rows, part_rows), cols],
+            L2.at[zh, pl.ds(q * part_rows, part_rows), cols],
+            d2_ss.at[l, p, q],
+            d2_rs.at[p, zh, q],
         )
 
+    def d_pass(l, p, q):
+        src, dst, ssem, rsem = d_hop(l, p, q)
+        to_self = (s == l) & (zh == s)
+
+        @pl.when(to_self)
+        def _():
+            pltpu.make_async_copy(src, dst, rsem).start()
+
+        @pl.when(jnp.logical_not(to_self))
+        def _():
+            remote(src, dst, ssem, rsem, (l, d, s * Hn + zl)).start()
+
     @scoped
-    def d_sum(l, p):
+    def d_total_rows(l, p):
         col, width = pieces[p]
         for k in (2, 3, 4, 5) if square else range(nd - 1):
             d_copy(l, p, k).wait_recv()
@@ -368,17 +402,11 @@
         for slot in range(2 if square else nd - 1):
             total = total + LW[l, slot, :, cols].astype(F32)
         W[l, rows, cols] = total.astype(BF)
-        to_self = (s == l) & (zh == s)
-
-        @pl.when(to_self)
-        def _():
-            pltpu.make_async_copy(
-                w_rows(l, d, p), L2.at[zh, :, cols], d2_rs.at[p, zh]
-            ).start()
-
-        @pl.when(jnp.logical_not(to_self))
-        def _():
-            d_hop(l, p).start()
+
+    def d_sum(l, p):
+        d_total_rows(l, p)
+        for q in range(4):
+            d_pass(l, p, q)
 
     def d_sent(l, p):
         for k in range(6 if square else nd - 1):
@@ -387,15 +415,58 @@
 
         @pl.when(jnp.logical_not(to_self))
         def _():
-            d_hop(l, p).wait_send()
+            for q in range(4):
+                remote(*d_hop(l, p, q), core_dev).wait_send()
+
+    outs = (
+        pltpu.make_async_copy(MQ, out_qkv, m_sem.at[0]),
+        pltpu.make_async_copy(MO, out_o, m_sem.at[1]),
+        pltpu.make_async_copy(MGU, out_gu, m_sem.at[2]),
+        pltpu.make_async_copy(MD, out_d, m_sem.at[3]),
+    )
+
+    def d_arrived(p):
+        col, width = pieces[p]
+        for half in range(2):
+            for q in range(4):
+                rows = pl.ds(q * part_rows, part_rows)
+                got(L2.at[half, rows, pl.ds(col, width)], d2_rs.at[p, half, q])
+
+    def d_total(col, width):
+        return L2[0, :, col : col + width].astype(F32) + L2[1, :, col : col + width].astype(F32)
 
     @scoped
     def d_final(p):
-        col, width = pieces[p]
-        for half in range(2):
-            got(L2.at[half, :, pl.ds(col, width)], d2_rs.at[p, half])
-        cols = pl.ds(col, width)
-        out_w[:, cols] = L2[0, :, cols].astype(F32) + L2[1, :, cols].astype(F32)
+        d_arrived(p)
+        if p == 0:
+            for j in range(3):
+                MQ[j] = d_total(j * C, C)
+            outs[0].start()
+        elif p == 1:
+            MO[...] = d_total(z_.oO, C).T
+            outs[1].start()
+        elif p == 3:
+            MGU[...] = d_total(z_.oG, z_.GUw).T[: 2 * F]
+            outs[2].start()
+        elif p == 4:
+            MD[...] = d_total(z_.oD, z_.Dw).T[:F]
+            outs[3].start()
+
+    def shard_attention():
+        masters[0].wait()
+        masters[1].wait()
+        for j in range(3):
+            L2[0, :, j * C : (j + 1) * C] = MQ[j].astype(BF)
+        L2[0, :, z_.oO : z_.oG] = MO[...].T.astype(BF)
+
+    def shard_feed():
+        masters[2].wait()
+        masters[3].wait()
+        for ref, col, width, rows in ((MGU, z_.oG, z_.GUw, 2 * F), (MD, z_.oD, z_.Dw, F)):
+            value = ref[...]
+            if width > rows:
+                value = jnp.concatenate([value, jnp.zeros((width - rows, Dr), F32)], axis=0)
+            L2[0, :, col : col + width] = value.T.astype(BF)
 
     def chunk_rows(m, c):
         return pl.ds(m * MB + c * R, R)
@@ -666,21 +737,28 @@
     def masks():
         row = lax.broadcasted_iota(jnp.int32, (BLOCK, BLOCK), 0)
         col = lax.broadcasted_iota(jnp.int32, (BLOCK, BLOCK), 1)
-        upper = (row <= col).astype(F32).astype(BF)
-        start = marks[...].astype(BF)
-        count_row = mm(start, upper)
-        count_col = mm(upper, start, (((0,), (1,)), ((), ())))
-        lane = lax.broadcasted_iota(jnp.int32, count_col.shape, 1)
-        for b in range(NBH):
-            c_row = count_row[b : b + 1, :]
-            c_col = jnp.sum(jnp.where(lane == b, count_col, 0.0), axis=1, keepdims=True)
-            last = jnp.sum(
-                jnp.where(col[0:1] == BLOCK - 1, c_row, 0.0), axis=1, keepdims=True
-            )
-            MSK[b] = jnp.where((c_row == c_col) & (row >= col), 1.0, 0.0)
-            CAR[b] = jnp.broadcast_to(jnp.where(c_col == 0.0, 1.0, 0.0), (BLOCK, 128))
-            TAIL[b] = jnp.broadcast_to(jnp.where(c_col == last, 1.0, 0.0), (BLOCK, 128))
-            KEEP[b] = jnp.broadcast_to(jnp.where(last == 0.0, 1.0, 0.0), (8, 128))
+        token = lax.broadcasted_iota(jnp.int32, (MB, BLOCK), 0)
+        lane = lax.broadcasted_iota(jnp.int32, (MB, BLOCK), 1)
+        start = jnp.concatenate([starts_in[zh * MH + m] for m in range(MH)], axis=0)
+        start = start.astype(F32).astype(BF)
+        chunk_lane = lax.broadcasted_iota(jnp.int32, (BLOCK, MH), 1)
+        for j in range(NB):
+            upper = ((token // BLOCK == j) & (token % BLOCK <= lane)).astype(F32).astype(BF)
+            count_row = mm(start, upper)
+            count_col = mm(upper, start, (((0,), (1,)), ((), ())))
+            for m in range(MH):
+                b = m * NB + j
+                c_row = count_row[m : m + 1, :]
+                c_col = jnp.sum(
+                    jnp.where(chunk_lane == m, count_col, 0.0), axis=1, keepdims=True
+                )
+                last = jnp.sum(
+                    jnp.where(col[0:1] == BLOCK - 1, c_row, 0.0), axis=1, keepdims=True
+                )
+                MSK[b] = jnp.where((c_row == c_col) & (row >= col), 1.0, 0.0)
+                CAR[b] = jnp.broadcast_to(jnp.where(c_col == 0.0, 1.0, 0.0), (BLOCK, 128))
+                TAIL[b] = jnp.broadcast_to(jnp.where(c_col == last, 1.0, 0.0), (BLOCK, 128))
+                KEEP[b] = jnp.broadcast_to(jnp.where(last == 0.0, 1.0, 0.0), (8, 128))
 
     place = d * nt + z
 
@@ -688,7 +766,11 @@
         return remote(GL.at[place], GL.at[place], gl_ss.at[i], gl_rs.at[i], section_dev(i))
 
     def gains_out():
-        GL[place] = gain_in[...]
+        width = gain_in.shape[1]
+        row = lax.broadcasted_iota(jnp.int32, (width, 128), 0)
+        col = lax.broadcasted_iota(jnp.int32, (width, 128), 1)
+        spot = (col % width == row) & (col // width == place % (128 // width))
+        GL[place] = mm(gain_in[...].astype(BF), spot.astype(F32).astype(BF))
 
         def one(i, carry):
             gain_copy(i).start()
@@ -756,7 +838,15 @@
         for step in range(1, nd):
             dp_gain(step).wait()
             total = total + DL2[step - 1]
-        out_gain[...] = total
+        GOWN[...] = total
+        width = out_gain.shape[1]
+        each = 128 // width
+        tile = GOWN[:, pl.ds(pl.multiple_of(place // each * 128, 128), 128)]
+        mine = jnp.zeros((2, width), F32)
+        for i in range(each):
+            piece = tile[:, i * width : (i + 1) * width]
+            mine = jnp.where(place % each == i, piece, mine)
+        out_gain[...] = mine
 
     def loop(count, fn):
         def step(i, carry):
@@ -772,6 +862,9 @@
     def w_cols(l, p):
         col, width = pieces[p]
         return W[l, :, col : col + width]
+
+    def w_gate_up(l):
+        return W[l, :, z_.oG : z_.oD]
 
     @scoped
     def state_copy(slot):
@@ -783,8 +876,7 @@
             (s, d, (z + Hn) % nt),
         )
 
-    @scoped
-    def pass_state(slot, value, sender):
+    def state_out(slot, value, sender):
         SEND_STATE[slot] = value.astype(BF)
 
         @pl.when(zh == sender)
@@ -792,6 +884,8 @@
             SIN[slot] = jnp.zeros((DH, C), BF)
             state_copy(slot).start()
 
+    @scoped
+    def state_in(slot, sender):
         @pl.when(zh != sender)
         def _():
             state_copy(slot).wait_recv()
@@ -809,102 +903,104 @@
 
         pl.when((s == l) & cond)(go)
 
+    def hand_near(ps):
+        for l in range(2):
+
+            @pl.when(s == l)
+            def _():
+                for p in ps:
+                    w_hand_near(l, p)
+
+    def x_out():
+        spread_tokens(xin, XF, 0)
+
     gains_out()
+    shard_attention()
     hand_far(0, s == 0, [5])
-    for l in range(2):
-
-        @pl.when(s == l)
-        def _():
-            for p in gathered:
-                w_hand_near(l, p)
-
+    hand_near([5])
+    only((s == 0) & inner, x_out)
+    pump_near([("s", 0, 5)])
     own_tokens(xin, XF, 0)
     own_tokens(cot, GF.at[1], 1)
-
-    def x_out():
-        spread_tokens(xin, XF, 0)
-
-    def x_and_feed():
-        x_out()
-        for p in (2, 3, 4):
-            w_hand_far(0, p)
-
-    only((s == 0) & inner, x_and_feed)
+    shard_feed()
+    hand_far(0, inner, [2, 3, 4])
+    hand_near([2, 3, 4])
     masks()
     for l in range(2):
         DG[l] = jnp.zeros((2, D), F32)
-    pump_near([("s", 0, 5), ("s", 0, 2)])
+    pump_near([("s", 0, 2)])
     gains_in()
     pump_far([("s", 0, 5)])
     only((s == 0) & outer & far, x_out)
     pump([("f", 0, 5)])
     hand_far(0, outer & far, [2, 3, 4])
-    pump_near([("f", 0, 2), ("s", 0, 3)])
+    pump_near([("f", 0, 2)])
     only((s == 0) & outer & near, x_out)
-    pump_near([("f", 0, 3), ("s", 0, 4)])
+    only(s == 1, gains_other)
+    await_tokens(XF, 0, 0)
     hand_far(0, outer & near, [2, 3, 4])
-    only(s == 1, gains_other)
 
     def cot_out():
         spread_tokens(cot, GF.at[1], 1)
 
     stage = {
         (0, "attended"): lambda: (
-            pump_near([("f", 0, 4), ("s", 1, 5)]),
+            pump_near([("f", 0, 3), ("f", 0, 4)]),
             pump_far([("s", 0, 2), ("s", 0, 3), ("f", 0, 2), ("s", 0, 4)]),
         ),
         (0, "hidden"): lambda: (
-            hand_far(1, inner, gathered),
+            hand_far(1, inner, [5, 4, 2, 3]),
             hand_far(1, outer, [5]),
-            pump_near([("f", 1, 5)]),
+            pump_near([("s", 1, 5)]),
             pump_far([("f", 0, 3), ("f", 0, 4)]),
         ),
         (0, "ready"): lambda: (
-            hand_far(1, outer, [2, 3]),
-            pump_near([("s", 1, 2)]),
+            pump_near([("f", 1, 5)]),
+            pump_far([("s", 1, 5)]),
+        ),
+        (0, "feeding"): lambda: (
+            hand_far(1, outer, [4]),
+            pump_near([("s", 1, 4)]),
         ),
         (0, "fed"): lambda: (
-            hand_far(1, outer, [4]),
-            pump_near([("f", 1, 2), ("s", 1, 3)]),
-            pump_far([("s", 1, 5)]),
+            hand_far(1, outer, [2, 3]),
+            pump_near([("s", 1, 2), ("f", 1, 4)]),
+            pump_far([("f", 1, 5), ("s", 1, 4)]),
             only(s == 0, gains_other),
         ),
         (0, "result"): lambda: (
-            pump_near([("f", 1, 3), ("s", 1, 4)]),
-            pump_far([("f", 1, 5), ("s", 1, 2)]),
+            pump_near([("s", 1, 3)]),
+            pump_far([("s", 1, 2), ("f", 1, 4)]),
         ),
         (1, "states"): lambda: (
             only(s == 1, cot_out),
-            pump_near([("f", 1, 4)]),
-            pump_far([("f", 1, 2), ("s", 1, 3)]),
+            pump_near([("f", 1, 2), ("f", 1, 3)]),
+            pump_far([("s", 1, 3), ("f", 1, 2)]),
         ),
-        (1, "attended"): lambda: (pump_far([("f", 1, 3), ("s", 1, 4)]),),
-        (1, "hidden"): lambda: (pump_far([("f", 1, 4)]),),
+        (1, "attended"): lambda: (pump_far([("f", 1, 3)]),),
+        (1, "hidden"): lambda: (),
         (1, "ready"): lambda: (),
         (1, "fed"): lambda: (),
-        (1, "result"): lambda: (),
         "b1 second": lambda: (),
-        "b1 middle": lambda: (),
-        "b1 feed": lambda: (d_mid(1, 4),),
-        "b1 third": lambda: (d_mid(1, 2),),
-        "b1 end": lambda: (d_mid(1, 3),),
-        "b0 second": lambda: (d_mid(1, 0), d_mid(1, 1), d_sum(1, 4)),
-        "b0 middle": lambda: (d_sum(1, 2),),
-        "b0 feed": lambda: (d_sum(1, 3), d_mid(0, 4)),
-        "b0 third": lambda: (d_sum(1, 0), d_sum(1, 1)),
+        "b1 middle": lambda: (d_mid(1, 4),),
+        "b1 feed": lambda: (),
+        "b1 third": lambda: (d_mid(1, 3), d_total_rows(1, 2)),
+        "b1 end": lambda: (d_mid(1, 1), d_mid(1, 0), d_total_rows(1, 3)),
+        "b0 second": lambda: (d_total_rows(1, 0),),
+        "b0 middle": lambda: (),
+        "b0 feed": lambda: (d_total_rows(1, 1), d_mid(0, 4)),
+        "b0 third": lambda: (d_mid(0, 2),),
         "b0 end": lambda: (
             core_gain().start(),
-            d_mid(0, 2),
             d_sum(0, 4),
             gain_second(),
-            d_mid(0, 3),
             d_sum(0, 2),
             d_mid(0, 0),
             d_sum(0, 3),
-            gain_third(),
             d_mid(0, 1),
             d_sum(0, 0),
             d_sum(0, 1),
+            gain_third(),
         ),
     }
 
@@ -912,6 +1008,12 @@
         if l == 0:
             return XF[chunk_rows(m, own), :].astype(F32)
         return Y[0, own_rows(m), :].astype(F32)
+
+    def gate_up_grad(grad, both):
+        parts = [grad * both[:, F : 2 * F], grad * both[:, :F]]
+        if z_.GUw > 2 * F:
+            parts.append(jnp.zeros((MB, z_.GUw - 2 * F), F32))
+        return jnp.concatenate(parts, axis=1).astype(BF)
 
     def finish_layer(l, rs2, ag3):
         def result(m):
@@ -930,7 +1032,8 @@
 
         def qkv_chunk(m):
             if l == 0:
-                await_tokens(XF, 0, m)
+                pl.when(m > 0)(lambda: await_tokens(XF, 0, m))
+                pl.when((m == 1) & near)(lambda: pump([("s", 0, 3), ("s", 0, 4)]))
                 rows = XF[chunk(m), :].astype(F32)
                 N1[0, chunk(m), :] = (rows * rms(rows) * gain(0, 0)).astype(BF)
             else:
@@ -963,7 +1066,15 @@
 
             with jax.named_scope('states'):
                 last = lax.fori_loop(0, MH, states, jnp.zeros((DH, C), F32))
-            pass_state(0, last, 0)
+            for p in gathered:
+                for k in range(2):
+
+                    @pl.when(s == k)
+                    def _():
+                        w_handed_out(k, p)
+
+            state_out(0, last, 0)
+            state_in(0, 0)
             stage[l, "states"]()
 
             def attend(m, passed):
@@ -986,22 +1097,41 @@
 
         loop(MH, hidden_rows)
         stage[l, "hidden"]()
+        w_ready(l, 4)
+        if l == 1:
+
+            def hidden_grad(m):
+                await_tokens(GF.at[1], 1, m)
+                GGU[chunk(m), 0 : z_.Dw] = mm(GF[1, chunk(m), :], w_cols(1, 4)).astype(BF)
+
+            loop(MH, hidden_grad)
         w_ready(l, 2)
         w_ready(l, 3)
-        w_ready(l, 4)
         stage[l, "ready"]()
 
         def feed(m):
             ag_forward(ag2, N2.at[l], m)
             ag_wait(ag2, N2.at[l], m)
             rows = N2[l, chunk(m), :]
-            gate = mm(rows, w_cols(l, 2))
-            up = mm(rows, w_cols(l, 3))
-            GATE[l, chunk(m), :] = gate.astype(BF)
-            UP[l, chunk(m), :] = up.astype(BF)
-            hidden = (gate * up).astype(BF)
+            both = mm(rows, w_gate_up(l))
+            if l == 0:
+                GU[l, chunk(m), :] = both.astype(BF)
+            else:
+                grad = GGU[chunk(m), 0 : z_.Dw].astype(F32)[:, :F]
+                GGU[chunk(m), :] = gate_up_grad(grad, both)
+            hidden = both[:, :F] * both[:, F : 2 * F]
+            if z_.Dw > F:
+                hidden = jnp.concatenate([hidden, jnp.zeros((MB, z_.Dw - F), F32)], axis=1)
+            hidden = hidden.astype(BF)
             HID[l, chunk(m), :] = hidden
             rs_first(rs2, m, mm(hidden, w_cols(l, 4), NT))
+            if l == 0:
+
+
+                @pl.when(m == 1)
+                def _():
+                    stage[0, "feeding"]()
+
             after(rs2, m, m - 1)
 
         loop(MH, feed)
@@ -1018,13 +1148,22 @@
     RB = min(D, 256)
 
     @scoped
-    def grad_weight(l, p, left, right):
+    def grad_weight(l, p, left, right, send=True):
         col, width = pieces[p]
         for r in range(D // RB):
             W[l, r * RB : (r + 1) * RB, col : col + width] = mm(
                 left[:, r * RB : (r + 1) * RB], right, TN
             ).astype(BF)
-        d_send(l, p)
+        if send:
+            d_send(l, p)
+
+    def rest(l, p):
+        for q in range(MH, 4):
+            d_pass(l, p, q)
+
+    def grad_part(l, p):
+        col, width = pieces[p]
+        grad_weight(l, p, N2[l], GGU[:, col - z_.oG : col - z_.oG + width])
 
     def backward(l, ag_in, rs1, ag2, rs2, ag_out):
         for p in gathered:
@@ -1035,22 +1174,22 @@
             if l == 0:
                 ag_forward(ag_in, GF.at[0], m)
                 ag_wait(ag_in, GF.at[0], m)
-            else:
-                await_tokens(GF.at[1], 1, m)
-            grad = mm(GF[l, chunk(m), :], w_cols(l, 4))
-            GGU[chunk(m), 0:FP] = (grad * UP[l, chunk(m), :].astype(F32)).astype(BF)
-            GGU[chunk(m), FP : 2 * FP] = (grad * GATE[l, chunk(m), :].astype(F32)).astype(BF)
-            rs_first(
-                rs1,
-                m,
-                mm(GGU[chunk(m), :], W[l, :, z_.oG : z_.oG + 2 * FP], NT),
-            )
+                grad = mm(GF[l, chunk(m), :], w_cols(l, 4))[:, :F]
+                GGU[chunk(m), :] = gate_up_grad(grad, GU[l, chunk(m), :].astype(F32))
+            rs_first(rs1, m, mm(GGU[chunk(m), :], w_gate_up(l), NT))
             after(rs1, i, m + 1)
-
+            if l == 0:
+                d_pass(1, 3, i)
+
+        if l == 1:
+            grad_weight(l, 4, GF[l], HID[l])
         loop(MH, feed_back)
         rs_second(rs1, 0)
-        grad_weight(l, 4, GF[l], HID[l])
-        if l == 1:
+        if l == 0:
+            rest(1, 3)
+            grad_weight(l, 4, GF[l], HID[l])
+        else:
+            grad_part(l, 2)
             finish_layer(1, 3, None)
         stage[f"b{l} second"]()
 
@@ -1063,11 +1202,16 @@
             GH[own_rows(m), :] = grad
             GA[l, chunk_rows(m, own), :] = grad.astype(BF)
             ag_send(ag2, GA.at[l], m)
+            if l == 0:
+                d_pass(1, 0, i)
 
         loop(MH, middle)
+        if l == 0:
+            rest(1, 0)
         stage[f"b{l} middle"]()
-        grad_weight(l, 2, N2[l], GGU[:, 0:FP])
-        grad_weight(l, 3, N2[l], GGU[:, FP : 2 * FP])
+        if l == 0:
+            grad_part(l, 2)
+        grad_part(l, 3)
         stage[f"b{l} feed"]()
 
         def grad_o(m):
@@ -1087,6 +1231,7 @@
                 for j in range(NB):
                     diag_backward(m * NB + j, grad[j * BLOCK : (j + 1) * BLOCK])
                 qkv_back(i, m)
+                d_pass(1, 1, i)
 
             loop(MH, attend)
         else:
@@ -1100,22 +1245,32 @@
 
             with jax.named_scope("states"):
                 last = lax.fori_loop(0, MH, states, jnp.zeros((DH, C), F32))
-            pass_state(1, last, 1)
+            state_out(1, last, 1)
+            d_mid(1, 2)
+            grad_weight(l, 1, GA[l], O[l])
+            state_in(1, 1)
+            d_total_rows(1, 4)
 
             def attend(i, passed):
                 m = MH - 1 - i
                 for j in reversed(range(NB)):
                     passed = norm_back_second(m * NB + j, passed)
                 qkv_back(i, m)
+                d_pass(1, 4, i)
                 return passed
 
             with jax.named_scope("attend"):
                 lax.fori_loop(0, MH, attend, jnp.ones((1, C), F32))
 
         rs_second(rs2, 0)
+        rest(1, 4 if l == 1 else 1)
         stage[f"b{l} third"]()
-        grad_weight(l, 0, N1[l], GQKV[...])
-        grad_weight(l, 1, GA[l], O[l])
+        grad_weight(l, 0, N1[l], GQKV[...], l == 1)
+        if l == 0:
+            grad_weight(l, 1, GA[l], O[l], False)
+            d_mid(0, 3)
+            d_send(0, 0)
+            d_send(0, 1)
 
         def result(i):
             m = MH - 1 - i
@@ -1126,8 +1281,11 @@
             if l == 1:
                 GF[0, chunk_rows(m, own), :] = low
                 ag_send(ag_out, GF.at[0], m)
+                d_pass(1, 2, i)
 
         loop(MH, result)
+        if l == 1:
+            rest(1, 2)
         stage[f"b{l} end"]()
 
     backward(1, None, 4, 3, 5, 4)
@@ -1136,14 +1294,11 @@
     for p in (4, 2, 3, 0, 1):
         d_final(p)
     gain_final()
+    for copy in outs:
+        copy.wait()
     for l in range(2):
         for p in range(5):
             d_sent(l, p)
-        for p in gathered:
-
-            @pl.when(s == l)
-            def _():
-                w_handed_out(l, p)
 
     ags = ((0, N2.at[0]), (1, N1.at[1]), (2, N2.at[1]), (3, GA.at[1]), (4, GF.at[0]), (5, GA.at[0]))
 
@@ -1180,6 +1335,21 @@
                     ).wait_send()
 
 
+def place_results(*refs):
+    count = (len(refs) - 2) // 3
+    sources, targets, held = refs[:count], refs[count : 2 * count], refs[2 * count : 3 * count]
+    in_sem, out_sem = refs[-2:]
+    reads = [pltpu.make_async_copy(sources[i], held[i], in_sem.at[i]) for i in range(count)]
+    writes = [pltpu.make_async_copy(held[i], targets[i], out_sem.at[i]) for i in range(count)]
+    for copy in reads:
+        copy.start()
+    for read, write in zip(reads, writes):
+        read.wait()
+        write.start()
+    for copy in writes:
+        copy.wait()
+
+
 def solution(mesh):
     nd, nt = mesh.shape["dp"], mesh.shape["tensor"]
 
@@ -1192,12 +1362,11 @@
             qkv_m.shape[3],
             gateup_m.shape[3],
         )
-        D, R, C, F, FP, Dr, M, MH, Hn, MB, T, NBH, N, NH = (
+        D, R, C, F, Dr, M, MH, Hn, MB, T, NBH, N, NH = (
             z_.D,
             z_.R,
             z_.C,
             z_.F,
-            z_.FP,
             z_.Dr,
             z_.M,
             z_.MH,
@@ -1208,35 +1377,18 @@
             z_.N,
             z_.NH,
         )
-        pad = ((0, 0), (0, FP - F))
-        shard = jnp.concatenate(
-            [
-                qkv_m[0].reshape(Dr, 3 * C).astype(BF),
-                out_m[0].T.astype(BF),
-                jnp.pad(gateup_m[0, :, 0].astype(BF), pad),
-                jnp.pad(gateup_m[0, :, 1].astype(BF), pad),
-                jnp.pad(down_m[0].T.astype(BF), pad),
-            ],
-            axis=1,
-        )
-        half = lax.axis_index("tensor") // Hn
-        marks = (
-            lax.dynamic_slice_in_dim(starts[0], half * MH, MH, 0)
-            .reshape(NBH, BLOCK)
-            .astype(F32)
-        )
         width = gain_m.shape[2]
-        place = lax.axis_index("dp") * nt + lax.axis_index("tensor")
-        low = gain_m[0].astype(BF).astype(F32)
-        each = 128 // width
-        gain_in = jnp.where(
-            jnp.arange(128)[None] // width == place % each, jnp.tile(low, (1, each)), 0.0
-        )
+        qkv_rows = jnp.transpose(qkv_m[0], (1, 0, 2))
+        gateup_rows = jnp.transpose(gateup_m[0], (1, 2, 0)).reshape(2 * F, Dr)
         anywhere = pl.BlockSpec(memory_space=pl.ANY)
         vmem = pl.BlockSpec(memory_space=pltpu.VMEM)
         DMA = pltpu.SemaphoreType.DMA
         V = pltpu.VMEM
         scratch = [
+            V((3, Dr, C), F32),
+            V((C, Dr), F32),
+            V((2 * F, Dr), F32),
+            V((F, Dr), F32),
             V((2, D, N), BF),
             V((2, nd - 1, Dr, N), BF),
             V((2, Dr, N), BF),
@@ -1246,13 +1398,12 @@
             V((2, T, D), BF),
             V((2, T, 3 * C), BF),
             V((2, T, C), BF),
-            V((2, T, FP), BF),
-            V((2, T, FP), BF),
-            V((2, T, FP), BF),
+            V((1, T, z_.GUw), BF),
+            V((2, T, z_.Dw), BF),
             V((2, MH * R, D), F32),
             V((2, MH * R, D), BF),
             V((2, T, D), BF),
-            V((T, 2 * FP), BF),
+            V((T, z_.GUw), BF),
             V((T, 3 * C), BF),
             V((MH * R, D), F32),
             V((2, MH * R, D), BF),
@@ -1298,40 +1449,58 @@
             DMA((2, 2, MH)),
             DMA((2, 5, max(6, nd - 1))),
             DMA((2, 5, max(6, nd - 1))),
-            DMA((2, 5)),
-            DMA((5, 2)),
+            DMA((2, 5, 4)),
+            DMA((5, 2, 4)),
             DMA((6, max(nd, nt) - 1)),
             DMA((6, max(nd, nt) - 1)),
             DMA((nd * nt,)),
             DMA((nd * nt,)),
+            DMA((4,)),
         ]
-        out_y, out_g, out_w, out_gain = pl.pallas_call(
+        out_y, out_g, grad_qkv, grad_o, grad_gu, grad_d, grad_gain = pl.pallas_call(
             functools.partial(body, z_),
             out_shape=(
                 jax.ShapeDtypeStruct((M, R, D), BF),
                 jax.ShapeDtypeStruct((M, R, D), BF),
-                jax.ShapeDtypeStruct((Dr, N), F32),
-                jax.ShapeDtypeStruct((2, D), F32),
+                jax.ShapeDtypeStruct((3, Dr, C), F32),
+                jax.ShapeDtypeStruct((C, Dr), F32),
+                jax.ShapeDtypeStruct((2 * F, Dr), F32),
+                jax.ShapeDtypeStruct((F, Dr), F32),
+                jax.ShapeDtypeStruct((2, width), F32),
             ),
-            in_specs=[anywhere, anywhere, anywhere, vmem, vmem],
-            out_specs=(anywhere, anywhere, vmem, vmem),
+            in_specs=[anywhere] * 6 + [vmem, vmem],
+            out_specs=(anywhere,) * 6 + (vmem,),
             scratch_shapes=scratch,
             compiler_params=pltpu.CompilerParams(
                 collective_id=0, has_side_effects=True, vmem_limit_bytes=63 * 1024 * 1024
             ),
-        )(shard, inputs[0], cotangent[0], marks, gain_in)
-        gateup = jnp.stack(
-            [out_w[:, z_.oG : z_.oG + F], out_w[:, z_.oU : z_.oU + F]], axis=1
+        )(
+            qkv_rows,
+            out_m[0],
+            gateup_rows,
+            down_m[0],
+            inputs[0],
+            cotangent[0],
+            jnp.transpose(starts, (1, 0, 2)),
+            gain_m[0],
         )
-        gain_share = lax.dynamic_slice_in_dim(out_gain, place * width, width, 1)
+        results = (out_y, out_g, grad_qkv, grad_o, grad_gu, grad_d, grad_gain)
+        out_y, out_g, grad_qkv, grad_o, grad_gu, grad_d, grad_gain = pl.pallas_call(
+            place_results,
+            out_shape=tuple(jax.ShapeDtypeStruct(r.shape, r.dtype) for r in results),
+            in_specs=[anywhere] * len(results),
+            out_specs=(anywhere,) * len(results),
+            scratch_shapes=[V(r.shape, r.dtype) for r in results]
+            + [DMA((len(results),)), DMA((len(results),))],
+        )(*results)
         return (
             out_y[None, None],
             out_g[None, None],
-            out_w[:, : 3 * C].reshape(1, Dr, 3, C),
-            out_w[:, z_.oO : z_.oO + C].T[None],
-            gateup[None],
-            out_w[:, z_.oD : z_.oD + F].T[None],
-            gain_share[None],
+            jnp.transpose(grad_qkv, (1, 0, 2))[None],
+            grad_o[None],
+            jnp.transpose(grad_gu.reshape(2, F, Dr), (2, 0, 1))[None],
+            grad_d[None],
+            grad_gain[None],
         )
 
     return jax.shard_map(

time: 328 us -> 295 us (0.90)
  local copies, waits for them, and re-layouts: 19.7 us -> 0 us
  Pallas kernels: 305 us -> 294 us
    pallas_call x1, Pallas kernels: 305 us -> 290 us  [on_device(): pl.pallas_call(functools.partial(body, z_), out_shape=(jax.ShapeDtypeStru...]
    unnamed x22 -> x0, local copies, waits for them, and re-layouts: 12.3 us -> none
    broadcast_in_dim x3 -> x0, local copies, waits for them, and re-layouts: 4.05 us -> none  [the longest x1 1.77 us: on_device(): out_w[:, z_.oD:z_.oD + F].T[None]]
    pallas_call x0 -> x1, Pallas kernels: none -> 3.79 us  [on_device(): pl.pallas_call(place_results, out_shape=tuple((jax.ShapeDtypeStruct(r.sha...]
where the time goes in v4:
time: 295 us
  Pallas kernels  294 us (100%)
    pallas_call x1, Pallas kernels, on_device(): pl.pallas_call(functools.partial(body, z_), out_shape=(jax.ShapeDtypeStru...  290 us

profile of v4, /device:TPU:0, one launch (start us, length us, event | category | flops | bytes accessed | tf_op | source)
XLA Modules:
  0.0 294.6 jit_solution(6858119756671880574)
XLA Ops:
  0.6 290.0 %shard_map.135 = (bf16[6,48,1024]{2,1,0:T(8,128)(2,1)}, bf16[6,48,1024]{2,1,0:T(8,128)(2,1)}, f32[3,256,256]{2,1,0:T(8,128)}, f32[256,256]{1,0:T(8,128)}, f32[14...) custom-call(f32[3,256,256]{2,1,0:T(8,128)} %bitcast.28, f32[256,256]{1,0:T(8,128)} %bitcast.32, ...), custom_call_target="tpu_custom_call" | custom-call | tf_op jit(solution)/shard_map/pallas_call | solution.py:1460
  290.6 3.8 %shard_map.136 = (bf16[6,48,1024]{2,1,0:T(8,128)(2,1)}, bf16[6,48,1024]{2,1,0:T(8,128)(2,1)}, f32[3,256,256]{2,1,0:T(8,128)}, f32[256,256]{1,0:T(8,128)}, f32[14...) custom-call(bf16[6,48,1024]{2,1,0:T(8,128)(2,1)} %get-tuple-element.21.refs_0_, ...), custom_call_target="tpu_custom_call" | custom-call | tf_op jit(solution)/shard_map/pallas_call | solution.py:1488

commit v5 on v4

--- a/solution.py
+++ b/solution.py
@@ -59,6 +59,9 @@
             (self.oG + first, self.GUw - first),
             (self.oD, self.Dw),
             (0, 4 * cols),
+            (0, cols),
+            (cols, cols),
+            (2 * cols, cols),
         )
 
 
@@ -123,15 +126,13 @@
     DL1,
     DL2,
     in_sem,
-    x_ss,
+    x_sem,
     x_rs,
-    x_fs,
     w1_ss,
     w1_rs,
     w2_ss,
     w2_rs,
     ag_ss,
-    ag_fs,
     ag_rs,
     r1_ss,
     r1_rs,
@@ -145,10 +146,10 @@
     d1_rs,
     d2_ss,
     d2_rs,
+    g1_sem,
     g_ss,
     g_rs,
-    gl_ss,
-    gl_rs,
+    gl_sem,
     m_sem,
 ):
     D, R, C, F, Dr, MH, Hn, MB, T, NH, NB, NBH = (
@@ -226,7 +227,7 @@
                 remote(
                     src.at[(other // Hn) * MH + m],
                     mine,
-                    x_ss.at[m, step - 1],
+                    x_sem.at[0],
                     x_rs.at[array, m, step - 1],
                     z_dev(step),
                 ).start()
@@ -240,8 +241,10 @@
             @pl.when(s == array)
             def _():
                 remote(
-                    rows, rows, x_fs.at[m, step - 1], x_rs.at[array, m, step - 1], core_dev
+                    rows, rows, x_sem.at[1], x_rs.at[array, m, step - 1], core_dev
                 ).start()
+
+    spot = {5: 0, 2: 1, 3: 2, 4: 3}
 
     def w_rows(l, block, p):
         col, width = pieces[p]
@@ -254,7 +257,7 @@
     def w_hand_near(l, p):
         @pl.when(zh == s)
         def _():
-            pltpu.make_async_copy(shard_cols(p), w_rows(l, d, p), w1_rs.at[l, p]).start()
+            pltpu.make_async_copy(shard_cols(p), w_rows(l, d, p), w1_rs.at[l, spot[p]]).start()
 
         @pl.when(zh != s)
         def _():
@@ -262,18 +265,18 @@
 
     def w_hand(l, p, which, dev):
         return remote(
-            shard_cols(p), w_rows(l, d, p), w1_ss.at[p, which], w1_rs.at[l, p], dev
+            shard_cols(p), w_rows(l, d, p), w1_ss.at[which], w1_rs.at[l, spot[p]], dev
         )
 
     def w_hand_far(l, p):
         w_hand(l, p, 1, (zh, d, (z + Hn) % nt)).start()
 
-    def w_handed_out(l, p):
+    def w_handed_out():
         @pl.when(zh != s)
         def _():
-            w_hand(l, p, 0, core_dev).wait_send()
-
-        w_hand(l, p, 1, core_dev).wait_send()
+            got(L2.at[0], w1_ss.at[0])
+
+        got(L2.at[0], w1_ss.at[1])
 
     square = nd == 4
     half_rows = Dr // 2
@@ -292,31 +295,30 @@
             rows, dev = w_half(l, dp_x, 0, p), (s, dp_y, z)
         else:
             rows, dev = w_half(l, dp_y, 1, p), (s, dp_x, z)
-        return remote(rows, rows, w2_ss.at[l, p, k], w2_rs.at[l, p, k], dev)
+        return remote(rows, rows, w2_ss.at[l], w2_rs.at[l, spot[p], k], dev)
 
     def w_share(l, p):
-        got(w_rows(l, d, p), w1_rs.at[l, p])
+        got(w_rows(l, d, p), w1_rs.at[l, spot[p]])
         for k in range(2 if square else nd - 1):
             w_copy(l, p, k).start()
 
     def w_forward(l, p):
         if square:
-            got(w_rows(l, dp_x, p), w2_rs.at[l, p, 0])
+            got(w_rows(l, dp_x, p), w2_rs.at[l, spot[p], 0])
             w_copy(l, p, 2).start()
-            got(w_rows(l, dp_y, p), w2_rs.at[l, p, 1])
+            got(w_rows(l, dp_y, p), w2_rs.at[l, spot[p], 1])
             w_copy(l, p, 3).start()
 
     def w_ready(l, p):
         if square:
-            got(w_half(l, 3 - d, 0, p), w2_rs.at[l, p, 2])
-            got(w_half(l, 3 - d, 1, p), w2_rs.at[l, p, 3])
+            got(w_half(l, 3 - d, 0, p), w2_rs.at[l, spot[p], 2])
+            got(w_half(l, 3 - d, 1, p), w2_rs.at[l, spot[p], 3])
         else:
             for step in range(1, nd):
-                got(w_rows(l, (d + nd - step) % nd, p), w2_rs.at[l, p, step - 1])
-
-    def w_shared(l, p):
-        for k in range(4 if square else nd - 1):
-            w_copy(l, p, k).wait_send()
+                got(w_rows(l, (d + nd - step) % nd, p), w2_rs.at[l, spot[p], step - 1])
+
+    def w_shared(l):
+        got(W.at[l, pl.ds(0, (nd - 1) * Dr)], w2_ss.at[l])
 
     def pump(ops):
         for what, l, p in ops:
@@ -331,6 +333,11 @@
 
     def pump_far(ops):
         pl.when(jnp.logical_not(near))(lambda: pump(ops))
+
+    where = {4: 0, 2: 1, 3: 2, 1: 3, 6: 4, 7: 5, 8: 6}
+
+    def split(p):
+        return (6, 7, 8) if p == 0 else (p,)
 
     def d_copy(l, p, k):
         col, width = pieces[p]
@@ -348,15 +355,20 @@
                 (dp_x, 1, 0, second, dp_x),
             )[k]
             src, dst, dev = w_half(l, block, half, p), LW.at[l, slot, rows, cols], (s, to, z)
-        return remote(src, dst, d1_ss.at[l, p, k], d1_rs.at[l, p, k], dev)
+        group = k if square and k < 2 else 2
+        return remote(src, dst, d1_ss.at[l], d1_rs.at[l, where[p], group], dev)
 
     def d_send(l, p):
-        for k in range(4 if square else nd - 1):
-            d_copy(l, p, k).start()
+        for part in split(p):
+            for k in range(4 if square else nd - 1):
+                d_copy(l, part, k).start()
 
     @scoped
     def d_mid(l, p):
-        if square:
+        if p == 0:
+            for part in split(p):
+                d_mid(l, part)
+        elif square:
             col, width = pieces[p]
             cols = pl.ds(col, width)
             for k, block, half in ((0, dp_y, 0), (1, dp_x, 1)):
@@ -369,54 +381,46 @@
 
     part_rows = Dr // 4
 
-    def d_hop(l, p, q):
-        col, width = pieces[p]
-        cols = pl.ds(col, width)
-        return (
-            W.at[l, pl.ds(d * Dr + q * part_rows, part_rows), cols],
-            L2.at[zh, pl.ds(q * part_rows, part_rows), cols],
-            d2_ss.at[l, p, q],
-            d2_rs.at[p, zh, q],
-        )
-
-    def d_pass(l, p, q):
-        src, dst, ssem, rsem = d_hop(l, p, q)
-        to_self = (s == l) & (zh == s)
-
-        @pl.when(to_self)
-        def _():
-            pltpu.make_async_copy(src, dst, rsem).start()
-
-        @pl.when(jnp.logical_not(to_self))
-        def _():
-            remote(src, dst, ssem, rsem, (l, d, s * Hn + zl)).start()
+    def d_pass(l, p, q, rows=part_rows):
+        for part in split(p):
+            col, width = pieces[part]
+            cols = pl.ds(col, width)
+            src = W.at[l, pl.ds(d * Dr + q * rows, rows), cols]
+            dst = L2.at[zh, pl.ds(q * rows, rows), cols]
+            arrival = d2_rs.at[where[part], zh]
+            to_self = (s == l) & (zh == s)
+
+            @pl.when(to_self)
+            def _():
+                pltpu.make_async_copy(src, dst, arrival).start()
+
+            @pl.when(jnp.logical_not(to_self))
+            def _():
+                remote(src, dst, d2_ss.at[l], arrival, (l, d, s * Hn + zl)).start()
 
     @scoped
     def d_total_rows(l, p):
-        col, width = pieces[p]
-        for k in (2, 3, 4, 5) if square else range(nd - 1):
-            d_copy(l, p, k).wait_recv()
-        rows = pl.ds(d * Dr, Dr)
-        cols = pl.ds(col, width)
-        total = W[l, rows, cols].astype(F32)
-        for slot in range(2 if square else nd - 1):
-            total = total + LW[l, slot, :, cols].astype(F32)
-        W[l, rows, cols] = total.astype(BF)
+        for part in split(p):
+            col, width = pieces[part]
+            cols = pl.ds(col, width)
+            slots = 2 if square else nd - 1
+            got(LW.at[l, pl.ds(0, slots), :, cols], d1_rs.at[l, where[part], 2])
+            rows = pl.ds(d * Dr, Dr)
+            total = W[l, rows, cols].astype(F32)
+            for slot in range(slots):
+                total = total + LW[l, slot, :, cols].astype(F32)
+            W[l, rows, cols] = total.astype(BF)
 
     def d_sum(l, p):
         d_total_rows(l, p)
-        for q in range(4):
-            d_pass(l, p, q)
-
-    def d_sent(l, p):
-        for k in range(6 if square else nd - 1):
-            d_copy(l, p, k).wait_send()
-        to_self = (s == l) & (zh == s)
-
-        @pl.when(jnp.logical_not(to_self))
+        d_pass(l, p, 0, Dr)
+
+    def d_sent(l):
+        got(W.at[l, pl.ds(0, (nd - 1) * Dr)], d1_ss.at[l])
+
+        @pl.when(jnp.logical_not((s == l) & (zh == s)))
         def _():
-            for q in range(4):
-                remote(*d_hop(l, p, q), core_dev).wait_send()
+            got(W.at[l, pl.ds(0, Dr)], d2_ss.at[l])
 
     outs = (
         pltpu.make_async_copy(MQ, out_qkv, m_sem.at[0]),
@@ -428,9 +432,7 @@
     def d_arrived(p):
         col, width = pieces[p]
         for half in range(2):
-            for q in range(4):
-                rows = pl.ds(q * part_rows, part_rows)
-                got(L2.at[half, rows, pl.ds(col, width)], d2_rs.at[p, half, q])
+            got(L2.at[half, :, pl.ds(col, width)], d2_rs.at[where[p], half])
 
     def d_total(col, width):
         return L2[0, :, col : col + width].astype(F32) + L2[1, :, col : col + width].astype(F32)
@@ -438,10 +440,10 @@
     @scoped
     def d_final(p):
         d_arrived(p)
-        if p == 0:
-            for j in range(3):
-                MQ[j] = d_total(j * C, C)
-            outs[0].start()
+        if p >= 6:
+            j = p - 6
+            MQ[j] = d_total(j * C, C)
+            pltpu.make_async_copy(MQ.at[j], out_qkv.at[j], m_sem.at[0]).start()
         elif p == 1:
             MO[...] = d_total(z_.oO, C).T
             outs[1].start()
@@ -452,6 +454,7 @@
             MD[...] = d_total(z_.oD, z_.Dw).T[:F]
             outs[3].start()
 
+    @scoped
     def shard_attention():
         masters[0].wait()
         masters[1].wait()
@@ -459,6 +462,7 @@
             L2[0, :, j * C : (j + 1) * C] = MQ[j].astype(BF)
         L2[0, :, z_.oO : z_.oG] = MO[...].T.astype(BF)
 
+    @scoped
     def shard_feed():
         masters[2].wait()
         masters[3].wait()
@@ -474,42 +478,29 @@
     def ag_send(k, buf, m):
         rows = buf.at[chunk_rows(m, own)]
         for step in range(1, Hn):
-            remote(
-                rows,
-                rows,
-                ag_ss.at[k, m, step],
-                ag_rs.at[k, m, own],
-                (s, d, zh * Hn + peer_zl(step)),
-            ).start()
-        remote(rows, rows, ag_ss.at[k, m, 0], ag_rs.at[k, m, own], core_dev).start()
+            dev = (s, d, zh * Hn + peer_zl(step))
+            remote(rows, rows, ag_ss.at[k], ag_rs.at[k, m, Hn - step], dev).start()
+        remote(rows, rows, ag_ss.at[k], ag_rs.at[k, m, 0], core_dev).start()
 
     def ag_forward(k, buf, m):
         for step in range(1, Hn):
-            c = s * Hn + peer_zl(step)
-            rows = buf.at[chunk_rows(m, c)]
-            got(rows, ag_rs.at[k, m, c])
-            remote(rows, rows, ag_fs.at[k, m, step - 1], ag_rs.at[k, m, c], core_dev).start()
+            rows = buf.at[chunk_rows(m, s * Hn + peer_zl(step))]
+            got(rows, ag_rs.at[k, m, step])
+            remote(rows, rows, ag_ss.at[k], ag_rs.at[k, m, 0], core_dev).start()
 
     def ag_wait(k, buf, m):
-        for step in range(Hn):
-            c = (1 - s) * Hn + step
-            got(buf.at[chunk_rows(m, c)], ag_rs.at[k, m, c])
-
-    def ag_sent(k, buf, m):
-        rows = buf.at[chunk_rows(m, own)]
-        for step in range(Hn):
-            remote(rows, rows, ag_ss.at[k, m, step], ag_rs.at[k, m, own], core_dev).wait_send()
-        for step in range(1, Hn):
-            rows = buf.at[chunk_rows(m, s * Hn + peer_zl(step))]
-            remote(rows, rows, ag_fs.at[k, m, step - 1], ag_rs.at[k, m, own], core_dev).wait_send()
+        got(buf.at[pl.ds(m * MB + (1 - s) * Hn * R, Hn * R)], ag_rs.at[k, m, 0])
+
+    def ag_sent(k, buf):
+        got(buf.at[pl.ds(0, MH * (2 * Hn - 1) * R)], ag_ss.at[k])
 
     def rs_copy1(k, m):
         par = k % 2
         return remote(
             PT.at[par, pl.ds(m * MB + (1 - s) * Hn * R, Hn * R)],
             RL1.at[par, m],
-            r1_ss.at[k, m],
-            r1_rs.at[k, m],
+            r1_ss.at[par, m],
+            r1_rs.at[par, m],
             core_dev,
         )
 
@@ -518,8 +509,8 @@
         return remote(
             RSB.at[par, m, step - 1],
             RL2.at[par, m, step - 1],
-            r2_ss.at[k, m, step - 1],
-            r2_rs.at[k, m, step - 1],
+            r2_ss.at[par, m, step - 1],
+            r2_rs.at[par, m, step - 1],
             (s, d, zh * Hn + peer_zl(step)),
         )
 
@@ -582,26 +573,13 @@
 
         @pl.when(to_self)
         def _():
-            pltpu.make_async_copy(src, dst, o_rs.at[which, zh, m]).start()
+            pltpu.make_async_copy(src, dst, o_rs.at[which, zh]).start()
 
         @pl.when(jnp.logical_not(to_self))
         def _():
             remote(
-                src, dst, o_ss.at[which, l, m], o_rs.at[which, zh, m], (l, d, s * Hn + zl)
+                src, dst, o_ss.at[l], o_rs.at[which, zh], (l, d, s * Hn + zl)
             ).start()
-
-    def sent_out(buf, l, out, which, m):
-        to_self = (s == l) & (zh == s)
-
-        @pl.when(jnp.logical_not(to_self))
-        def _():
-            remote(
-                buf.at[l, own_rows(m)],
-                out.at[zh * MH + m],
-                o_ss.at[which, l, m],
-                o_rs.at[which, zh, m],
-                core_dev,
-            ).wait_send()
 
     lane_head = lax.broadcasted_iota(jnp.int32, (1, C), 1) // DH
     head_bf = [(lane_head == h).astype(F32).astype(BF) for h in range(NH)]
@@ -713,24 +691,30 @@
     def ST2_store(b, state):
         ST[NBH + b] = state
 
-    def norm_back_second(b, passed):
+    def sigmoid(values):
+        return 1.0 / (1.0 + jnp.exp(-values.astype(F32)))
+
+    def norm_back_local(b):
         rows = block_rows(b)
         q, k, v = qkv_block(1, b)
         query, key = features(q), features(k)
         low = DU[rows, :]
         stacked = stack(low)
-        grad_state = ST[NBH + b] + passed * SIN[1].astype(F32)
-        grad_wide = unfold(grad_state)
         grad_a = jnp.where(tall(MSK[b]) > 0.5, mm(stacked, v, NT), 0.0).astype(BF)
-        tail, carry = wide_lanes(TAIL[b]), wide_lanes(CAR[b])
-        grad_q = unstack(mm(grad_a, key)) + carry * mm(low, unfold(ST[b]), NT)
-        grad_k = mm(grad_a, stack(query), TN) + tail * mm(v, grad_wide, NT)
-        grad_v = mm(AP[1, b], stacked, TN) + tail * mm(key, grad_wide)
-        sig_q = 1.0 / (1.0 + jnp.exp(-q.astype(F32)))
-        sig_k = 1.0 / (1.0 + jnp.exp(-k.astype(F32)))
-        GQKV[rows, 0:C] = (grad_q * sig_q).astype(BF)
-        GQKV[rows, C : 2 * C] = (grad_k * sig_k).astype(BF)
-        GQKV[rows, 2 * C : 3 * C] = grad_v.astype(BF)
+        grad_q = unstack(mm(grad_a, key)) + wide_lanes(CAR[b]) * mm(low, unfold(ST[b]), NT)
+        GQKV[rows, 0:C] = (grad_q * sigmoid(q)).astype(BF)
+        GQKV[rows, C : 2 * C] = (mm(grad_a, stack(query), TN) * sigmoid(k)).astype(BF)
+        GQKV[rows, 2 * C : 3 * C] = mm(AP[1, b], stacked, TN).astype(BF)
+
+    def norm_back_state(b, passed):
+        rows = block_rows(b)
+        q, k, v = qkv_block(1, b)
+        grad_wide = unfold(ST[NBH + b] + passed * SIN[1].astype(F32))
+        tail = wide_lanes(TAIL[b])
+        grad_k = tail * mm(v, grad_wide, NT) * sigmoid(k)
+        grad_v = tail * mm(features(k), grad_wide)
+        GQKV[rows, C : 2 * C] = (GQKV[rows, C : 2 * C].astype(F32) + grad_k).astype(BF)
+        GQKV[rows, 2 * C : 3 * C] = (GQKV[rows, 2 * C : 3 * C].astype(F32) + grad_v).astype(BF)
         return passed * wide_lanes(KEEP[b, 0:1, :])
 
     @scoped
@@ -763,8 +747,9 @@
     place = d * nt + z
 
     def gain_copy(i):
-        return remote(GL.at[place], GL.at[place], gl_ss.at[i], gl_rs.at[i], section_dev(i))
-
+        return remote(GL.at[place], GL.at[place], gl_sem.at[0], gl_sem.at[1], section_dev(i))
+
+    @scoped
     def gains_out():
         width = gain_in.shape[1]
         row = lax.broadcasted_iota(jnp.int32, (width, 128), 0)
@@ -780,13 +765,8 @@
 
     @scoped
     def gains_in():
-        def one(i, carry):
-            gain_copy(i).wait_send()
-            source = (d + nd - i // nt) % nd * nt + (z + nt - i % nt) % nt
-            got(GL.at[source], gl_rs.at[i])
-            return carry
-
-        lax.fori_loop(1, nd * nt, one, 0)
+        for k in (1, 0):
+            got(GL.at[pl.ds(0, nd * nt - 1)], gl_sem.at[k])
         each = nd * nt * 128 // D
         for t in range(D // 128):
             total = GL[t * each]
@@ -796,23 +776,23 @@
         gain_swap().start()
 
     def gain_swap():
-        return remote(GV.at[s], GV.at[s], g_ss.at[2, 0], g_rs.at[2, 0], core_dev)
+        return remote(GV.at[s], GV.at[s], g1_sem.at[0], g1_sem.at[1], core_dev)
 
     def gains_other():
         gain_swap().wait_send()
-        got(GV.at[1 - s], g_rs.at[2, 0])
+        got(GV.at[1 - s], g1_sem.at[1])
 
     def dp_gain(step):
         return remote(
-            GOWN, DL2.at[step - 1], g_ss.at[5, step - 1], g_rs.at[5, step - 1], dp_dev(step)
+            GOWN, DL2.at[step - 1], g_ss.at[1, step - 1], g_rs.at[1, step - 1], dp_dev(step)
         )
 
     def core_gain():
-        return remote(DG.at[1 - s], DL0, g_ss.at[3, 0], g_rs.at[3, 0], core_dev)
+        return remote(DG.at[1 - s], DL0, g1_sem.at[2], g1_sem.at[3], core_dev)
 
     def z_gain(step):
         return remote(
-            DG.at[s], DL1.at[step - 1], g_ss.at[4, step - 1], g_rs.at[4, step - 1], z_dev(step)
+            DG.at[s], DL1.at[step - 1], g_ss.at[0, step - 1], g_rs.at[0, step - 1], z_dev(step)
         )
 
     @scoped
@@ -969,11 +949,11 @@
             only(s == 0, gains_other),
         ),
         (0, "result"): lambda: (
+            only(s == 1, cot_out),
             pump_near([("s", 1, 3)]),
             pump_far([("s", 1, 2), ("f", 1, 4)]),
         ),
         (1, "states"): lambda: (
-            only(s == 1, cot_out),
             pump_near([("f", 1, 2), ("f", 1, 3)]),
             pump_far([("s", 1, 3), ("f", 1, 2)]),
         ),
@@ -985,24 +965,41 @@
         "b1 middle": lambda: (d_mid(1, 4),),
         "b1 feed": lambda: (),
         "b1 third": lambda: (d_mid(1, 3), d_total_rows(1, 2)),
-        "b1 end": lambda: (d_mid(1, 1), d_mid(1, 0), d_total_rows(1, 3)),
+        "b1 end": lambda: (d_total_rows(1, 3),),
         "b0 second": lambda: (d_total_rows(1, 0),),
         "b0 middle": lambda: (),
-        "b0 feed": lambda: (d_total_rows(1, 1), d_mid(0, 4)),
-        "b0 third": lambda: (d_mid(0, 2),),
+        "b0 feed": lambda: (d_total_rows(1, 1),),
+        "b0 third": lambda: (
+            only(far, lambda: run(d_mid, 2)),
+            only(near, lambda: run(d_mid, 4) or run(d_send, 2, 3)),
+        ),
         "b0 end": lambda: (
             core_gain().start(),
-            d_sum(0, 4),
+            only(near, lambda: run(d_send, 0, 1)),
             gain_second(),
-            d_sum(0, 2),
-            d_mid(0, 0),
-            d_sum(0, 3),
-            d_mid(0, 1),
-            d_sum(0, 0),
-            d_sum(0, 1),
+            only(far, lambda: far_tail()),
+            only(near, lambda: near_tail()),
             gain_third(),
         ),
     }
+
+    def run(step, *parts):
+        for p in parts:
+            step(0, p)
+
+    def far_tail():
+        run(d_sum, 2)
+        run(d_mid, 6)
+        run(d_sum, 3)
+        run(d_mid, 7, 8)
+        run(d_sum, 6)
+        run(d_mid, 1)
+        run(d_sum, 7, 8, 1)
+
+    def near_tail():
+        run(d_sum, 4)
+        run(d_mid, 2, 3, 6, 7, 8, 1)
+        run(d_sum, 2, 3, 6, 7, 8, 1)
 
     def input_rows(l, m):
         if l == 0:
@@ -1066,13 +1063,7 @@
 
             with jax.named_scope('states'):
                 last = lax.fori_loop(0, MH, states, jnp.zeros((DH, C), F32))
-            for p in gathered:
-                for k in range(2):
-
-                    @pl.when(s == k)
-                    def _():
-                        w_handed_out(k, p)
-
+            w_handed_out()
             state_out(0, last, 0)
             state_in(0, 0)
             stage[l, "states"]()
@@ -1161,13 +1152,12 @@
         for q in range(MH, 4):
             d_pass(l, p, q)
 
-    def grad_part(l, p):
+    def grad_part(l, p, send=True):
         col, width = pieces[p]
-        grad_weight(l, p, N2[l], GGU[:, col - z_.oG : col - z_.oG + width])
+        grad_weight(l, p, N2[l], GGU[:, col - z_.oG : col - z_.oG + width], send)
 
     def backward(l, ag_in, rs1, ag2, rs2, ag_out):
-        for p in gathered:
-            w_shared(l, p)
+        w_shared(l)
 
         def feed_back(i):
             m = MH - 1 - i
@@ -1179,15 +1169,21 @@
             rs_first(rs1, m, mm(GGU[chunk(m), :], w_gate_up(l), NT))
             after(rs1, i, m + 1)
             if l == 0:
+
+                @pl.when(i == 0)
+                def _():
+                    d_mid(1, 1)
+                    d_mid(1, 0)
+
                 d_pass(1, 3, i)
-
         if l == 1:
             grad_weight(l, 4, GF[l], HID[l])
         loop(MH, feed_back)
         rs_second(rs1, 0)
         if l == 0:
             rest(1, 3)
-            grad_weight(l, 4, GF[l], HID[l])
+            grad_weight(l, 4, GF[l], HID[l], False)
+            only(far, lambda: d_send(0, 4))
         else:
             grad_part(l, 2)
             finish_layer(1, 3, None)
@@ -1203,6 +1199,7 @@
             GA[l, chunk_rows(m, own), :] = grad.astype(BF)
             ag_send(ag2, GA.at[l], m)
             if l == 0:
+                only((i == 1) & near, lambda: d_send(0, 4))
                 d_pass(1, 0, i)
 
         loop(MH, middle)
@@ -1210,8 +1207,17 @@
             rest(1, 0)
         stage[f"b{l} middle"]()
         if l == 0:
-            grad_part(l, 2)
-        grad_part(l, 3)
+            grad_part(l, 2, False)
+
+            @pl.when(far)
+            def _():
+                d_mid(0, 4)
+                d_send(0, 2)
+
+            grad_part(l, 3, False)
+            only(far, lambda: d_send(0, 3))
+        else:
+            grad_part(l, 3)
         stage[f"b{l} feed"]()
 
         def grad_o(m):
@@ -1232,6 +1238,7 @@
                     diag_backward(m * NB + j, grad[j * BLOCK : (j + 1) * BLOCK])
                 qkv_back(i, m)
                 d_pass(1, 1, i)
+                only((i == 0) & far, lambda: d_sum(0, 4))
 
             loop(MH, attend)
         else:
@@ -1248,29 +1255,47 @@
             state_out(1, last, 1)
             d_mid(1, 2)
             grad_weight(l, 1, GA[l], O[l])
+            d_total_rows(1, 4)
+
+            def attend_local(m):
+                for j in range(NB):
+                    norm_back_local(m * NB + j)
+
+            loop(MH, attend_local)
             state_in(1, 1)
-            d_total_rows(1, 4)
+            pl.when(zh == 0)(lambda: d_pass(1, 4, 0, Dr))
 
             def attend(i, passed):
                 m = MH - 1 - i
                 for j in reversed(range(NB)):
-                    passed = norm_back_second(m * NB + j, passed)
+                    passed = norm_back_state(m * NB + j, passed)
                 qkv_back(i, m)
-                d_pass(1, 4, i)
+
+                @pl.when(zh == 1)
+                def _():
+                    d_pass(1, 4, i)
+
                 return passed
 
             with jax.named_scope("attend"):
                 lax.fori_loop(0, MH, attend, jnp.ones((1, C), F32))
 
         rs_second(rs2, 0)
-        rest(1, 4 if l == 1 else 1)
+        if l == 0:
+            rest(1, 1)
+        else:
+            pl.when(zh == 1)(lambda: rest(1, 4))
         stage[f"b{l} third"]()
         grad_weight(l, 0, N1[l], GQKV[...], l == 1)
         if l == 0:
             grad_weight(l, 1, GA[l], O[l], False)
-            d_mid(0, 3)
-            d_send(0, 0)
-            d_send(0, 1)
+
+            @pl.when(far)
+            def _():
+                d_mid(0, 3)
+                d_send(0, 0)
+                d_send(0, 1)
+
 
         def result(i):
             m = MH - 1 - i
@@ -1291,14 +1316,13 @@
     backward(1, None, 4, 3, 5, 4)
     backward(0, 4, 6, 5, 7, None)
 
-    for p in (4, 2, 3, 0, 1):
+    for p in (4, 2, 3, 6, 7, 8, 1):
         d_final(p)
     gain_final()
     for copy in outs:
         copy.wait()
     for l in range(2):
-        for p in range(5):
-            d_sent(l, p)
+        d_sent(l)
 
     ags = ((0, N2.at[0]), (1, N1.at[1]), (2, N2.at[1]), (3, GA.at[1]), (4, GF.at[0]), (5, GA.at[0]))
 
@@ -1308,31 +1332,19 @@
         def _():
             state_copy(slot).wait_send()
 
-    def finish(m):
-        for k, buf in ags:
-            ag_sent(k, buf, m)
-        for l in range(2):
-            sent_out(Y, l, out_y, 0, m)
-            sent_out(GX, l, out_g, 1, m)
-        for half in range(2):
-            got(out_y.at[half * MH + m], o_rs.at[0, half, m])
-            got(out_g.at[half * MH + m], o_rs.at[1, half, m])
-
-    loop(MH, finish)
-    for array, src, dst in ((0, xin, XF), (1, cot, GF.at[1])):
-
-        @pl.when(s == array)
+    for k, buf in ags:
+        ag_sent(k, buf)
+    for l in range(2):
+
+        @pl.when(jnp.logical_not((s == l) & (zh == s)))
         def _():
-            for m in range(MH):
-                mine = dst.at[pl.ds(m * MB + z * R, R)]
-                for step in range(1, nt):
-                    copy = remote(
-                        src.at[m], mine, x_ss.at[m, step - 1], x_rs.at[array, m, step - 1], core_dev
-                    )
-                    copy.wait_send()
-                    remote(
-                        mine, mine, x_fs.at[m, step - 1], x_rs.at[array, m, step - 1], core_dev
-                    ).wait_send()
+            got(XF.at[pl.ds(0, 2 * MH * R)], o_ss.at[l])
+
+    for half in range(2):
+        got(out_y.at[pl.ds(half * MH, MH)], o_rs.at[0, half])
+        got(out_g.at[pl.ds(half * MH, MH)], o_rs.at[1, half])
+    for k in range(2):
+        got(XF.at[pl.ds(0, MH * (nt - 1) * R)], x_sem.at[k])
 
 
 def place_results(*refs):
@@ -1429,32 +1441,30 @@
             V((nt - 1, 2, D), F32),
             V((nd - 1, 2, D), F32),
             DMA((2, MH)),
-            DMA((MH, nt - 1)),
+            DMA((2,)),
             DMA((2, MH, nt - 1)),
-            DMA((MH, nt - 1)),
-            DMA((6, 2)),
-            DMA((2, 6)),
-            DMA((2, 6, max(4, nd - 1))),
-            DMA((2, 6, max(4, nd - 1))),
+            DMA((2,)),
+            DMA((2, 4)),
+            DMA((2,)),
+            DMA((2, 4, max(4, nd - 1))),
+            DMA((6,)),
             DMA((6, MH, Hn)),
-            DMA((6, MH, Hn - 1)),
-            DMA((6, MH, nt)),
-            DMA((8, MH)),
-            DMA((8, MH)),
-            DMA((8, MH, Hn - 1)),
-            DMA((8, MH, Hn - 1)),
+            DMA((2, MH)),
+            DMA((2, MH)),
+            DMA((2, MH, Hn - 1)),
+            DMA((2, MH, Hn - 1)),
             DMA((2,)),
             DMA((2,)),
-            DMA((2, 2, MH)),
-            DMA((2, 2, MH)),
-            DMA((2, 5, max(6, nd - 1))),
-            DMA((2, 5, max(6, nd - 1))),
-            DMA((2, 5, 4)),
-            DMA((5, 2, 4)),
-            DMA((6, max(nd, nt) - 1)),
-            DMA((6, max(nd, nt) - 1)),
-            DMA((nd * nt,)),
-            DMA((nd * nt,)),
+            DMA((2,)),
+            DMA((2, 2)),
+            DMA((2,)),
+            DMA((2, 7, 3)),
+            DMA((2,)),
+            DMA((7, 2)),
+            DMA((4,)),
+            DMA((2, max(nd, nt) - 1)),
+            DMA((2, max(nd, nt) - 1)),
+            DMA((2,)),
             DMA((4,)),
         ]
         out_y, out_g, grad_qkv, grad_o, grad_gu, grad_d, grad_gain = pl.pallas_call(

time: 295 us -> 284 us (0.963)
  Pallas kernels: 294 us -> 283 us
    pallas_call x1, Pallas kernels: 290 us -> 279 us  [on_device(): pl.pallas_call(functools.partial(body, z_), out_shape=(jax.ShapeDtypeStru...]
where the time goes in v5:
time: 284 us; the launch traced here: 283 us
  Pallas kernels  283 us (100%)
    pallas_call x1, Pallas kernels, on_device(): pl.pallas_call(functools.partial(body, z_), out_shape=(jax.ShapeDtypeStru...  279 us

profile of v5, /device:TPU:0, one launch (start us, length us, event | category | flops | bytes accessed | tf_op | source)
XLA Modules:
  0.0 283.4 jit_solution(2614344146001395004)
XLA Ops:
  0.6 278.8 %shard_map.135 = (bf16[6,48,1024]{2,1,0:T(8,128)(2,1)}, bf16[6,48,1024]{2,1,0:T(8,128)(2,1)}, f32[3,256,256]{2,1,0:T(8,128)}, f32[256,256]{1,0:T(8,128)}, f32[14...) custom-call(f32[3,256,256]{2,1,0:T(8,128)} %bitcast.28, f32[256,256]{1,0:T(8,128)} %bitcast.32, ...), custom_call_target="tpu_custom_call" | custom-call | tf_op jit(solution)/shard_map/pallas_call | solution.py:1470
  279.4 3.8 %shard_map.136 = (bf16[6,48,1024]{2,1,0:T(8,128)(2,1)}, bf16[6,48,1024]{2,1,0:T(8,128)(2,1)}, f32[3,256,256]{2,1,0:T(8,128)}, f32[256,256]{1,0:T(8,128)}, f32[14...) custom-call(bf16[6,48,1024]{2,1,0:T(8,128)(2,1)} %get-tuple-element.21.refs_0_, ...), custom_call_target="tpu_custom_call" | custom-call | tf_op jit(solution)/shard_map/pallas_call | solution.py:1498

commit v6 on v5

--- a/solution.py
+++ b/solution.py
@@ -224,19 +224,41 @@
             mine = dst.at[pl.ds(m * MB + z * R, R)]
             for step in range(1, nt):
                 other = (z + step) % nt
+
+                @pl.when((other // Hn == zh) | (step == Hn))
+                def _():
+                    remote(
+                        src.at[(other // Hn) * MH + m],
+                        mine,
+                        x_sem.at[0],
+                        x_rs.at[array, m, step - 1],
+                        z_dev(step),
+                    ).start()
+
+    def relay_tokens(dst, array, m):
+        @pl.when(s == array)
+        def _():
+            chip = (z + Hn) % nt
+            rows = dst.at[pl.ds(m * MB + chip * R, R)]
+            got(rows, x_rs.at[array, m, Hn - 1])
+            for step in range(1, Hn):
+                peer = zh * Hn + peer_zl(step)
                 remote(
-                    src.at[(other // Hn) * MH + m],
-                    mine,
+                    rows,
+                    rows,
                     x_sem.at[0],
-                    x_rs.at[array, m, step - 1],
-                    z_dev(step),
+                    x_rs.at[array, m, (peer + nt - chip) % nt - 1],
+                    (s, d, peer),
                 ).start()
 
     def await_tokens(dst, array, m):
         got(dst.at[pl.ds(m * MB + z * R, R)], in_sem.at[array, m])
         for step in range(1, nt):
             rows = dst.at[pl.ds(m * MB + (z + nt - step) % nt * R, R)]
-            got(rows, x_rs.at[array, m, step - 1])
+            if step == Hn:
+                pl.when(s != array)(lambda: got(rows, x_rs.at[array, m, step - 1]))
+            else:
+                got(rows, x_rs.at[array, m, step - 1])
 
             @pl.when(s == array)
             def _():
@@ -903,7 +925,6 @@
     own_tokens(xin, XF, 0)
     own_tokens(cot, GF.at[1], 1)
     shard_feed()
-    hand_far(0, inner, [2, 3, 4])
     hand_near([2, 3, 4])
     masks()
     for l in range(2):
@@ -913,12 +934,13 @@
     pump_far([("s", 0, 5)])
     only((s == 0) & outer & far, x_out)
     pump([("f", 0, 5)])
-    hand_far(0, outer & far, [2, 3, 4])
     pump_near([("f", 0, 2)])
     only((s == 0) & outer & near, x_out)
     only(s == 1, gains_other)
+    for m in range(MH):
+        relay_tokens(XF, 0, m)
+    hand_far(0, s == 0, [2, 3, 4])
     await_tokens(XF, 0, 0)
-    hand_far(0, outer & near, [2, 3, 4])
 
     def cot_out():
         spread_tokens(cot, GF.at[1], 1)
@@ -954,6 +976,7 @@
             pump_far([("s", 1, 2), ("f", 1, 4)]),
         ),
         (1, "states"): lambda: (
+            [relay_tokens(GF.at[1], 1, m) for m in reversed(range(MH))],
             pump_near([("f", 1, 2), ("f", 1, 3)]),
             pump_far([("s", 1, 3), ("f", 1, 2)]),
         ),

time: 284 us -> 277 us (0.975)
  Pallas kernels: 283 us -> 276 us
    pallas_call x1, Pallas kernels: 279 us -> 272 us  [on_device(): pl.pallas_call(functools.partial(body, z_), out_shape=(jax.ShapeDtypeStru...]
where the time goes in v6:
time: 277 us
  Pallas kernels  276 us (100%)
    pallas_call x1, Pallas kernels, on_device(): pl.pallas_call(functools.partial(body, z_), out_shape=(jax.ShapeDtypeStru...  272 us

profile of v6, /device:TPU:0, one launch (start us, length us, event | category | flops | bytes accessed | tf_op | source)
XLA Modules:
  0.0 276.6 jit_solution(10660795769680931469)
XLA Ops:
  0.6 272.0 %shard_map.135 = (bf16[6,48,1024]{2,1,0:T(8,128)(2,1)}, bf16[6,48,1024]{2,1,0:T(8,128)(2,1)}, f32[3,256,256]{2,1,0:T(8,128)}, f32[256,256]{1,0:T(8,128)}, f32[14...) custom-call(f32[3,256,256]{2,1,0:T(8,128)} %bitcast.28, f32[256,256]{1,0:T(8,128)} %bitcast.32, ...), custom_call_target="tpu_custom_call" | custom-call | tf_op jit(solution)/shard_map/pallas_call | solution.py:1493
  272.7 3.8 %shard_map.136 = (bf16[6,48,1024]{2,1,0:T(8,128)(2,1)}, bf16[6,48,1024]{2,1,0:T(8,128)(2,1)}, f32[3,256,256]{2,1,0:T(8,128)}, f32[256,256]{1,0:T(8,128)}, f32[14...) custom-call(bf16[6,48,1024]{2,1,0:T(8,128)(2,1)} %get-tuple-element.21.refs_0_, ...), custom_call_target="tpu_custom_call" | custom-call | tf_op jit(solution)/shard_map/pallas_call | solution.py:1521

commit v7 on v6

--- a/solution.py
+++ b/solution.py
@@ -981,17 +981,17 @@
             pump_far([("s", 1, 3), ("f", 1, 2)]),
         ),
         (1, "attended"): lambda: (pump_far([("f", 1, 3)]),),
-        (1, "hidden"): lambda: (),
+        (1, "hidden"): lambda: (results_out(Y, 0, out_y, 0),),
         (1, "ready"): lambda: (),
         (1, "fed"): lambda: (),
         "b1 second": lambda: (),
-        "b1 middle": lambda: (d_mid(1, 4),),
+        "b1 middle": lambda: (results_out(Y, 1, out_y, 0), d_mid(1, 4)),
         "b1 feed": lambda: (),
-        "b1 third": lambda: (d_mid(1, 3), d_total_rows(1, 2)),
+        "b1 third": lambda: (d_mid(1, 3),),
         "b1 end": lambda: (d_total_rows(1, 3),),
         "b0 second": lambda: (d_total_rows(1, 0),),
         "b0 middle": lambda: (),
-        "b0 feed": lambda: (d_total_rows(1, 1),),
+        "b0 feed": lambda: (results_out(GX, 1, out_g, 1), d_total_rows(1, 1)),
         "b0 third": lambda: (
             only(far, lambda: run(d_mid, 2)),
             only(near, lambda: run(d_mid, 4) or run(d_send, 2, 3)),
@@ -999,7 +999,6 @@
         "b0 end": lambda: (
             core_gain().start(),
             only(near, lambda: run(d_send, 0, 1)),
-            gain_second(),
             only(far, lambda: far_tail()),
             only(near, lambda: near_tail()),
             gain_third(),
@@ -1011,18 +1010,26 @@
             step(0, p)
 
     def far_tail():
-        run(d_sum, 2)
+        gain_second()
         run(d_mid, 6)
         run(d_sum, 3)
         run(d_mid, 7, 8)
         run(d_sum, 6)
         run(d_mid, 1)
         run(d_sum, 7, 8, 1)
+        results_out(GX, 0, out_g, 1)
 
     def near_tail():
         run(d_sum, 4)
-        run(d_mid, 2, 3, 6, 7, 8, 1)
+        run(d_mid, 2, 3)
+        gain_second()
+        run(d_mid, 6, 7, 8, 1)
+        results_out(GX, 0, out_g, 1)
         run(d_sum, 2, 3, 6, 7, 8, 1)
+
+    def results_out(buf, l, out, which):
+        for m in range(MH):
+            send_out(buf, l, out, which, m)
 
     def input_rows(l, m):
         if l == 0:
@@ -1039,7 +1046,6 @@
         def result(m):
             rows = (H[l, own_rows(m), :] + rs_third(rs2, m)).astype(BF)
             Y[l, own_rows(m), :] = rows
-            send_out(Y, l, out_y, 0, m)
             if l == 0:
                 wide = rows.astype(F32)
                 N1[1, chunk_rows(m, own), :] = (wide * rms(wide) * gain(1, 0)).astype(BF)
@@ -1278,13 +1284,13 @@
             state_out(1, last, 1)
             d_mid(1, 2)
             grad_weight(l, 1, GA[l], O[l])
-            d_total_rows(1, 4)
 
             def attend_local(m):
                 for j in range(NB):
                     norm_back_local(m * NB + j)
 
             loop(MH, attend_local)
+            d_total_rows(1, 4)
             state_in(1, 1)
             pl.when(zh == 0)(lambda: d_pass(1, 4, 0, Dr))
 
@@ -1318,6 +1324,7 @@
                 d_mid(0, 3)
                 d_send(0, 0)
                 d_send(0, 1)
+                d_sum(0, 2)
 
 
         def result(i):
@@ -1325,10 +1332,10 @@
             grad = GH[own_rows(m), :] + rms_back(l, 0, input_rows(l, m), rs_third(rs2, m))
             low = grad.astype(BF)
             GX[l, own_rows(m), :] = low
-            send_out(GX, l, out_g, 1, m)
             if l == 1:
                 GF[0, chunk_rows(m, own), :] = low
                 ag_send(ag_out, GF.at[0], m)
+                pl.when(i == 0)(lambda: d_total_rows(1, 2))
                 d_pass(1, 2, i)
 
         loop(MH, result)

time: 277 us -> 275 us (level)
  no operation moved by 1% of the time
where the time goes in v7:
time: 275 us
  Pallas kernels  274 us (100%)
    pallas_call x1, Pallas kernels, on_device(): pl.pallas_call(functools.partial(body, z_), out_shape=(jax.ShapeDtypeStru...  270 us

profile of v7, /device:TPU:0, one launch (start us, length us, event | category | flops | bytes accessed | tf_op | source)
XLA Modules:
  0.0 274.5 jit_solution(3560873771167832189)
XLA Ops:
  0.6 269.9 %shard_map.135 = (bf16[6,48,1024]{2,1,0:T(8,128)(2,1)}, bf16[6,48,1024]{2,1,0:T(8,128)(2,1)}, f32[3,256,256]{2,1,0:T(8,128)}, f32[256,256]{1,0:T(8,128)}, f32[14...) custom-call(f32[3,256,256]{2,1,0:T(8,128)} %bitcast.28, f32[256,256]{1,0:T(8,128)} %bitcast.32, ...), custom_call_target="tpu_custom_call" | custom-call | tf_op jit(solution)/shard_map/pallas_call | solution.py:1500
  270.5 3.8 %shard_map.136 = (bf16[6,48,1024]{2,1,0:T(8,128)(2,1)}, bf16[6,48,1024]{2,1,0:T(8,128)(2,1)}, f32[3,256,256]{2,1,0:T(8,128)}, f32[256,256]{1,0:T(8,128)}, f32[14...) custom-call(bf16[6,48,1024]{2,1,0:T(8,128)(2,1)} %get-tuple-element.21.refs_0_, ...), custom_call_target="tpu_custom_call" | custom-call | tf_op jit(solution)/shard_map/pallas_call | solution.py:1528

commit v8 on v7

--- a/solution.py
+++ b/solution.py
@@ -957,15 +957,16 @@
             pump_far([("f", 0, 3), ("f", 0, 4)]),
         ),
         (0, "ready"): lambda: (
+            hand_far(1, outer & far, [4]),
             pump_near([("f", 1, 5)]),
+            hand_far(1, outer & near, [4]),
             pump_far([("s", 1, 5)]),
         ),
         (0, "feeding"): lambda: (
-            hand_far(1, outer, [4]),
+            hand_far(1, outer, [2, 3]),
             pump_near([("s", 1, 4)]),
         ),
         (0, "fed"): lambda: (
-            hand_far(1, outer, [2, 3]),
             pump_near([("s", 1, 2), ("f", 1, 4)]),
             pump_far([("f", 1, 5), ("s", 1, 4)]),
             only(s == 0, gains_other),

time: 275 us -> 271 us (0.985)
  Pallas kernels: 274 us -> 270 us
    pallas_call x1, Pallas kernels: 270 us -> 266 us  [on_device(): pl.pallas_call(functools.partial(body, z_), out_shape=(jax.ShapeDtypeStru...]
where the time goes in v8:
time: 271 us
  Pallas kernels  270 us (100%)
    pallas_call x1, Pallas kernels, on_device(): pl.pallas_call(functools.partial(body, z_), out_shape=(jax.ShapeDtypeStru...  266 us

profile of v8, /device:TPU:0, one launch (start us, length us, event | category | flops | bytes accessed | tf_op | source)
XLA Modules:
  0.0 270.8 jit_solution(14300441158284366304)
XLA Ops:
  0.6 266.2 %shard_map.135 = (bf16[6,48,1024]{2,1,0:T(8,128)(2,1)}, bf16[6,48,1024]{2,1,0:T(8,128)(2,1)}, f32[3,256,256]{2,1,0:T(8,128)}, f32[256,256]{1,0:T(8,128)}, f32[14...) custom-call(f32[3,256,256]{2,1,0:T(8,128)} %bitcast.28, f32[256,256]{1,0:T(8,128)} %bitcast.32, ...), custom_call_target="tpu_custom_call" | custom-call | tf_op jit(solution)/shard_map/pallas_call | solution.py:1501
  266.9 3.8 %shard_map.136 = (bf16[6,48,1024]{2,1,0:T(8,128)(2,1)}, bf16[6,48,1024]{2,1,0:T(8,128)(2,1)}, f32[3,256,256]{2,1,0:T(8,128)}, f32[256,256]{1,0:T(8,128)}, f32[14...) custom-call(bf16[6,48,1024]{2,1,0:T(8,128)(2,1)} %get-tuple-element.21.refs_0_, ...), custom_call_target="tpu_custom_call" | custom-call | tf_op jit(solution)/shard_map/pallas_call | solution.py:1529

commit v9 on v8

--- a/solution.py
+++ b/solution.py
@@ -961,9 +961,10 @@
             pump_near([("f", 1, 5)]),
             hand_far(1, outer & near, [4]),
             pump_far([("s", 1, 5)]),
+            hand_far(1, outer & far, [2, 3]),
         ),
         (0, "feeding"): lambda: (
-            hand_far(1, outer, [2, 3]),
+            hand_far(1, outer & near, [2, 3]),
             pump_near([("s", 1, 4)]),
         ),
         (0, "fed"): lambda: (

time: 271 us -> 271 us (level)
  no operation moved by 1% of the time
where the time goes in v9:
time: 271 us; the launch traced here: 270 us
  Pallas kernels  270 us (100%)
    pallas_call x1, Pallas kernels, on_device(): pl.pallas_call(functools.partial(body, z_), out_shape=(jax.ShapeDtypeStru...  266 us

profile of v9, /device:TPU:0, one launch (start us, length us, event | category | flops | bytes accessed | tf_op | source)
XLA Modules:
  0.0 270.4 jit_solution(6573477028510705243)
XLA Ops:
  0.6 265.8 %shard_map.135 = (bf16[6,48,1024]{2,1,0:T(8,128)(2,1)}, bf16[6,48,1024]{2,1,0:T(8,128)(2,1)}, f32[3,256,256]{2,1,0:T(8,128)}, f32[256,256]{1,0:T(8,128)}, f32[14...) custom-call(f32[3,256,256]{2,1,0:T(8,128)} %bitcast.28, f32[256,256]{1,0:T(8,128)} %bitcast.32, ...), custom_call_target="tpu_custom_call" | custom-call | tf_op jit(solution)/shard_map/pallas_call | solution.py:1502
  266.5 3.8 %shard_map.136 = (bf16[6,48,1024]{2,1,0:T(8,128)(2,1)}, bf16[6,48,1024]{2,1,0:T(8,128)(2,1)}, f32[3,256,256]{2,1,0:T(8,128)}, f32[256,256]{1,0:T(8,128)}, f32[14...) custom-call(bf16[6,48,1024]{2,1,0:T(8,128)(2,1)} %get-tuple-element.21.refs_0_, ...), custom_call_target="tpu_custom_call" | custom-call | tf_op jit(solution)/shard_map/pallas_call | solution.py:1530

commit v10 on v9

--- a/solution.py
+++ b/solution.py
@@ -968,7 +968,7 @@
             pump_near([("s", 1, 4)]),
         ),
         (0, "fed"): lambda: (
-            pump_near([("s", 1, 2), ("f", 1, 4)]),
+            pump_near([("f", 1, 4), ("s", 1, 2)]),
             pump_far([("f", 1, 5), ("s", 1, 4)]),
             only(s == 0, gains_other),
         ),

time: 271 us -> 270 us (level)
  no operation moved by 1% of the time
where the time goes in v10:
time: 270 us
  Pallas kernels  269 us (100%)
    pallas_call x1, Pallas kernels, on_device(): pl.pallas_call(functools.partial(body, z_), out_shape=(jax.ShapeDtypeStru...  266 us

profile of v10, /device:TPU:0, one launch (start us, length us, event | category | flops | bytes accessed | tf_op | source)
XLA Modules:
  0.0 270.2 jit_solution(2041808245111476193)
XLA Ops:
  0.6 265.6 %shard_map.135 = (bf16[6,48,1024]{2,1,0:T(8,128)(2,1)}, bf16[6,48,1024]{2,1,0:T(8,128)(2,1)}, f32[3,256,256]{2,1,0:T(8,128)}, f32[256,256]{1,0:T(8,128)}, f32[14...) custom-call(f32[3,256,256]{2,1,0:T(8,128)} %bitcast.28, f32[256,256]{1,0:T(8,128)} %bitcast.32, ...), custom_call_target="tpu_custom_call" | custom-call | tf_op jit(solution)/shard_map/pallas_call | solution.py:1502
  266.2 3.8 %shard_map.136 = (bf16[6,48,1024]{2,1,0:T(8,128)(2,1)}, bf16[6,48,1024]{2,1,0:T(8,128)(2,1)}, f32[3,256,256]{2,1,0:T(8,128)}, f32[256,256]{1,0:T(8,128)}, f32[14...) custom-call(bf16[6,48,1024]{2,1,0:T(8,128)(2,1)} %get-tuple-element.21.refs_0_, ...), custom_call_target="tpu_custom_call" | custom-call | tf_op jit(solution)/shard_map/pallas_call | solution.py:1530
